TPU v7x, 256 devices: a whole 4x4x8 slice. The times are simulated.
256 devices in a mesh: heads: 4 (over x), ctx: 64 (over z, y, core).
Axes of the slice: x: 4, y: 4, z: 8, core: 2. Of those that a mesh axis runs over, the one named last changes fastest.
Arguments:
- context_q: bfloat16 [16384, 8192], P('ctx', 'heads'), may hold values from -120 to 120
- context_k: bfloat16 [16384, 1024], P('ctx', 'heads'), may hold values from -8 to 8, as said below
- context_v: bfloat16 [16384, 1024], P('ctx', 'heads'), may hold values from -6 to 6
- question: bfloat16 [256, 8192], P('ctx', 'heads'), may hold values from -120 to 120
- block_lengths: int32 [64], replicated, may hold values from 1 to 256, 12288 in all
- anchor_index: int32 [64], replicated, may hold values from 0 to 63, each once
- question_length: int32 [1], replicated, may hold values from 128 to 256
Outputs:
- mixed: bfloat16 [16384, 8192], P('ctx', 'heads')
- key_cache: bfloat16 [16384, 1024], P('ctx', 'heads')
- value_cache: bfloat16 [16384, 1024], P('ctx', 'heads')
- answer: bfloat16 [256, 8192], P(None, 'heads')
Inputs may be any that keep to these rules, and one draw needn't show every extreme that they name: `context_k`: real values of order one. `block_lengths`: the lengths sum to three quarters of 16384; some block is full. `anchor_index`: each block number appears once.
All inputs are finite; a program needn't handle non-finite values.
Results may differ from a plain program's by a relative error of at most 0.0034.
The roundings to bfloat16 on the way count: a program that leaves them out, or rounds other values in their place, can miss the bound.
Values may be sent and summed in bfloat16 or wider, within the bound.
No kernel may reach another device: no remote copies, remote signals or barrier semaphores. Data moves between devices by JAX's collectives and lax.ppermute only.
A program may use at most 320 MiB of HBM per device.

v0:
```python
import jax
import jax.numpy as jnp
import numpy as np
from jax import lax
from jax.sharding import PartitionSpec as P

HD = 128


def spread(block, axis, holder):
    block = jnp.where(lax.axis_index(axis) == holder, block, jnp.zeros_like(block))
    return lax.psum(block, axis)


def sign_table(count):
    index = np.arange(count)
    both = index[:, None] & index[None, :]
    parity = np.zeros((count, count), np.int64)
    for bit_place in range(16):
        parity = parity ^ both >> bit_place & 1
    return jnp.asarray(1 - 2 * parity, jnp.bfloat16)


def rotate(rows, table):
    flat = rows.reshape(-1, HD)
    turned = jnp.dot(flat, table, preferred_element_type=jnp.float32) * HD ** (-0.5)
    return turned.astype(jnp.bfloat16).reshape(rows.shape)


def encode_group(q_g, k_g, v_g, anchor_k, anchor_v, length, anchor_len, is_anchor):
    factor = HD ** (-0.5)
    s_far = jnp.einsum("tjd,sd->tjs", q_g, anchor_k, preferred_element_type=jnp.float32) * factor
    s_own = jnp.einsum("tjd,sd->tjs", q_g, k_g, preferred_element_type=jnp.float32) * factor
    place = jnp.arange(q_g.shape[0])
    far_ok = (place < anchor_len) & jnp.logical_not(is_anchor)
    own_ok = (place[None, :] <= place[:, None]) & (place[None, :] < length)
    s_far = jnp.where(far_ok[None, None, :], s_far, -jnp.inf)
    s_own = jnp.where(own_ok[:, None, :], s_own, -jnp.inf)
    top = jnp.maximum(jnp.max(s_far, -1), jnp.max(s_own, -1))
    e_far = jnp.exp(s_far - top[..., None])
    e_own = jnp.exp(s_own - top[..., None])
    total = jnp.sum(e_far, -1) + jnp.sum(e_own, -1)
    summed = jnp.einsum(
        "tjs,sd->tjd", e_far.astype(jnp.bfloat16), anchor_v, preferred_element_type=jnp.float32
    )
    summed = summed + jnp.einsum(
        "tjs,sd->tjd", e_own.astype(jnp.bfloat16), v_g, preferred_element_type=jnp.float32
    )
    return (summed / total[..., None]).astype(jnp.bfloat16)


def question_group(q_g, k_g, v_g, length):
    factor = HD ** (-0.5)
    scores = jnp.einsum("rjd,sd->rjs", q_g, k_g, preferred_element_type=jnp.float32) * factor
    valid = jnp.arange(k_g.shape[0]) < length
    scores = jnp.where(valid[None, None, :], scores, -jnp.inf)
    top = jnp.max(scores, -1)
    expo = jnp.exp(scores - top[..., None])
    total = jnp.sum(expo, -1)
    summed = jnp.einsum(
        "rjs,sd->rjd", expo.astype(jnp.bfloat16), v_g, preferred_element_type=jnp.float32
    )
    return (top, total, summed)


def finish(result, table, length):
    count = result.shape[0]
    flat = result.reshape(-1, HD)
    back = jnp.dot(flat, table.astype(jnp.float32), precision=lax.Precision.HIGHEST) * HD ** (-0.5)
    back = back.reshape(count, -1)
    live = jnp.arange(count) < length
    return jnp.where(live[:, None], back, 0.0).astype(jnp.bfloat16)


def on_device(
    context_q, context_k, context_v, question, block_lengths, anchor_index, question_length
):
    groups = context_k.shape[1] // HD
    per = context_q.shape[1] // context_k.shape[1]
    size = context_q.shape[0]
    table = sign_table(HD)
    place = lax.axis_index("ctx")
    anchor = anchor_index[0]
    local_rows = question.shape[0]
    question_rot = rotate(question.reshape(local_rows, groups, per, HD), table).reshape(
        local_rows, -1
    )
    anchor_k, anchor_v = (spread(context_k, "ctx", anchor), spread(context_v, "ctx", anchor))
    length = lax.dynamic_index_in_dim(block_lengths, place, 0, keepdims=False)
    anchor_len = lax.dynamic_index_in_dim(block_lengths, anchor, 0, keepdims=False)
    is_anchor = place == anchor
    q_b = context_q.reshape(size, groups, per, HD)
    k_b = context_k.reshape(size, groups, HD)
    v_b = context_v.reshape(size, groups, HD)
    k_groups = jnp.moveaxis(k_b, 1, 0)
    v_groups = jnp.moveaxis(v_b, 1, 0)

    def encode_one(items):
        q_g, k_g, v_g, far_k, far_v = items
        return encode_group(q_g, k_g, v_g, far_k, far_v, length, anchor_len, is_anchor)

    encoded = lax.map(
        encode_one,
        (
            jnp.moveaxis(q_b, 1, 0),
            k_groups,
            v_groups,
            jnp.moveaxis(anchor_k.reshape(size, groups, HD), 1, 0),
            jnp.moveaxis(anchor_v.reshape(size, groups, HD), 1, 0),
        ),
    )
    mixed = jnp.moveaxis(encoded, 0, 1).reshape(context_q.shape)
    k_rot = rotate(k_b, table)
    v_rot = rotate(v_b, table)
    gathered = lax.all_gather(question_rot, "ctx", axis=0, tiled=True)
    q_rot = gathered.reshape(gathered.shape[0], groups, per, HD)

    def question_one(items):
        q_g, k_g, v_g = items
        return question_group(q_g, k_g, v_g, length)

    tops, totals, sums = lax.map(
        question_one,
        (jnp.moveaxis(q_rot, 1, 0), jnp.moveaxis(k_rot, 1, 0), jnp.moveaxis(v_rot, 1, 0)),
    )
    top = jnp.moveaxis(tops, 0, 1)
    total = jnp.moveaxis(totals, 0, 1)
    summed = jnp.moveaxis(sums, 0, 1)
    limit = question_length[0]
    peak = lax.pmax(top, "ctx")
    factor = jnp.exp(top - peak)
    total_all, summed_all = lax.psum((total * factor, summed * factor[..., None]), "ctx")
    answer = finish(summed_all / total_all[..., None], table, limit)
    return (mixed, k_rot.reshape(context_k.shape), v_rot.reshape(context_v.shape), answer)


def solution(mesh):
    placed = (
        P("ctx", "heads"),
        P("ctx", "heads"),
        P("ctx", "heads"),
        P("ctx", "heads"),
        P(),
        P(),
        P(),
    )
    return jax.shard_map(
        on_device,
        mesh=mesh,
        in_specs=placed,
        out_specs=(P("ctx", "heads"), P("ctx", "heads"), P("ctx", "heads"), P(None, "heads")),
        check_vma=False,
    )
```

profile of v0, /device:TPU:1, one launch (start us, length us, event | category | flops | bytes accessed | tf_op | source)
XLA Modules:
  0.0 624.1 jit_solution(17318534113718311383)
XLA Ops:
  7.2 0.8 reshape_reshape.22
  8.0 0.9 fusion.66
  8.9 0.6 reshape.111
  9.6 1.0 copy.48
  10.7 1.1 copy.46
  12.4 0.7 broadcast_select_fusion
  14.5 1.6 reshape_reshape.18
  16.1 1.0 reshape_reshape.20
  17.1 0.5 copy.45
  17.7 1.1 fusion.64
  18.9 0.7 reshape_reshape.19
  19.9 0.7 reshape_reshape.21
  21.4 0.6 iota_compare_fusion.3
  22.0 0.7 fusion.67
  22.7 68.8 %all-gather.3.cloned.1.call-done = bf16[64,4,2048]{2,1,0:T(4,128)(2,1)} async-done(((bf16[1,4,2048]{2,1,0:T(4,128)(2,1)}), bf16[64,4,2048]{2,1,0:T(4,128)(2,1)}) %all-gather.3.cloned.1.call-update) | async-done | bytes 1048592 | tf_op jit(solution)/shard_map/all_gather | solution.py:115
  91.4 1.7 reshape.106
  93.2 10.4 %while.27 = (s32[]{:T(128)}, f32[2,256,8]{1,2,0:T(8,128)S(1)}, f32[2,256,8]{1,2,0:T(8,128)}, f32[2,256,8,128]{3,2,0,1:T(8,128)}, s32[]{:T(128)}, /*index=5*/bf16...) while((s32[]{:T(128)}, f32[2,256,8]{1,2,0:T(8,128)S(1)}, ...), condition=%wide.region_11.12_spmd, body=%wide.region_8.11_spmd.sunk | while | flops 274198784 | bytes 28116716 | solution.py:122
  93.2 0.6 iota_compare_fusion.5
  94.8 0.8 convolution_bitcast_fusion.2
  95.6 0.8 copy-done
  96.4 0.7 copy_dynamic-update-slice_fusion.2
  97.1 1.3 copy-done.1
  98.4 0.5 iota_compare_fusion.5
  100.0 0.8 convolution_bitcast_fusion.2
  100.8 0.8 copy-done
  101.6 0.7 copy_dynamic-update-slice_fusion.2
  102.3 1.3 copy-done.1
  103.6 243.2 %pmax.7 = f32[256,2,8]{0,2,1:T(8,128)S(1)} all-reduce(f32[256,2,8]{0,2,1:T(8,128)S(1)} %bitcast.152), channel_id=1, replica_groups=mesh['heads'=4,'ctx'=64] {'ctx'}, use_global_device_ids=true, to_apply=%region_12.13 | all-reduce | flops 4096 | bytes 32768 | tf_op jit(solution)/shard_map/pmax | solution.py:130
  346.7 0.7 bitcast_multiply_fusion.1
  347.6 3.5 bitcast_multiply_fusion
  351.2 0.8 copy-done.7
  352.1 12.1 %while.26 = (s32[]{:T(128)}, bf16[2,256,8,128]{3,1,2,0:T(8,128)(2,1)S(1)}, s32[]{:T(128)}, pred[]{:T(512)}, bf16[2,256,8,128]{1,3,2,0:T(8,128)(2,1)S(1)}, /*inde...) while((s32[]{:T(128)}, ...), condition=%wide.region_7.8_spmd, body=%wide.region_2.7_spmd.sunk | while | flops 549319424 | bytes 17421468 | solution.py:102
  352.1 1.2 compare_and_fusion.2
  353.3 1.3 fusion.94
  355.5 0.8 fusion.97
  356.3 0.9 fusion.98
  357.2 0.9 fusion.99
  358.2 1.2 compare_and_fusion.2
  359.3 1.3 fusion.94
  361.6 0.8 fusion.97
  362.3 0.9 fusion.98
  363.3 0.9 fusion.99
  364.2 0.7 copy.55
  364.9 1.2 copy.84
  366.1 246.4 %psum.31 = f32[256,2,8]{0,2,1:T(8,128)S(1)} all-reduce(f32[256,2,8]{0,2,1:T(8,128)S(1)} %get-tuple-element.244), channel_id=1, replica_groups=mesh['heads'=4,'ctx'=64] {'ctx'}, use_global_device_ids=true, to_apply=%region_14.15 | all-reduce | flops 4096 | bytes 32768 | tf_op jit(solution)/shard_map/psum | solution.py:132
  612.8 1.9 broadcast_divide_fusion
  614.7 1.1 convolution_multiply_fusion
  616.4 1.2 select_convert_fusion
  (67 shorter events, 5.3 us)
Async XLA Ops:
  7.2 10.5 %copy-start.4 = (bf16[128,128]{1,0:T(8,128)(2,1)S(1)}, bf16[128,128]{1,0:T(8,128)(2,1)}, u32[]{:S(2)}) copy-start(bf16[128,128]{1,0:T(8,128)(2,1)} %constant.78.clone) | copy-start | bytes 98308
  7.2 9.9 %copy-start.2 = (bf16[256,2048]{1,0:T(8,128)(2,1)S(1)}, bf16[256,2048]{1,0:T(8,128)(2,1)}, u32[]{:S(2)}) copy-start(bf16[256,2048]{1,0:T(8,128)(2,1)} %param.12) | copy-start | bytes 3145732
  7.2 84.2 %all-gather.3.cloned.1.call-start = ((), (), s32[]{:S(2)}) async-start(), calls=%async_computation.1 | async-start | bytes 1064960 | tf_op jit(solution)/shard_map/all_gather | solution.py:115
  9.6 341.6 %all-reduce.6.cloned.1.call-start = ((), (), s32[]{:S(2)}) async-start(), calls=%async_computation.2 | async-start | bytes 524288 | tf_op jit(solution)/shard_map/psum | solution.py:12
  10.7 2.5 copy-start.6
  13.1 599.6 %all-reduce.4.cloned.1.call-start = ((), (), s32[]{:S(2)}) async-start(), calls=%async_computation | async-start | bytes 4194304 | tf_op jit(solution)/shard_map/psum | solution.py:132
  17.1 4.8 copy-start.12
  17.1 4.9 copy-start.10
  93.8 1.0 copy-start.8
  94.8 1.6 copy-start
  94.8 2.3 copy-start.9
  97.1 1.3 copy-start.1
  99.0 1.0 copy-start.8
  100.0 1.6 copy-start
  100.0 2.3 copy-start.9
  102.3 1.3 copy-start.1
  351.2 0.9 copy-start.7
  354.6 0.9 copy-start.3
  360.7 0.9 copy-start.3
  612.7 2.0 copy-start.5
  614.7 1.6 copy-start.11
Sparse Core Ops, SparseCore 0:
  10.8 80.5 all-gather.2
  95.6 173.1 all-reduce.5
  351.3 190.6 all-reduce.3
where the time goes:
time: 629 us; the launch traced here: 624 us
  blocking collectives  490 us (78%)
  waiting for transfers between devices  68.9 us (11%)
  local copies, waits for them, and re-layouts  20.5 us (3%)
  between operations  16.7 us (3%)
  other arithmetic  15.2 us (2%)
  matrix products  12.8 us (2%)
    psum x1, blocking collectives, on_device(): lax.psum((total * factor, summed * factor[..., None]), 'ctx')  246 us
    pmax x1, blocking collectives, on_device(): peak = lax.pmax(top, 'ctx')  243 us
    all_gather x1, waiting for transfers between devices, on_device(): gathered = lax.all_gather(question_rot, 'ctx', axis=0, tiled=True)  68.8 us
  transfers between devices with their start and end apart: 3, of which 1 were waited for; matrix products, arithmetic and copies ran while one was open for 6% of the time, Pallas kernels for 0%

commit v1 on v0

v1 whole, which is shorter than its diff:
```python
import functools

import jax
import jax.numpy as jnp
from jax import lax
from jax.experimental import pallas as pl
from jax.experimental.pallas import tpu as pltpu
from jax.sharding import PartitionSpec as P

HD = 128
SC = HD ** (-0.5)
NZ, NY, NC = 8, 4, 2
BLK = 256
BF = jnp.bfloat16
F32 = jnp.float32
SMEM = pl.BlockSpec(memory_space=pltpu.SMEM)
VMEM = pl.BlockSpec(memory_space=pltpu.VMEM)


def index_of(z, y, c):
    return (z * NY + y) * NC + c


def permutation(move):
    return [
        (index_of(z, y, c), index_of(*move(z, y, c)))
        for z in range(NZ)
        for y in range(NY)
        for c in range(NC)
    ]


Z_GROUPS = [[index_of(z, y, c) for z in range(NZ)] for y in range(NY) for c in range(NC)]
OTHER_CORE = permutation(lambda z, y, c: (z, y, 1 - c))
Y_SHIFTS = [permutation(lambda z, y, c, d=d: (z, (y + d) % NY, c)) for d in range(NY)]


def coordinates():
    place = lax.axis_index("ctx")
    return place // (NY * NC), (place // NC) % NY, place % NC


def sign_table():
    shape = (HD, HD)
    both = lax.broadcasted_iota(jnp.int32, shape, 0) & lax.broadcasted_iota(jnp.int32, shape, 1)
    both = both ^ (both >> 4)
    both = both ^ (both >> 2)
    both = both ^ (both >> 1)
    return (1 - 2 * (both & 1)).astype(F32).astype(BF)


def rotated(rows, table):
    return (jnp.dot(rows, table, preferred_element_type=F32) * SC).astype(BF)


def across(a, b):
    return lax.dot_general(a, b, (((1,), (1,)), ((), ())), preferred_element_type=F32)


def prepare_kernel(question_ref, k_ref, v_ref, send_ref, both_ref, rows_ref):
    both_ref[0:BLK, :] = k_ref[...]
    both_ref[BLK : 2 * BLK, :] = v_ref[...]
    question = question_ref[...].astype(F32)
    for k in range(8):
        rows_ref[4 * k : 4 * k + 4, :] = question[:, 256 * k : 256 * k + 256]
    rows = rows_ref[...].astype(BF)
    for z in range(NZ):
        send_ref[z, 0:32, :] = k_ref[32 * z : 32 * z + 32, :]
        send_ref[z, 32:64, :] = v_ref[32 * z : 32 * z + 32, :]
        send_ref[z, 64:96, :] = rows


def prepare(question, k, v):
    return pl.pallas_call(
        prepare_kernel,
        out_shape=(
            jax.ShapeDtypeStruct((NZ, 96, 256), BF),
            jax.ShapeDtypeStruct((2 * BLK, 256), BF),
        ),
        in_specs=[VMEM] * 3,
        out_specs=(VMEM, VMEM),
        scratch_shapes=[pltpu.VMEM((32, 256), F32)],
        name="prepare",
    )(question, k, v)


def question_kernel(lengths_ref, got_ref, *refs):
    blocks, send_ref = refs[:8], refs[8]
    z, y, c = coordinates()
    table = sign_table()
    lane = lax.broadcasted_iota(jnp.int32, (BLK, BLK), 1)
    ids = [index_of(z, lax.rem(y + NY - d, NY), c) for d in range(NY)]
    ids += [index_of(z, lax.rem(y + NY - d, NY), 1 - c) for d in range(NY)]
    stats = []
    for g in range(2):
        halves = [
            got_ref[:, 64 + 16 * g : 80 + 16 * g, HD * half : HD * half + HD].reshape(NZ * 16, HD)
            for half in range(2)
        ]
        q = rotated(jnp.concatenate(halves, axis=0), table)
        top = total = summed = None
        for which in range(8):
            k = rotated(blocks[which][0:BLK, HD * g : HD * g + HD], table)
            v = rotated(blocks[which][BLK : 2 * BLK, HD * g : HD * g + HD], table)
            part = jnp.where(lane < lengths_ref[ids[which]], across(q, k) * SC, -jnp.inf)
            m = jnp.max(part, axis=1, keepdims=True)
            e = jnp.exp(part - m)
            d = jnp.sum(e, axis=1, keepdims=True)
            n = jnp.dot(e.astype(BF), v, preferred_element_type=F32)
            if which == 0:
                top, total, summed = m, d, n
            else:
                new = jnp.maximum(top, m)
                old_scale, scale = jnp.exp(top - new), jnp.exp(m - new)
                top = new
                total = total * old_scale + d * scale
                summed = summed * old_scale + n * scale
        for half in range(2):
            rows = slice(128 * half, 128 * half + 128)
            at = 16 * (2 * g + half)
            send_ref[:, at : at + 16, :] = summed[rows].reshape(NZ, 16, HD)
            stats.append((top[rows], total[rows]))
    lanes = lax.broadcasted_iota(jnp.int32, (HD, HD), 1)
    packed = jnp.zeros((HD, HD), F32)
    for i in range(4):
        packed = jnp.where(lanes == i, stats[i][0], packed)
        packed = jnp.where(lanes == 4 + i, stats[i][1], packed)
    tile = packed.T[0:8, :]
    for i in range(NZ):
        send_ref[i, 64:72, :] = tile


def question_pass(lengths, got, blocks):
    return pl.pallas_call(
        question_kernel,
        out_shape=jax.ShapeDtypeStruct((NZ, 72, HD), F32),
        in_specs=[SMEM] + [VMEM] * 9,
        out_specs=VMEM,
        compiler_params=pltpu.CompilerParams(vmem_limit_bytes=48 * 1024 * 1024),
        cost_estimate=pl.CostEstimate(
            flops=900_000_000, bytes_accessed=2_500_000, transcendentals=1_100_000
        ),
        name="question_pass",
    )(lengths, got, *blocks)


def combine_kernel(anchor_ref, limit_ref, parts_ref, *refs):
    pieces, send_ref, columns_ref = refs[:4], refs[4], refs[5]
    z, y, c = coordinates()
    table = sign_table()
    tiles = [parts_ref[s, 64:72, :] for s in range(NZ)]
    square = jnp.concatenate(tiles + [jnp.zeros((HD - 64, HD), F32)], axis=0)
    columns_ref[...] = square.T
    columns = columns_ref[pl.ds(pl.multiple_of(z * 16, 16), 16), :]
    row = lax.broadcasted_iota(jnp.int32, (64, HD), 0)
    results = []
    for i in range(4):
        tops = [columns[:, 8 * s + i : 8 * s + i + 1] for s in range(NZ)]
        peak = functools.reduce(jnp.maximum, tops)
        total = jnp.zeros((16, 1), F32)
        summed = jnp.zeros((16, HD), F32)
        for s in range(NZ):
            scale = jnp.exp(tops[s] - peak)
            total = total + scale * columns[:, 8 * s + 4 + i : 8 * s + 5 + i]
            summed = summed + scale * parts_ref[s, 16 * i : 16 * i + 16, :]
        results.append(summed / total)
    result = jnp.concatenate(results, axis=0)
    high = result.astype(BF)
    rest = result - high.astype(F32)
    middle = rest.astype(BF)
    low = (rest - middle.astype(F32)).astype(BF)
    back = jnp.dot(low, table, preferred_element_type=F32)
    back = back + jnp.dot(middle, table, preferred_element_type=F32)
    back = (back + jnp.dot(high, table, preferred_element_type=F32)) * SC
    position = index_of(z, y, c) * 4 + (row & 3)
    back = jnp.where(position < limit_ref[0], back, 0.0).astype(BF)
    anchor = anchor_ref[0]
    shift = lax.rem(y + NY - lax.rem(anchor // NC, NY), NY)
    piece = pieces[0][...]
    for d in range(1, NY):
        piece = jnp.where(shift == d, pieces[d][...], piece)
    for i in range(NZ):
        for g in range(2):
            for half in range(2):
                at = 16 * (2 * g + half)
                send_ref[i, 16 * g : 16 * g + 16, HD * half : HD * half + HD] = back[at : at + 16]
        send_ref[i, 32:96, :] = piece


def combine(anchor_index, limit, parts, pieces):
    return pl.pallas_call(
        combine_kernel,
        out_shape=jax.ShapeDtypeStruct((NZ, 96, 256), BF),
        in_specs=[SMEM, SMEM] + [VMEM] * 5,
        out_specs=VMEM,
        scratch_shapes=[pltpu.VMEM((HD, HD), F32)],
        name="combine",
    )(anchor_index, limit, parts, *pieces)


def encode_kernel(anchor_ref, lengths_ref, q_ref, k_ref, v_ref, got_ref, mixed_ref, krot_ref, vrot_ref):
    place = lax.axis_index("ctx")
    anchor = anchor_ref[0]
    k, v = k_ref[...], v_ref[...]

    @pl.when(lax.rem(pl.program_id(0), 8) == 0)
    def _():
        table = sign_table()
        krot_ref[...] = rotated(k, table)
        vrot_ref[...] = rotated(v, table)

    far_k = got_ref[:, 32:64, :].reshape(BLK, HD)
    far_v = got_ref[:, 64:96, :].reshape(BLK, HD)
    q = q_ref[...]
    row = lax.broadcasted_iota(jnp.int32, (BLK, BLK), 0)
    lane = lax.broadcasted_iota(jnp.int32, (BLK, BLK), 1)
    far_len = jnp.where(place == anchor, 0, lengths_ref[anchor])
    s_far = jnp.where(lane < far_len, across(q, far_k) * SC, -jnp.inf)
    own_ok = (lane <= row) & (lane < lengths_ref[place])
    s_own = jnp.where(own_ok, across(q, k) * SC, -jnp.inf)
    top = jnp.max(jnp.maximum(s_far, s_own), axis=1, keepdims=True)
    e_far = jnp.exp(s_far - top)
    e_own = jnp.exp(s_own - top)
    total = jnp.sum(e_far + e_own, axis=1, keepdims=True)
    summed = jnp.dot(e_far.astype(BF), far_v, preferred_element_type=F32)
    summed = summed + jnp.dot(e_own.astype(BF), v, preferred_element_type=F32)
    mixed_ref[...] = (summed / total).astype(BF)


def encode(anchor_index, lengths, q, k, v, got):
    head = pl.BlockSpec((BLK, HD), lambda h: (0, h))
    group = pl.BlockSpec((BLK, HD), lambda h: (0, h // 8))
    return pl.pallas_call(
        encode_kernel,
        grid=(16,),
        out_shape=(
            jax.ShapeDtypeStruct(q.shape, BF),
            jax.ShapeDtypeStruct(k.shape, BF),
            jax.ShapeDtypeStruct(v.shape, BF),
        ),
        in_specs=[
            SMEM,
            SMEM,
            head,
            group,
            group,
            pl.BlockSpec((NZ, 96, HD), lambda h: (0, 0, h // 8)),
        ],
        out_specs=(head, group, group),
        cost_estimate=pl.CostEstimate(
            flops=1_100_000_000, bytes_accessed=3_500_000, transcendentals=2_100_000
        ),
        name="encode",
    )(anchor_index, lengths, q, k, v, got)


def assemble_kernel(*refs):
    own, other, out_ref = refs[0:4], refs[4:8], refs[8]
    z, y, c = coordinates()
    upper = lax.broadcasted_iota(jnp.int32, (8, 256), 0) < 4
    for d in range(NY):
        at = lax.rem(y + NY - d, NY)
        mine = own[d][0].astype(F32)
        theirs = other[d][0].astype(F32)
        first = jnp.where(c == 0, mine, theirs)
        second = jnp.where(c == 0, theirs, mine)
        for m in range(4):
            a, b = first[8 * m : 8 * m + 8], second[8 * m : 8 * m + 8]
            even = jnp.where(upper, a, pltpu.roll(b, 4, 0))
            odd = jnp.where(upper, pltpu.roll(a, 4, 0), b)
            out_ref[0, at, :, 512 * m : 512 * m + 256] = even.astype(BF)
            out_ref[0, at, :, 512 * m + 256 : 512 * m + 512] = odd.astype(BF)


def assemble(own, other):
    part = pl.BlockSpec((1, 32, 256), lambda i: (i, 0, 0))
    return pl.pallas_call(
        assemble_kernel,
        grid=(NZ,),
        out_shape=jax.ShapeDtypeStruct((NZ, NY, 8, 2048), BF),
        in_specs=[part] * 8,
        out_specs=pl.BlockSpec((1, NY, 8, 2048), lambda i: (i, 0, 0, 0)),
        name="assemble",
    )(*own, *other)


def on_device(
    context_q, context_k, context_v, question, block_lengths, anchor_index, question_length
):
    def swap(x):
        return lax.ppermute(x, "ctx", OTHER_CORE)

    def along_y(x):
        return [x] + [lax.ppermute(x, "ctx", Y_SHIFTS[d]) for d in range(1, NY)]

    def over_z(x):
        return lax.all_to_all(x, "ctx", 0, 0, axis_index_groups=Z_GROUPS)

    send, both = prepare(question, context_k, context_v)
    blocks = along_y(both)
    got = over_z(send)
    blocks = blocks + [swap(b) for b in blocks]
    anchor = anchor_index[0]
    piece = lax.dynamic_index_in_dim(got[:, 0:64, :], anchor // (NY * NC), 0, keepdims=False)
    core = lax.axis_index("ctx") % NC
    piece = jnp.where(anchor % NC == core, piece, swap(piece))
    pieces = along_y(piece)
    parts = over_z(question_pass(block_lengths, got, blocks))
    final = over_z(combine(anchor_index, question_length, parts, pieces))
    own = along_y(final[:, 0:32, :])
    mixed, key_cache, value_cache = encode(
        anchor_index, block_lengths, context_q, context_k, context_v, final
    )
    other = [swap(x) for x in own]
    answer = assemble(own, other).reshape(256, 2048)
    return mixed, key_cache, value_cache, answer


def solution(mesh):
    placed = (
        P("ctx", "heads"),
        P("ctx", "heads"),
        P("ctx", "heads"),
        P("ctx", "heads"),
        P(),
        P(),
        P(),
    )
    return jax.shard_map(
        on_device,
        mesh=mesh,
        in_specs=placed,
        out_specs=(P("ctx", "heads"), P("ctx", "heads"), P("ctx", "heads"), P(None, "heads")),
        check_vma=False,
    )
```

time: 629 us -> 108 us (0.17)
  blocking collectives: 490 us -> 15.4 us
  waiting for transfers between devices: 68.9 us -> 14.3 us
  starting transfers between devices: 0.12 us -> 43.9 us
  Pallas kernels: 0 us -> 28.2 us
  local copies, waits for them, and re-layouts: 20.5 us -> 2.8 us
  other arithmetic: 15.2 us -> 0.01 us
  between operations: 16.7 us -> 1.65 us
  matrix products: 12.8 us -> 0 us
    psum x1 -> x0, blocking collectives: 246 us -> none  [on_device(): lax.psum((total * factor, summed * factor[..., None]), 'ctx')]
    pmax x1 -> x0, blocking collectives: 243 us -> none  [on_device(): peak = lax.pmax(top, 'ctx')]
    all_gather x1 -> x0, waiting for transfers between devices: 68.8 us -> none  [on_device(): gathered = lax.all_gather(question_rot, 'ctx', axis=0, tiled=True)]
    pallas_call x0 -> x5, Pallas kernels: none -> 28.2 us  [the longest x1 13 us: encode(): pl.pallas_call(encode_kernel, grid=(16,), out_shape=(jax.ShapeDtypeStruct...]
    ppermute x0 -> x18, starting transfers between devices: none -> 28.1 us  [the longest x9 15.7 us: swap(): return lax.ppermute(x, 'ctx', OTHER_CORE)]
    all_to_all x0 -> x2, starting transfers between devices: none -> 15.8 us  [over_z(): return lax.all_to_all(x, 'ctx', 0, 0, axis_index_groups=Z_GROUPS)]
    all_to_all x0 -> x1, blocking collectives: none -> 15.4 us  [over_z(): return lax.all_to_all(x, 'ctx', 0, 0, axis_index_groups=Z_GROUPS)]
    dot_general x16 -> x0, matrix products: 12.8 us -> none  [the longest x2 2.65 us: encode_group(): jnp.einsum('tjd,sd->tjs', q_g, anchor_k, preferred_element_type=jnp.float32)]
  transfers between devices with their start and end apart: 3 -> 20, of which waited for: 1 -> 8; matrix products, arithmetic and copies ran while one was open for 6% -> 0% of each run, Pallas kernels for 0% -> 12%
where the time goes in v1:
time: 108 us; the launch traced here: 106 us
  starting transfers between devices  43.9 us (41%)
  Pallas kernels  28.2 us (26%)
  blocking collectives  15.4 us (14%)
  waiting for transfers between devices  14.3 us (13%)
  local copies, waits for them, and re-layouts  2.8 us (3%)
  between operations  1.65 us (2%)
    all_to_all x2, starting transfers between devices, over_z(): return lax.all_to_all(x, 'ctx', 0, 0, axis_index_groups=Z_GROUPS)  15.8 us
    ppermute x9, starting transfers between devices, swap(): return lax.ppermute(x, 'ctx', OTHER_CORE)  15.7 us
    all_to_all x1, blocking collectives, over_z(): return lax.all_to_all(x, 'ctx', 0, 0, axis_index_groups=Z_GROUPS)  15.4 us
    pallas_call x1, Pallas kernels, encode(): pl.pallas_call(encode_kernel, grid=(16,), out_shape=(jax.ShapeDtypeStruct...  13 us
    ppermute x9, starting transfers between devices, along_y(): return [x] + [lax.ppermute(x, 'ctx', Y_SHIFTS[d]) for d in range(1, NY)]  12.4 us
    ppermute x9, waiting for transfers between devices, along_y(): return [x] + [lax.ppermute(x, 'ctx', Y_SHIFTS[d]) for d in range(1, NY)]  8.43 us
    pallas_call x1, Pallas kernels, question_pass(): pl.pallas_call(question_kernel, out_shape=jax.ShapeDtypeStruct((NZ, 72, H...  5.93 us
    pallas_call x1, Pallas kernels, assemble(): pl.pallas_call(assemble_kernel, grid=(NZ,), out_shape=jax.ShapeDtypeStruc...  5.05 us
  transfers between devices with their start and end apart: 20, of which 8 were waited for; matrix products, arithmetic and copies ran while one was open for 0% of the time, Pallas kernels for 12%

profile of v1, /device:TPU:1, one launch (start us, length us, event | category | flops | bytes accessed | tf_op | source)
XLA Modules:
  0.0 106.2 jit_solution(13333727463735915302)
XLA Ops:
  0.6 1.9 %prepare.1 = (bf16[8,96,256]{2,1,0:T(8,128)(2,1)}, bf16[512,256]{1,0:T(8,128)(2,1)}) custom-call(bf16[4,2048]{1,0:T(4,128)(2,1)} %question_ref.1, bf16[256,256]{1,0:T(8,128)(2,1)} %k_ref.3, bf16[256,256]{1,0:T(8,128)(2,1)} %v_ref.3), custom_call_target="tpu_custom_call" | custom-call | tf_op jit(solution)/shard_map/prepare/pallas_call | solution.py:74
  2.5 9.1 %all-to-all-start = ((bf16[8,96,256]{2,1,0:T(8,128)(2,1)}), bf16[8,96,256]{2,1,0:T(8,128)(2,1)S(1)}, u32[]{:S(2)}, u32[]{:S(2)}) async-start(bf16[8,96,256]{2,1,0:T(8,128)(2,1)} %get-tuple-element.9), calls=%async_computation | async-start | bytes 786432 | tf_op jit(solution)/shard_map/all_to_all | solution.py:297
  11.6 1.4 %collective-permute-start = (bf16[512,256]{1,0:T(8,128)(2,1)S(1)}, bf16[512,256]{1,0:T(8,128)(2,1)S(1)}, u32[]{:S(2)}, u32[]{:S(2)}) collective-permute-start(bf16[512,256]{1,0:T(8,128)(2,1)S(1)} %copy-done), channel_id=1, source_target_pairs={{0,2},{1,3},{2,4},{3,5},{4,6},{5,7},{6,0},{7,1},{8,10},{9,11},{10,... | collective-permute-start | bytes 786440 | tf_op jit(solution)/shard_map/ppermute | solution.py:294
  13.0 2.6 %collective-permute-start.1 = (bf16[512,256]{1,0:T(8,128)(2,1)S(1)}, bf16[512,256]{1,0:T(8,128)(2,1)S(1)}, u32[]{:S(2)}, u32[]{:S(2)}) collective-permute-start(bf16[512,256]{1,0:T(8,128)(2,1)S(1)} %copy-done), channel_id=1, source_target_pairs={{0,4},{1,5},{2,6},{3,7},{4,0},{5,1},{6,2},{7,3},{8,12},{9,13},{10,... | collective-permute-start | bytes 786440 | tf_op jit(solution)/shard_map/ppermute | solution.py:294
  15.6 1.1 %collective-permute-start.2 = (bf16[512,256]{1,0:T(8,128)(2,1)S(1)}, bf16[512,256]{1,0:T(8,128)(2,1)S(1)}, u32[]{:S(2)}, u32[]{:S(2)}) collective-permute-start(bf16[512,256]{1,0:T(8,128)(2,1)S(1)} %copy-done), channel_id=1, source_target_pairs={{0,6},{1,7},{2,0},{3,1},{4,2},{5,3},{6,4},{7,5},{8,14},{9,15},{10,... | collective-permute-start | bytes 786440 | tf_op jit(solution)/shard_map/ppermute | solution.py:294
  16.7 1.8 %collective-permute-start.3 = (bf16[512,256]{1,0:T(8,128)(2,1)S(1)}, bf16[512,256]{1,0:T(8,128)(2,1)S(1)}, u32[]{:S(2)}, u32[]{:S(2)}) collective-permute-start(bf16[512,256]{1,0:T(8,128)(2,1)S(1)} %copy-done), channel_id=1, source_target_pairs={{0,1},{1,0},{2,3},{3,2},{4,5},{5,4},{6,7},{7,6},{8,9},{9,8},{10,11... | collective-permute-start | bytes 786440 | tf_op jit(solution)/shard_map/ppermute | solution.py:291
  18.5 1.4 %collective-permute-done.refs_1_ = bf16[512,256]{1,0:T(8,128)(2,1)S(1)} collective-permute-done((bf16[512,256]{1,0:T(8,128)(2,1)S(1)}, bf16[512,256]{1,0:T(8,128)(2,1)S(1)}, u32[]{:S(2)}, u32[]{:S(2)}) %collective-permute-start) | collective-permute-done | bytes 262176 | tf_op jit(solution)/shard_map/ppermute | solution.py:294
  19.9 2.1 %collective-permute-start.4 = (bf16[512,256]{1,0:T(8,128)(2,1)S(1)}, bf16[512,256]{1,0:T(8,128)(2,1)S(1)}, u32[]{:S(2)}, u32[]{:S(2)}) collective-permute-start(bf16[512,256]{1,0:T(8,128)(2,1)S(1)} %collective-permute-done.refs_1_), channel_id=1, source_target_pairs={{0,1},{1,0},{2,3},{3,2},{4,5},{5,4},{6,7},{7,6},{8,9},{9,8},{10,11... | collective-permute-start | bytes 786440 | tf_op jit(solution)/shard_map/ppermute | solution.py:291
  22.0 4.6 %collective-permute-done.1.refs_2_ = bf16[512,256]{1,0:T(8,128)(2,1)S(1)} collective-permute-done((bf16[512,256]{1,0:T(8,128)(2,1)S(1)}, bf16[512,256]{1,0:T(8,128)(2,1)S(1)}, u32[]{:S(2)}, u32[]{:S(2)}) %collective-permute-start.1) | collective-permute-done | bytes 262176 | tf_op jit(solution)/shard_map/ppermute | solution.py:294
  26.7 1.9 %collective-permute-start.5 = (bf16[512,256]{1,0:T(8,128)(2,1)S(1)}, bf16[512,256]{1,0:T(8,128)(2,1)S(1)}, u32[]{:S(2)}, u32[]{:S(2)}) collective-permute-start(bf16[512,256]{1,0:T(8,128)(2,1)S(1)} %collective-permute-done.1.refs_2_), channel_id=1, source_target_pairs={{0,1},{1,0},{2,3},{3,2},{4,5},{5,4},{6,7},{7,6},{8,9},{9,8},{10,11... | collective-permute-start | bytes 786440 | tf_op jit(solution)/shard_map/ppermute | solution.py:291
  28.5 0.0 collective-permute-done.2.refs_3_
  28.5 0.0 collective-permute-start.6
  28.5 0.0 collective-permute-done.3.refs_4_
  28.5 0.0 collective-permute-done.4.refs_5_
  28.5 1.1 %collective-permute-done.5.refs_6_ = bf16[512,256]{1,0:T(8,128)(2,1)S(1)} collective-permute-done((bf16[512,256]{1,0:T(8,128)(2,1)S(1)}, bf16[512,256]{1,0:T(8,128)(2,1)S(1)}, u32[]{:S(2)}, u32[]{:S(2)}) %collective-permute-start.5) | collective-permute-done | bytes 262176 | tf_op jit(solution)/shard_map/ppermute | solution.py:291
  29.7 0.4 collective-permute-done.6.refs_7_
  30.1 5.9 %question_pass.1 = f32[8,72,128]{2,1,0:T(8,128)} custom-call(s32[64]{0:T(128)S(1)} %copy-done.1, bf16[8,96,256]{2,1,0:T(8,128)(2,1)S(1)} %all-to-all-done.got_ref, bf16[512,256]{1,0:T(8,128)(2,1)S(1)} %copy-done, bf16[512,256]{1,0:T(8,128)(2,1)S(1)} %collective-permute-done.refs_1_, bf16[512,256]{1,0:T(8,128)(2,1)S(1)} %collective-permute-done.1.refs_2_, ...), custom_call_target="tpu_custom_call" | custom-call | flops 900000000 | bytes 2500000 | tf_op jit(solution)/shard_map/question_pass/pallas_call | solution.py:134
  36.0 6.6 %all-to-all-start.1 = ((f32[8,72,128]{2,1,0:T(8,128)}), f32[8,72,128]{2,1,0:T(8,128)S(1)}, u32[]{:S(2)}, u32[]{:S(2)}) async-start(f32[8,72,128]{2,1,0:T(8,128)} %question_pass.1), calls=%async_computation.1 | async-start | bytes 589824 | tf_op jit(solution)/shard_map/all_to_all | solution.py:297
  42.6 0.7 copy-done.16
  43.5 0.7 collective-permute-start.7
  44.2 0.9 collective-permute-done.7
  45.1 1.6 %collective-permute-start.10 = (bf16[64,256]{1,0:T(8,128)(2,1)S(1)}, bf16[64,256]{1,0:T(8,128)(2,1)S(1)}, u32[]{:S(2)}, u32[]{:S(2)}) collective-permute-start(bf16[64,256]{1,0:T(8,128)(2,1)S(1)} %broadcast_select_fusion.refs_0_), channel_id=1, source_target_pairs={{0,6},{1,7},{2,0},{3,1},{4,2},{5,3},{6,4},{7,5},{8,14},{9,15},{10,... | collective-permute-start | bytes 98312 | tf_op jit(solution)/shard_map/ppermute | solution.py:294
  46.7 0.0 collective-permute-start.8
  46.7 1.9 %collective-permute-start.9 = (bf16[64,256]{1,0:T(8,128)(2,1)S(1)}, bf16[64,256]{1,0:T(8,128)(2,1)S(1)}, u32[]{:S(2)}, u32[]{:S(2)}) collective-permute-start(bf16[64,256]{1,0:T(8,128)(2,1)S(1)} %broadcast_select_fusion.refs_0_), channel_id=1, source_target_pairs={{0,4},{1,5},{2,6},{3,7},{4,0},{5,1},{6,2},{7,3},{8,12},{9,13},{10,... | collective-permute-start | bytes 98312 | tf_op jit(solution)/shard_map/ppermute | solution.py:294
  49.2 0.0 collective-permute-done.10.refs_3_
  49.2 1.8 %collective-permute-done.8.refs_1_ = bf16[64,256]{1,0:T(8,128)(2,1)S(1)} collective-permute-done((bf16[64,256]{1,0:T(8,128)(2,1)S(1)}, bf16[64,256]{1,0:T(8,128)(2,1)S(1)}, u32[]{:S(2)}, u32[]{:S(2)}) %collective-permute-start.8) | collective-permute-done | bytes 32800 | tf_op jit(solution)/shard_map/ppermute | solution.py:294
  51.0 0.6 collective-permute-done.9.refs_2_
  51.6 3.4 %all-to-all-done.1.parts_ref = f32[8,72,128]{2,1,0:T(8,128)S(1)} async-done(((f32[8,72,128]{2,1,0:T(8,128)}), f32[8,72,128]{2,1,0:T(8,128)S(1)}, u32[]{:S(2)}, u32[]{:S(2)}) %all-to-all-start.1) | async-done | bytes 294944 | tf_op jit(solution)/shard_map/all_to_all | solution.py:297
  55.1 0.0 copy-start.2
  55.1 0.7 copy-done.2
  55.8 2.4 %combine.1 = bf16[8,96,256]{2,1,0:T(8,128)(2,1)} custom-call(s32[64]{0:T(128)} %anchor_ref.3, s32[1]{0:T(128)S(6)} %copy.11.limit_ref, f32[8,72,128]{2,1,0:T(8,128)} %copy-done.2, bf16[64,256]{1,0:T(8,128)(2,1)} %copy-done.12, bf16[64,256]{1,0:T(8,128)(2,1)} %copy-done.14, bf16[64,256]{1,0:T(8,128)(2,1)} %copy-done.15, bf16[64,256]{1,0:T(8,128)(2,1)} %copy-done.13), custom_call_target="tpu_custom_call" | custom-call | tf_op jit(solution)/shard_map/combine/pallas_call | solution.py:191
  58.2 15.4 %all_to_all.15.got_ref = bf16[8,96,256]{2,1,0:T(8,128)(2,1)S(1)} all-to-all(bf16[8,96,256]{2,1,0:T(8,128)(2,1)} %combine.1), channel_id=1, replica_groups={{0,8,16,24,32,40,48,56},{1,9,17,25,33,41,49,57},{2,10,18,26,34,42,50,58..., dimensions={0} | all-to-all | bytes 786432 | tf_op jit(solution)/shard_map/all_to_all | solution.py:297
  73.6 0.4 collective-permute-start.11
  74.0 3.2 %collective-permute-start.12 = (bf16[8,32,256]{2,1,0:T(8,128)(2,1)S(1)}, bf16[8,32,256]{2,1,0:T(8,128)(2,1)S(1)}, u32[]{:S(2)}, u32[]{:S(2)}) collective-permute-start(bf16[8,32,256]{2,1,0:T(8,128)(2,1)S(1)} %slice.13.refs_0_), channel_id=1, source_target_pairs={{0,4},{1,5},{2,6},{3,7},{4,0},{5,1},{6,2},{7,3},{8,12},{9,13},{10,... | collective-permute-start | bytes 393224 | tf_op jit(solution)/shard_map/ppermute | solution.py:294
  77.1 0.4 collective-permute-start.13
  77.5 4.8 %collective-permute-start.14 = (bf16[8,32,256]{2,1,0:T(8,128)(2,1)S(1)}, bf16[8,32,256]{2,1,0:T(8,128)(2,1)S(1)}, u32[]{:S(2)}, u32[]{:S(2)}) collective-permute-start(bf16[8,32,256]{2,1,0:T(8,128)(2,1)S(1)} %slice.13.refs_0_), channel_id=1, source_target_pairs={{0,1},{1,0},{2,3},{3,2},{4,5},{5,4},{6,7},{7,6},{8,9},{9,8},{10,11... | collective-permute-start | bytes 393224 | tf_op jit(solution)/shard_map/ppermute | solution.py:291
  82.3 0.0 collective-permute-done.11.refs_1_
  82.3 1.6 %collective-permute-start.15 = (bf16[8,32,256]{2,1,0:T(8,128)(2,1)S(1)}, bf16[8,32,256]{2,1,0:T(8,128)(2,1)S(1)}, u32[]{:S(2)}, u32[]{:S(2)}) collective-permute-start(bf16[8,32,256]{2,1,0:T(8,128)(2,1)S(1)} %collective-permute-done.11.refs_1_), channel_id=1, source_target_pairs={{0,1},{1,0},{2,3},{3,2},{4,5},{5,4},{6,7},{7,6},{8,9},{9,8},{10,11... | collective-permute-start | bytes 393224 | tf_op jit(solution)/shard_map/ppermute | solution.py:291
  83.9 2.2 %collective-permute-start.16 = (bf16[8,32,256]{2,1,0:T(8,128)(2,1)S(1)}, bf16[8,32,256]{2,1,0:T(8,128)(2,1)S(1)}, u32[]{:S(2)}, u32[]{:S(2)}) collective-permute-start(bf16[8,32,256]{2,1,0:T(8,128)(2,1)S(1)} %collective-permute-done.12.refs_2_), channel_id=1, source_target_pairs={{0,1},{1,0},{2,3},{3,2},{4,5},{5,4},{6,7},{7,6},{8,9},{9,8},{10,11... | collective-permute-start | bytes 393224 | tf_op jit(solution)/shard_map/ppermute | solution.py:291
  86.1 0.6 collective-permute-start.17
  86.7 13.0 %encode.1 = (bf16[256,2048]{1,0:T(8,128)(2,1)}, bf16[256,256]{1,0:T(8,128)(2,1)}, bf16[256,256]{1,0:T(8,128)(2,1)}) custom-call(s32[64]{0:T(128)} %anchor_ref.3, s32[64]{0:T(128)} %lengths_ref.3, bf16[256,2048]{1,0:T(8,128)(2,1)} %q_ref.1, bf16[256,256]{1,0:T(8,128)(2,1)} %k_ref.3, bf16[256,256]{1,0:T(8,128)(2,1)} %v_ref.3, bf16[8,96,256]{2,1,0:T(8,128)(2,1)} %copy-done.3), custom_call_target="tpu_custom_call" | custom-call | flops 1100000000 | bytes 3500000 | tf_op jit(solution)/shard_map/encode/pallas_call | solution.py:233
  99.7 0.0 collective-permute-done.14.refs_4_
  99.8 0.0 collective-permute-done.17.refs_7_
  99.8 0.6 copy-done.8
  100.4 0.1 copy-done.9
  100.5 0.1 copy-done.10
  100.5 0.6 copy-done.11
  101.2 5.0 %assemble.1 = bf16[8,4,8,2048]{3,2,1,0:T(8,128)(2,1)} custom-call(bf16[8,32,256]{2,1,0:T(8,128)(2,1)} %copy-done.4, bf16[8,32,256]{2,1,0:T(8,128)(2,1)} %copy-done.5, bf16[8,32,256]{2,1,0:T(8,128)(2,1)} %copy-done.6, bf16[8,32,256]{2,1,0:T(8,128)(2,1)} %copy-done.7, bf16[8,32,256]{2,1,0:T(8,128)(2,1)} %copy-done.8, bf16[8,32,256]{2,1,0:T(8,128)(2,1)} %copy-done.9, ...), custom_call_target="tpu_custom_call" | custom-call | tf_op jit(solution)/shard_map/assemble/pallas_call | solution.py:277
  (36 shorter events, 0.1 us)
Async XLA Ops:
  2.5 9.2 %copy-start = (bf16[512,256]{1,0:T(8,128)(2,1)S(1)}, bf16[512,256]{1,0:T(8,128)(2,1)}, u32[]{:S(2)}) copy-start(bf16[512,256]{1,0:T(8,128)(2,1)} %get-tuple-element.10.refs_0_) | copy-start | bytes 786436
  2.5 27.6 %all-to-all-start = ((bf16[8,96,256]{2,1,0:T(8,128)(2,1)}), bf16[8,96,256]{2,1,0:T(8,128)(2,1)S(1)}, u32[]{:S(2)}, u32[]{:S(2)}) async-start(bf16[8,96,256]{2,1,0:T(8,128)(2,1)} %get-tuple-element.9), calls=%async_computation | async-start | bytes 786432 | tf_op jit(solution)/shard_map/all_to_all | solution.py:297
  11.6 18.4 %copy-start.1 = (s32[64]{0:T(128)S(1)}, s32[64]{0:T(128)}, u32[]{:S(2)}) copy-start(s32[64]{0:T(128)} %lengths_ref.3) | copy-start | bytes 772
  11.6 8.3 %collective-permute-start = (bf16[512,256]{1,0:T(8,128)(2,1)S(1)}, bf16[512,256]{1,0:T(8,128)(2,1)S(1)}, u32[]{:S(2)}, u32[]{:S(2)}) collective-permute-start(bf16[512,256]{1,0:T(8,128)(2,1)S(1)} %copy-done), channel_id=1, source_target_pairs={{0,2},{1,3},{2,4},{3,5},{4,6},{5,7},{6,0},{7,1},{8,10},{9,11},{10,... | collective-permute-start | bytes 786440 | tf_op jit(solution)/shard_map/ppermute | solution.py:294
  13.0 13.6 %collective-permute-start.1 = (bf16[512,256]{1,0:T(8,128)(2,1)S(1)}, bf16[512,256]{1,0:T(8,128)(2,1)S(1)}, u32[]{:S(2)}, u32[]{:S(2)}) collective-permute-start(bf16[512,256]{1,0:T(8,128)(2,1)S(1)} %copy-done), channel_id=1, source_target_pairs={{0,4},{1,5},{2,6},{3,7},{4,0},{5,1},{6,2},{7,3},{8,12},{9,13},{10,... | collective-permute-start | bytes 786440 | tf_op jit(solution)/shard_map/ppermute | solution.py:294
  15.6 12.9 %collective-permute-start.2 = (bf16[512,256]{1,0:T(8,128)(2,1)S(1)}, bf16[512,256]{1,0:T(8,128)(2,1)S(1)}, u32[]{:S(2)}, u32[]{:S(2)}) collective-permute-start(bf16[512,256]{1,0:T(8,128)(2,1)S(1)} %copy-done), channel_id=1, source_target_pairs={{0,6},{1,7},{2,0},{3,1},{4,2},{5,3},{6,4},{7,5},{8,14},{9,15},{10,... | collective-permute-start | bytes 786440 | tf_op jit(solution)/shard_map/ppermute | solution.py:294
  16.7 11.8 %collective-permute-start.3 = (bf16[512,256]{1,0:T(8,128)(2,1)S(1)}, bf16[512,256]{1,0:T(8,128)(2,1)S(1)}, u32[]{:S(2)}, u32[]{:S(2)}) collective-permute-start(bf16[512,256]{1,0:T(8,128)(2,1)S(1)} %copy-done), channel_id=1, source_target_pairs={{0,1},{1,0},{2,3},{3,2},{4,5},{5,4},{6,7},{7,6},{8,9},{9,8},{10,11... | collective-permute-start | bytes 786440 | tf_op jit(solution)/shard_map/ppermute | solution.py:291
  19.9 8.6 %collective-permute-start.4 = (bf16[512,256]{1,0:T(8,128)(2,1)S(1)}, bf16[512,256]{1,0:T(8,128)(2,1)S(1)}, u32[]{:S(2)}, u32[]{:S(2)}) collective-permute-start(bf16[512,256]{1,0:T(8,128)(2,1)S(1)} %collective-permute-done.refs_1_), channel_id=1, source_target_pairs={{0,1},{1,0},{2,3},{3,2},{4,5},{5,4},{6,7},{7,6},{8,9},{9,8},{10,11... | collective-permute-start | bytes 786440 | tf_op jit(solution)/shard_map/ppermute | solution.py:291
  26.7 3.0 %collective-permute-start.5 = (bf16[512,256]{1,0:T(8,128)(2,1)S(1)}, bf16[512,256]{1,0:T(8,128)(2,1)S(1)}, u32[]{:S(2)}, u32[]{:S(2)}) collective-permute-start(bf16[512,256]{1,0:T(8,128)(2,1)S(1)} %collective-permute-done.1.refs_2_), channel_id=1, source_target_pairs={{0,1},{1,0},{2,3},{3,2},{4,5},{5,4},{6,7},{7,6},{8,9},{9,8},{10,11... | collective-permute-start | bytes 786440 | tf_op jit(solution)/shard_map/ppermute | solution.py:291
  28.5 1.5 %collective-permute-start.6 = (bf16[512,256]{1,0:T(8,128)(2,1)S(1)}, bf16[512,256]{1,0:T(8,128)(2,1)S(1)}, u32[]{:S(2)}, u32[]{:S(2)}) collective-permute-start(bf16[512,256]{1,0:T(8,128)(2,1)S(1)} %collective-permute-done.2.refs_3_), channel_id=1, source_target_pairs={{0,1},{1,0},{2,3},{3,2},{4,5},{5,4},{6,7},{7,6},{8,9},{9,8},{10,11... | collective-permute-start | bytes 786440 | tf_op jit(solution)/shard_map/ppermute | solution.py:291
  36.0 19.0 %all-to-all-start.1 = ((f32[8,72,128]{2,1,0:T(8,128)}), f32[8,72,128]{2,1,0:T(8,128)S(1)}, u32[]{:S(2)}, u32[]{:S(2)}) async-start(f32[8,72,128]{2,1,0:T(8,128)} %question_pass.1), calls=%async_computation.1 | async-start | bytes 589824 | tf_op jit(solution)/shard_map/all_to_all | solution.py:297
  42.6 0.7 copy-start.16
  43.5 1.6 %collective-permute-start.7 = (bf16[64,256]{1,0:T(8,128)(2,1)S(1)}, bf16[64,256]{1,0:T(8,128)(2,1)S(1)}, u32[]{:S(2)}, u32[]{:S(2)}) collective-permute-start(bf16[64,256]{1,0:T(8,128)(2,1)S(1)} %dynamic-slice_bitcast_fusion), channel_id=1, source_target_pairs={{0,1},{1,0},{2,3},{3,2},{4,5},{5,4},{6,7},{7,6},{8,9},{9,8},{10,11... | collective-permute-start | bytes 98312 | tf_op jit(solution)/shard_map/ppermute | solution.py:291
  45.1 9.9 %copy-start.12 = (bf16[64,256]{1,0:T(8,128)(2,1)}, bf16[64,256]{1,0:T(8,128)(2,1)S(1)}, u32[]{:S(2)}) copy-start(bf16[64,256]{1,0:T(8,128)(2,1)S(1)} %broadcast_select_fusion.refs_0_) | copy-start | bytes 98308
  45.1 4.1 %collective-permute-start.10 = (bf16[64,256]{1,0:T(8,128)(2,1)S(1)}, bf16[64,256]{1,0:T(8,128)(2,1)S(1)}, u32[]{:S(2)}, u32[]{:S(2)}) collective-permute-start(bf16[64,256]{1,0:T(8,128)(2,1)S(1)} %broadcast_select_fusion.refs_0_), channel_id=1, source_target_pairs={{0,6},{1,7},{2,0},{3,1},{4,2},{5,3},{6,4},{7,5},{8,14},{9,15},{10,... | collective-permute-start | bytes 98312 | tf_op jit(solution)/shard_map/ppermute | solution.py:294
  46.7 4.3 %collective-permute-start.8 = (bf16[64,256]{1,0:T(8,128)(2,1)S(1)}, bf16[64,256]{1,0:T(8,128)(2,1)S(1)}, u32[]{:S(2)}, u32[]{:S(2)}) collective-permute-start(bf16[64,256]{1,0:T(8,128)(2,1)S(1)} %broadcast_select_fusion.refs_0_), channel_id=1, source_target_pairs={{0,2},{1,3},{2,4},{3,5},{4,6},{5,7},{6,0},{7,1},{8,10},{9,11},{10,... | collective-permute-start | bytes 98312 | tf_op jit(solution)/shard_map/ppermute | solution.py:294
  46.7 4.9 %collective-permute-start.9 = (bf16[64,256]{1,0:T(8,128)(2,1)S(1)}, bf16[64,256]{1,0:T(8,128)(2,1)S(1)}, u32[]{:S(2)}, u32[]{:S(2)}) collective-permute-start(bf16[64,256]{1,0:T(8,128)(2,1)S(1)} %broadcast_select_fusion.refs_0_), channel_id=1, source_target_pairs={{0,4},{1,5},{2,6},{3,7},{4,0},{5,1},{6,2},{7,3},{8,12},{9,13},{10,... | collective-permute-start | bytes 98312 | tf_op jit(solution)/shard_map/ppermute | solution.py:294
  49.2 5.8 %copy-start.13 = (bf16[64,256]{1,0:T(8,128)(2,1)}, bf16[64,256]{1,0:T(8,128)(2,1)S(1)}, u32[]{:S(2)}) copy-start(bf16[64,256]{1,0:T(8,128)(2,1)S(1)} %collective-permute-done.10.refs_3_) | copy-start | bytes 98308
  51.0 4.0 %copy-start.14 = (bf16[64,256]{1,0:T(8,128)(2,1)}, bf16[64,256]{1,0:T(8,128)(2,1)S(1)}, u32[]{:S(2)}) copy-start(bf16[64,256]{1,0:T(8,128)(2,1)S(1)} %collective-permute-done.8.refs_1_) | copy-start | bytes 98308
  51.6 3.5 %copy-start.15 = (bf16[64,256]{1,0:T(8,128)(2,1)}, bf16[64,256]{1,0:T(8,128)(2,1)S(1)}, u32[]{:S(2)}) copy-start(bf16[64,256]{1,0:T(8,128)(2,1)S(1)} %collective-permute-done.9.refs_2_) | copy-start | bytes 98308
  55.1 0.7 copy-start.2
  73.6 13.1 %copy-start.3 = (bf16[8,96,256]{2,1,0:T(8,128)(2,1)}, bf16[8,96,256]{2,1,0:T(8,128)(2,1)S(1)}, u32[]{:S(2)}) copy-start(bf16[8,96,256]{2,1,0:T(8,128)(2,1)S(1)} %all_to_all.15.got_ref) | copy-start | bytes 1179652
  73.6 26.1 %copy-start.4 = (bf16[8,32,256]{2,1,0:T(8,128)(2,1)}, bf16[8,32,256]{2,1,0:T(8,128)(2,1)S(1)}, u32[]{:S(2)}) copy-start(bf16[8,32,256]{2,1,0:T(8,128)(2,1)S(1)} %slice.13.refs_0_) | copy-start | bytes 393220
  73.6 8.7 %collective-permute-start.11 = (bf16[8,32,256]{2,1,0:T(8,128)(2,1)S(1)}, bf16[8,32,256]{2,1,0:T(8,128)(2,1)S(1)}, u32[]{:S(2)}, u32[]{:S(2)}) collective-permute-start(bf16[8,32,256]{2,1,0:T(8,128)(2,1)S(1)} %slice.13.refs_0_), channel_id=1, source_target_pairs={{0,2},{1,3},{2,4},{3,5},{4,6},{5,7},{6,0},{7,1},{8,10},{9,11},{10,... | collective-permute-start | bytes 393224 | tf_op jit(solution)/shard_map/ppermute | solution.py:294
  74.0 9.9 %collective-permute-start.12 = (bf16[8,32,256]{2,1,0:T(8,128)(2,1)S(1)}, bf16[8,32,256]{2,1,0:T(8,128)(2,1)S(1)}, u32[]{:S(2)}, u32[]{:S(2)}) collective-permute-start(bf16[8,32,256]{2,1,0:T(8,128)(2,1)S(1)} %slice.13.refs_0_), channel_id=1, source_target_pairs={{0,4},{1,5},{2,6},{3,7},{4,0},{5,1},{6,2},{7,3},{8,12},{9,13},{10,... | collective-permute-start | bytes 393224 | tf_op jit(solution)/shard_map/ppermute | solution.py:294
  77.1 9.0 %collective-permute-start.13 = (bf16[8,32,256]{2,1,0:T(8,128)(2,1)S(1)}, bf16[8,32,256]{2,1,0:T(8,128)(2,1)S(1)}, u32[]{:S(2)}, u32[]{:S(2)}) collective-permute-start(bf16[8,32,256]{2,1,0:T(8,128)(2,1)S(1)} %slice.13.refs_0_), channel_id=1, source_target_pairs={{0,6},{1,7},{2,0},{3,1},{4,2},{5,3},{6,4},{7,5},{8,14},{9,15},{10,... | collective-permute-start | bytes 393224 | tf_op jit(solution)/shard_map/ppermute | solution.py:294
  77.5 22.2 %collective-permute-start.14 = (bf16[8,32,256]{2,1,0:T(8,128)(2,1)S(1)}, bf16[8,32,256]{2,1,0:T(8,128)(2,1)S(1)}, u32[]{:S(2)}, u32[]{:S(2)}) collective-permute-start(bf16[8,32,256]{2,1,0:T(8,128)(2,1)S(1)} %slice.13.refs_0_), channel_id=1, source_target_pairs={{0,1},{1,0},{2,3},{3,2},{4,5},{5,4},{6,7},{7,6},{8,9},{9,8},{10,11... | collective-permute-start | bytes 393224 | tf_op jit(solution)/shard_map/ppermute | solution.py:291
  82.3 17.4 %copy-start.5 = (bf16[8,32,256]{2,1,0:T(8,128)(2,1)}, bf16[8,32,256]{2,1,0:T(8,128)(2,1)S(1)}, u32[]{:S(2)}) copy-start(bf16[8,32,256]{2,1,0:T(8,128)(2,1)S(1)} %collective-permute-done.11.refs_1_) | copy-start | bytes 393220
  82.3 17.5 %collective-permute-start.15 = (bf16[8,32,256]{2,1,0:T(8,128)(2,1)S(1)}, bf16[8,32,256]{2,1,0:T(8,128)(2,1)S(1)}, u32[]{:S(2)}, u32[]{:S(2)}) collective-permute-start(bf16[8,32,256]{2,1,0:T(8,128)(2,1)S(1)} %collective-permute-done.11.refs_1_), channel_id=1, source_target_pairs={{0,1},{1,0},{2,3},{3,2},{4,5},{5,4},{6,7},{7,6},{8,9},{9,8},{10,11... | collective-permute-start | bytes 393224 | tf_op jit(solution)/shard_map/ppermute | solution.py:291
  83.9 15.9 %copy-start.6 = (bf16[8,32,256]{2,1,0:T(8,128)(2,1)}, bf16[8,32,256]{2,1,0:T(8,128)(2,1)S(1)}, u32[]{:S(2)}) copy-start(bf16[8,32,256]{2,1,0:T(8,128)(2,1)S(1)} %collective-permute-done.12.refs_2_) | copy-start | bytes 393220
  83.9 15.9 %collective-permute-start.16 = (bf16[8,32,256]{2,1,0:T(8,128)(2,1)S(1)}, bf16[8,32,256]{2,1,0:T(8,128)(2,1)S(1)}, u32[]{:S(2)}, u32[]{:S(2)}) collective-permute-start(bf16[8,32,256]{2,1,0:T(8,128)(2,1)S(1)} %collective-permute-done.12.refs_2_), channel_id=1, source_target_pairs={{0,1},{1,0},{2,3},{3,2},{4,5},{5,4},{6,7},{7,6},{8,9},{9,8},{10,11... | collective-permute-start | bytes 393224 | tf_op jit(solution)/shard_map/ppermute | solution.py:291
  86.1 13.6 %copy-start.7 = (bf16[8,32,256]{2,1,0:T(8,128)(2,1)}, bf16[8,32,256]{2,1,0:T(8,128)(2,1)S(1)}, u32[]{:S(2)}) copy-start(bf16[8,32,256]{2,1,0:T(8,128)(2,1)S(1)} %collective-permute-done.13.refs_3_) | copy-start | bytes 393220
  86.1 13.7 %collective-permute-start.17 = (bf16[8,32,256]{2,1,0:T(8,128)(2,1)S(1)}, bf16[8,32,256]{2,1,0:T(8,128)(2,1)S(1)}, u32[]{:S(2)}, u32[]{:S(2)}) collective-permute-start(bf16[8,32,256]{2,1,0:T(8,128)(2,1)S(1)} %collective-permute-done.13.refs_3_), channel_id=1, source_target_pairs={{0,1},{1,0},{2,3},{3,2},{4,5},{5,4},{6,7},{7,6},{8,9},{9,8},{10,11... | collective-permute-start | bytes 393224 | tf_op jit(solution)/shard_map/ppermute | solution.py:291
  99.7 0.7 copy-start.8
  99.8 0.7 copy-start.9
  99.8 0.7 copy-start.10
  100.5 0.6 copy-start.11

commit v2 on v1

v2 whole, which is shorter than its diff:
```python
import functools
import math

import jax
import jax.numpy as jnp
from jax import lax
from jax.experimental import pallas as pl
from jax.experimental.pallas import tpu as pltpu
from jax.sharding import PartitionSpec as P

HD = 128
SC = HD ** (-0.5)
SC2 = SC * math.log2(math.e)
NZ, NY, NC = 8, 4, 2
BLK = 256
BF = jnp.bfloat16
F32 = jnp.float32
SMEM = pl.BlockSpec(memory_space=pltpu.SMEM)
VMEM = pl.BlockSpec(memory_space=pltpu.VMEM)
PARAMS = pltpu.CompilerParams(vmem_limit_bytes=20 * 1024 * 1024)


def index_of(z, y, c):
    return (z * NY + y) * NC + c


def permutation(move):
    return [
        (index_of(z, y, c), index_of(*move(z, y, c)))
        for z in range(NZ)
        for y in range(NY)
        for c in range(NC)
    ]


Z_GROUPS = [[index_of(z, y, c) for z in range(NZ)] for y in range(NY) for c in range(NC)]
CHIP_GROUPS = [[index_of(z, y, c) for z in range(NZ) for y in range(NY)] for c in range(NC)]
OTHER_CORE = permutation(lambda z, y, c: (z, y, 1 - c))
Y_SHIFTS = [permutation(lambda z, y, c, d=d: (z, (y + d) % NY, c)) for d in range(NY)]
Z_SHIFTS = [permutation(lambda z, y, c, d=d: ((z + d) % NZ, y, c)) for d in range(NZ)]


def coordinates():
    place = lax.axis_index("ctx")
    return place // (NY * NC), (place // NC) % NY, place % NC


def sign_table():
    shape = (HD, HD)
    both = lax.broadcasted_iota(jnp.int32, shape, 0) & lax.broadcasted_iota(jnp.int32, shape, 1)
    both = both ^ (both >> 4)
    both = both ^ (both >> 2)
    both = both ^ (both >> 1)
    return (1 - 2 * (both & 1)).astype(F32).astype(BF)


def across(a, b):
    return lax.dot_general(a, b, (((1,), (1,)), ((), ())), preferred_element_type=F32)


def dot(a, b):
    return jnp.dot(a, b, preferred_element_type=F32)


def rotated(rows, table):
    return (dot(rows, table) * SC).astype(BF)


def join_kernel(k_ref, v_ref, both_ref, sems):
    copies = [
        pltpu.make_async_copy(k_ref, both_ref.at[0:BLK, :], sems.at[0]),
        pltpu.make_async_copy(v_ref, both_ref.at[BLK : 2 * BLK, :], sems.at[1]),
    ]
    for copy in copies:
        copy.start()
    for copy in copies:
        copy.wait()


def join(k, v):
    return pl.pallas_call(
        join_kernel,
        out_shape=jax.ShapeDtypeStruct((2 * BLK, 256), BF),
        in_specs=[pl.BlockSpec(memory_space=pl.ANY)] * 2,
        out_specs=VMEM,
        scratch_shapes=[pltpu.SemaphoreType.DMA((2,))],
        name="join",
    )(k, v)


def repeat_kernel(question_ref, send_ref, scratch_ref):
    question = question_ref[...].astype(F32)
    for k in range(8):
        scratch_ref[4 * k : 4 * k + 4, :] = question[:, 256 * k : 256 * k + 256]
    rows = scratch_ref[...].astype(BF)
    for i in range(NZ):
        send_ref[i] = rows


def repeat(question):
    return pl.pallas_call(
        repeat_kernel,
        out_shape=jax.ShapeDtypeStruct((NZ, 32, 256), BF),
        in_specs=[VMEM],
        out_specs=VMEM,
        scratch_shapes=[pltpu.VMEM((32, 256), F32)],
        name="repeat",
    )(question)


def gate_kernel(*refs):
    pass


def gate(arrays, token):
    anywhere = pl.BlockSpec(memory_space=pl.ANY)
    return pl.pallas_call(
        gate_kernel,
        out_shape=[jax.ShapeDtypeStruct(x.shape, x.dtype) for x in arrays],
        in_specs=[anywhere] * (len(arrays) + 1),
        out_specs=[anywhere] * len(arrays),
        input_output_aliases={i: i for i in range(len(arrays))},
        compiler_params=pltpu.CompilerParams(vmem_limit_bytes=1024 * 1024),
        name="gate",
    )(*arrays, token)


def pick_kernel(anchor_ref, *refs):
    blocks, out_ref, sems = refs[:8], refs[8], refs[9]
    z, y, c = coordinates()
    wanted = lax.rem(anchor_ref[0], NY * NC)
    first = pl.multiple_of(64 * y, 64)
    for which in range(8):
        core = c if which < NY else 1 - c
        place = NC * lax.rem(y + NY - which % NY, NY) + core

        @pl.when(place == wanted)
        def _(which=which):
            copies = [
                pltpu.make_async_copy(
                    blocks[which].at[pl.ds(first + BLK * i, 64), :],
                    out_ref.at[64 * i : 64 * i + 64, :],
                    sems.at[i],
                )
                for i in range(2)
            ]
            for copy in copies:
                copy.start()
            for copy in copies:
                copy.wait()


def pick(anchor_index, blocks):
    anywhere = pl.BlockSpec(memory_space=pl.ANY)
    return pl.pallas_call(
        pick_kernel,
        out_shape=jax.ShapeDtypeStruct((HD, 256), BF),
        in_specs=[SMEM] + [anywhere] * 8,
        out_specs=VMEM,
        scratch_shapes=[pltpu.SemaphoreType.DMA((2,))],
        compiler_params=pltpu.CompilerParams(vmem_limit_bytes=1024 * 1024),
        name="pick",
    )(anchor_index, *blocks)


def thirds(x):
    high = x.astype(BF)
    rest = x - high.astype(F32)
    middle = rest.astype(BF)
    return high, middle, (rest - middle.astype(F32)).astype(BF)


def question_kernel(lengths_ref, got_ref, *refs):
    blocks, send_ref = refs[:8], refs[8]
    z, y, c = coordinates()
    table = sign_table()
    lane = lax.broadcasted_iota(jnp.int32, (BLK, BLK), 1)
    ids = [index_of(z, lax.rem(y + NY - d, NY), c) for d in range(NY)]
    ids += [index_of(z, lax.rem(y + NY - d, NY), 1 - c) for d in range(NY)]
    stats = []
    for g in range(2):
        lanes = slice(HD * g, HD * g + HD)
        halves = [
            got_ref[:, 16 * g : 16 * g + 16, HD * half : HD * half + HD].reshape(NZ * 16, HD)
            for half in range(2)
        ]
        q = rotated(jnp.concatenate(halves, axis=0), table)
        top = total = summed = None
        for which in range(8):
            k = rotated(blocks[which][0:BLK, lanes], table)
            v = rotated(blocks[which][BLK : 2 * BLK, lanes], table)
            part = jnp.where(lane < lengths_ref[ids[which]], across(q, k) * SC2, -jnp.inf)
            m = jnp.max(part, axis=1, keepdims=True)
            e = jnp.exp2(part - m)
            d = jnp.sum(e, axis=1, keepdims=True)
            n = dot(e.astype(BF), v)
            if which == 0:
                top, total, summed = m, d, n
            else:
                new = jnp.maximum(top, m)
                old_scale, scale = jnp.exp2(top - new), jnp.exp2(m - new)
                top = new
                total = total * old_scale + d * scale
                summed = summed * old_scale + n * scale
        for half in range(2):
            rows = slice(HD * half, HD * half + HD)
            at = 16 * (2 * g + half)
            send_ref[:, at : at + 16, :] = summed[rows].reshape(NZ, 16, HD)
            stats.append((top[rows], total[rows]))
    lanes = lax.broadcasted_iota(jnp.int32, (HD, HD), 1)
    packed = jnp.zeros((HD, HD), F32)
    for i in range(4):
        packed = jnp.where(lanes == i, stats[i][0], packed)
        packed = jnp.where(lanes == 4 + i, stats[i][1], packed)
    tile = packed.T[0:8, :]
    for i in range(NZ):
        send_ref[i, 64:72, :] = tile


def question_pass(lengths, got, blocks):
    return pl.pallas_call(
        question_kernel,
        out_shape=jax.ShapeDtypeStruct((NZ, 72, HD), F32),
        in_specs=[SMEM] + [VMEM] * 9,
        out_specs=VMEM,
        compiler_params=PARAMS,
        cost_estimate=pl.CostEstimate(
            flops=900_000_000, bytes_accessed=2_500_000, transcendentals=1_100_000
        ),
        name="question_pass",
    )(lengths, got, *blocks)


def combine_kernel(limit_ref, parts_ref, piece_ref, send_ref, columns_ref):
    z, y, c = coordinates()
    table = sign_table()
    tiles = [parts_ref[s, 64:72, :] for s in range(NZ)]
    square = jnp.concatenate(tiles + [jnp.zeros((HD - 64, HD), F32)], axis=0)
    columns_ref[...] = square.T
    columns = columns_ref[pl.ds(pl.multiple_of(z * 16, 16), 16), :]
    row = lax.broadcasted_iota(jnp.int32, (64, HD), 0)
    results = []
    for i in range(4):
        tops = [columns[:, 8 * s + i : 8 * s + i + 1] for s in range(NZ)]
        peak = functools.reduce(jnp.maximum, tops)
        total = jnp.zeros((16, 1), F32)
        summed = jnp.zeros((16, HD), F32)
        for s in range(NZ):
            scale = jnp.exp2(tops[s] - peak)
            total = total + scale * columns[:, 8 * s + 4 + i : 8 * s + 5 + i]
            summed = summed + scale * parts_ref[s, 16 * i : 16 * i + 16, :]
        results.append(summed / total)
    high, middle, low = thirds(jnp.concatenate(results, axis=0))
    back = (dot(low, table) + dot(middle, table) + dot(high, table)) * SC
    position = index_of(z, y, c) * 4 + (row & 3)
    back = jnp.where(position < limit_ref[0], back, 0.0).astype(BF)
    for i in range(NZ * NY):
        send_ref[i] = back


def combine(limit, parts, piece):
    return pl.pallas_call(
        combine_kernel,
        out_shape=jax.ShapeDtypeStruct((NZ * NY, 64, HD), BF),
        in_specs=[SMEM, VMEM, pl.BlockSpec(memory_space=pl.ANY)],
        out_specs=VMEM,
        scratch_shapes=[pltpu.VMEM((HD, HD), F32)],
        compiler_params=PARAMS,
        name="combine",
    )(limit, parts, piece)


def encode_kernel(anchor_ref, lengths_ref, q_ref, k_ref, v_ref, *refs):
    pieces = refs[:NY]
    mixed_ref, krot_ref, vrot_ref, far_k_ref, far_v_ref = refs[NY:]
    z, y, c = coordinates()
    place = index_of(z, y, c)
    anchor = anchor_ref[0]
    k, v = k_ref[...], v_ref[...]
    table = sign_table()
    krot_ref[...] = rotated(k, table)
    vrot_ref[...] = rotated(v, table)
    for d in range(NY):
        at = pl.multiple_of(64 * lax.rem(y + NY - d, NY), 64)
        far_k_ref[pl.ds(at, 64), :] = pieces[d][0:64, :]
        far_v_ref[pl.ds(at, 64), :] = pieces[d][64:128, :]
    far_k, far_v = far_k_ref[...], far_v_ref[...]
    far_len = jnp.where(place == anchor, 0, lengths_ref[anchor])
    own_len = lengths_ref[place]
    query = lax.broadcasted_iota(jnp.int32, (BLK, BLK), 0)
    key = lax.broadcasted_iota(jnp.int32, (BLK, BLK), 1)
    far_ok = key < far_len
    own_ok = (key <= query) & (key < own_len)
    for j in range(8):
        q = q_ref[:, HD * j : HD * j + HD]
        s_far = jnp.where(far_ok, across(q, far_k) * SC2, -jnp.inf)
        s_own = jnp.where(own_ok, across(q, k) * SC2, -jnp.inf)
        top = jnp.max(jnp.maximum(s_far, s_own), axis=1, keepdims=True)
        e_far = jnp.exp2(s_far - top)
        e_own = jnp.exp2(s_own - top)
        total = jnp.sum(e_far + e_own, axis=1, keepdims=True)
        summed = dot(e_far.astype(BF), far_v) + dot(e_own.astype(BF), v)
        mixed_ref[:, HD * j : HD * j + HD] = (summed / total).astype(BF)


def encode(anchor_index, lengths, q, k, v, pieces):
    heads = pl.BlockSpec((BLK, 8 * HD), lambda g: (0, g))
    group = pl.BlockSpec((BLK, HD), lambda g: (0, g))
    piece = pl.BlockSpec((HD, HD), lambda g: (0, g))
    return pl.pallas_call(
        encode_kernel,
        grid=(2,),
        out_shape=(
            jax.ShapeDtypeStruct(q.shape, BF),
            jax.ShapeDtypeStruct(k.shape, BF),
            jax.ShapeDtypeStruct(v.shape, BF),
        ),
        in_specs=[SMEM, SMEM, heads, group, group] + [piece] * NY,
        out_specs=(heads, group, group),
        scratch_shapes=[pltpu.VMEM((BLK, HD), BF), pltpu.VMEM((BLK, HD), BF)],
        compiler_params=PARAMS,
        cost_estimate=pl.CostEstimate(
            flops=1_100_000_000, bytes_accessed=3_500_000, transcendentals=2_100_000
        ),
        name="encode",
    )(anchor_index, lengths, q, k, v, *pieces)


def assemble_kernel(own_ref, other_ref, out_ref):
    c = coordinates()[2]
    upper = lax.broadcasted_iota(jnp.int32, (8, HD), 0) < 4
    for pair in range(4):
        sources = []
        for i in (2 * pair, 2 * pair + 1):
            mine = own_ref[i].astype(F32)
            theirs = other_ref[i].astype(F32)
            sources.append((jnp.where(c == 0, mine, theirs), jnp.where(c == 0, theirs, mine)))
        for at in range(8):
            evens, odds = [], []
            for first, second in sources:
                a, b = first[8 * at : 8 * at + 8], second[8 * at : 8 * at + 8]
                evens.append(jnp.where(upper, a, pltpu.roll(b, 4, 0)))
                odds.append(jnp.where(upper, pltpu.roll(a, 4, 0), b))
            g, half, pair_of = at // 4, at // 2 % 2, at % 2
            head = 8 * g + 4 * pair_of + half
            rows = slice(16 * pair, 16 * pair + 16)
            out_ref[rows, HD * head : HD * head + HD] = jnp.concatenate(evens, axis=0).astype(BF)
            head = head + 2
            out_ref[rows, HD * head : HD * head + HD] = jnp.concatenate(odds, axis=0).astype(BF)


def assemble(own, other):
    part = pl.BlockSpec((8, 64, HD), lambda i: (i, 0, 0))
    return pl.pallas_call(
        assemble_kernel,
        grid=(4,),
        out_shape=jax.ShapeDtypeStruct((256, 2048), BF),
        in_specs=[part] * 2,
        out_specs=pl.BlockSpec((64, 2048), lambda i: (i, 0)),
        compiler_params=PARAMS,
        name="assemble",
    )(own, other)


def on_device(
    context_q, context_k, context_v, question, block_lengths, anchor_index, question_length
):
    def swap(x):
        return lax.ppermute(x, "ctx", OTHER_CORE)

    def along_y(x):
        return [x] + [lax.ppermute(x, "ctx", Y_SHIFTS[d]) for d in range(1, NY)]

    def along_z(x, d):
        return lax.ppermute(x, "ctx", Z_SHIFTS[d]), lax.ppermute(x, "ctx", Z_SHIFTS[NZ - d])

    def with_other_core(parts):
        return parts + [swap(x) for x in parts]

    both = join(context_k, context_v)
    blocks = along_y(both)
    got = lax.all_to_all(repeat(question), "ctx", 0, 0, axis_index_groups=Z_GROUPS)
    blocks = with_other_core([both, *gate(blocks[1:], got)])
    piece = pick(anchor_index, blocks)
    below, above = along_z(piece, 1)
    send = question_pass(block_lengths, got, blocks)
    parts = lax.all_to_all(send, "ctx", 0, 0, axis_index_groups=Z_GROUPS)
    distance = (lax.axis_index("ctx") // (NY * NC) - anchor_index[0] // (NY * NC)) & (NZ - 1)
    piece = jnp.where(distance == 1, below, jnp.where(distance == NZ - 1, above, piece))
    below, above = along_z(piece, 3)
    near = (distance < 2) | (distance == NZ - 1)
    piece = jnp.where(near, piece, jnp.where(distance < 5, below, above))
    spread = combine(question_length, parts, piece)
    own = lax.all_to_all(spread, "ctx", 0, 0, axis_index_groups=CHIP_GROUPS)
    mixed, key_cache, value_cache = encode(
        anchor_index, block_lengths, context_q, context_k, context_v, along_y(piece)
    )
    (own,) = gate([own], key_cache)
    answer = assemble(own, swap(own))
    return mixed, key_cache, value_cache, answer


def solution(mesh):
    placed = (
        P("ctx", "heads"),
        P("ctx", "heads"),
        P("ctx", "heads"),
        P("ctx", "heads"),
        P(),
        P(),
        P(),
    )
    return jax.shard_map(
        on_device,
        mesh=mesh,
        in_specs=placed,
        out_specs=(P("ctx", "heads"), P("ctx", "heads"), P("ctx", "heads"), P(None, "heads")),
        check_vma=False,
    )
```

time: 108 us -> 86.4 us (0.80); the launches traced: 106 us -> 85.9 us
  blocking collectives: 15.4 us -> 0 us
  Pallas kernels: 28.2 us -> 19.7 us
  waiting for transfers between devices: 14.3 us -> 19.9 us
  local copies, waits for them, and re-layouts: 2.8 us -> 1.58 us
    all_to_all x1 -> x0, blocking collectives: 15.4 us -> none  [over_z(): return lax.all_to_all(x, 'ctx', 0, 0, axis_index_groups=Z_GROUPS)]
    pallas_call x4 -> x8, Pallas kernels: 22.3 us -> 13.8 us  [the longest x1 6.79 us: encode(): pl.pallas_call(encode_kernel, grid=(2,), out_shape=(jax.ShapeDtypeStruct(...]
    ppermute x9 -> x5, starting transfers between devices: 15.7 us -> 8.34 us  [swap(): return lax.ppermute(x, 'ctx', OTHER_CORE)]
    ppermute x0 -> x4, waiting for transfers between devices: none -> 6.4 us  [the longest x2 3.37 us: along_z(): lax.ppermute(x, 'ctx', Z_SHIFTS[NZ - d])]
    ppermute x0 -> x4, starting transfers between devices: none -> 6.01 us  [the longest x2 4.82 us: along_z(): lax.ppermute(x, 'ctx', Z_SHIFTS[NZ - d])]
    all_to_all x2 -> x3, starting transfers between devices: 15.8 us -> 20.4 us  [the longest x1 8.79 us: on_device(): own = lax.all_to_all(spread, 'ctx', 0, 0, axis_index_groups=CHIP_GROUPS)]
    ppermute x9 -> x6, starting transfers between devices: 12.4 us -> 8.35 us  [along_y(): return [x] + [lax.ppermute(x, 'ctx', Y_SHIFTS[d]) for d in range(1, NY)]]
    ppermute x9 -> x6, waiting for transfers between devices: 8.43 us -> 5.37 us  [along_y(): return [x] + [lax.ppermute(x, 'ctx', Y_SHIFTS[d]) for d in range(1, NY)]]
  transfers between devices with their start and end apart: 20 -> 18, of which waited for: 8 -> 9; matrix products, arithmetic and copies ran while one was open for 0% -> 0% of each run, Pallas kernels for 12% -> 16%
where the time goes in v2:
time: 86.4 us; the launch traced here: 85.9 us
  starting transfers between devices  43.1 us (50%)
  waiting for transfers between devices  19.9 us (23%)
  Pallas kernels  19.7 us (23%)
  between operations  1.62 us (2%)
  local copies, waits for them, and re-layouts  1.58 us (2%)
    all_to_all x1, starting transfers between devices, on_device(): own = lax.all_to_all(spread, 'ctx', 0, 0, axis_index_groups=CHIP_GROUPS)  8.79 us
    ppermute x6, starting transfers between devices, along_y(): return [x] + [lax.ppermute(x, 'ctx', Y_SHIFTS[d]) for d in range(1, NY)]  8.35 us
    ppermute x5, starting transfers between devices, swap(): return lax.ppermute(x, 'ctx', OTHER_CORE)  8.34 us
    all_to_all x1, starting transfers between devices, on_device(): lax.all_to_all(repeat(question), 'ctx', 0, 0, axis_index_groups=Z_GROUPS)  8.19 us
    pallas_call x1, Pallas kernels, encode(): pl.pallas_call(encode_kernel, grid=(2,), out_shape=(jax.ShapeDtypeStruct(...  6.79 us
    all_to_all x1, waiting for transfers between devices, on_device(): lax.all_to_all(repeat(question), 'ctx', 0, 0, axis_index_groups=Z_GROUPS)  6.04 us
    pallas_call x1, Pallas kernels, question_pass(): pl.pallas_call(question_kernel, out_shape=jax.ShapeDtypeStruct((NZ, 72, H...  5.87 us
    ppermute x6, waiting for transfers between devices, along_y(): return [x] + [lax.ppermute(x, 'ctx', Y_SHIFTS[d]) for d in range(1, NY)]  5.37 us
  transfers between devices with their start and end apart: 18, of which 9 were waited for; matrix products, arithmetic and copies ran while one was open for 0% of the time, Pallas kernels for 16%

profile of v2, /device:TPU:1, one launch (start us, length us, event | category | flops | bytes accessed | tf_op | source)
XLA Modules:
  0.0 85.9 jit_solution(4692333556515228361)
XLA Ops:
  0.6 1.7 %join.1.refs_0_ = bf16[512,256]{1,0:T(8,128)(2,1)} custom-call(bf16[256,256]{1,0:T(8,128)(2,1)} %k_ref.3, bf16[256,256]{1,0:T(8,128)(2,1)} %v_ref.3), custom_call_target="tpu_custom_call" | custom-call | tf_op jit(solution)/shard_map/join/pallas_call | solution.py:81
  2.3 0.0 copy-start
  2.3 3.6 %collective-permute-start.2 = (bf16[512,256]{1,0:T(8,128)(2,1)}, bf16[512,256]{1,0:T(8,128)(2,1)S(1)}, u32[]{:S(2)}, u32[]{:S(2)}) collective-permute-start(bf16[512,256]{1,0:T(8,128)(2,1)} %join.1.refs_0_), channel_id=1, source_target_pairs={{0,6},{1,7},{2,0},{3,1},{4,2},{5,3},{6,4},{7,5},{8,14},{9,15},{10,... | collective-permute-start | bytes 786440 | tf_op jit(solution)/shard_map/ppermute | solution.py:372
  6.0 0.3 collective-permute-start.1
  6.3 0.7 collective-permute-start
  7.0 1.4 %repeat.1 = bf16[8,32,256]{2,1,0:T(8,128)(2,1)} custom-call(bf16[4,2048]{1,0:T(4,128)(2,1)} %question_ref.1), custom_call_target="tpu_custom_call" | custom-call | tf_op jit(solution)/shard_map/repeat/pallas_call | solution.py:101
  8.4 8.2 %all-to-all-start = ((bf16[8,32,256]{2,1,0:T(8,128)(2,1)}), bf16[8,32,256]{2,1,0:T(8,128)(2,1)S(1)}, u32[]{:S(2)}, u32[]{:S(2)}) async-start(bf16[8,32,256]{2,1,0:T(8,128)(2,1)} %repeat.1), calls=%async_computation | async-start | bytes 262144 | tf_op jit(solution)/shard_map/all_to_all | solution.py:382
  16.6 1.9 %collective-permute-start.3 = (bf16[512,256]{1,0:T(8,128)(2,1)S(1)}, bf16[512,256]{1,0:T(8,128)(2,1)S(1)}, u32[]{:S(2)}, u32[]{:S(2)}) collective-permute-start(bf16[512,256]{1,0:T(8,128)(2,1)S(1)} %copy-done), channel_id=1, source_target_pairs={{0,1},{1,0},{2,3},{3,2},{4,5},{5,4},{6,7},{7,6},{8,9},{9,8},{10,11... | collective-permute-start | bytes 786440 | tf_op jit(solution)/shard_map/ppermute | solution.py:369
  18.5 6.0 %all-to-all-done.refs_3_.got_ref = bf16[8,32,256]{2,1,0:T(8,128)(2,1)S(1)} async-done(((bf16[8,32,256]{2,1,0:T(8,128)(2,1)}), bf16[8,32,256]{2,1,0:T(8,128)(2,1)S(1)}, u32[]{:S(2)}, u32[]{:S(2)}) %all-to-all-start) | async-done | bytes 131104 | tf_op jit(solution)/shard_map/all_to_all | solution.py:382
  24.5 0.0 collective-permute-done.2.refs_2_
  24.5 0.0 collective-permute-done.1.refs_1_
  24.5 0.0 collective-permute-done.refs_0_
  24.6 3.0 %collective-permute-start.4 = (bf16[512,256]{1,0:T(8,128)(2,1)S(1)}, bf16[512,256]{1,0:T(8,128)(2,1)S(1)}, u32[]{:S(2)}, u32[]{:S(2)}) collective-permute-start(bf16[512,256]{1,0:T(8,128)(2,1)S(1)} %get-tuple-element.10.refs_1_), channel_id=1, source_target_pairs={{0,1},{1,0},{2,3},{3,2},{4,5},{5,4},{6,7},{7,6},{8,9},{9,8},{10,11... | collective-permute-start | bytes 786440 | tf_op jit(solution)/shard_map/ppermute | solution.py:369
  27.6 0.1 collective-permute-start.5
  27.7 0.4 collective-permute-start.6
  28.1 0.7 copy-done.4
  28.9 0.0 copy-start.6
  28.9 0.0 collective-permute-done.3.refs_4_
  28.9 0.0 collective-permute-done.4.refs_5_
  29.0 0.2 collective-permute-done.5.refs_6_
  29.1 0.4 collective-permute-done.6.refs_7_
  29.5 0.7 pick.1
  30.2 0.4 collective-permute-start.8
  30.6 1.2 %collective-permute-start.7 = (bf16[128,256]{1,0:T(8,128)(2,1)S(1)}, bf16[128,256]{1,0:T(8,128)(2,1)S(1)}, u32[]{:S(2)}, u32[]{:S(2)}) collective-permute-start(bf16[128,256]{1,0:T(8,128)(2,1)S(1)} %pick.1), channel_id=1, source_target_pairs={{0,8},{1,9},{2,10},{3,11},{4,12},{5,13},{6,14},{7,15},{8,16},{9,17... | collective-permute-start | bytes 196616 | tf_op jit(solution)/shard_map/ppermute | solution.py:375
  31.8 5.9 %question_pass.1 = f32[8,72,128]{2,1,0:T(8,128)} custom-call(s32[64]{0:T(128)S(1)} %copy-done.6, bf16[8,32,256]{2,1,0:T(8,128)(2,1)S(1)} %all-to-all-done.refs_3_.got_ref, bf16[512,256]{1,0:T(8,128)(2,1)S(1)} %copy-done, bf16[512,256]{1,0:T(8,128)(2,1)S(1)} %get-tuple-element.10.refs_1_, bf16[512,256]{1,0:T(8,128)(2,1)S(1)} %get-tuple-element.11.refs_2_, ...), custom_call_target="tpu_custom_call" | custom-call | flops 900000000 | bytes 2500000 | tf_op jit(solution)/shard_map/question_pass/pallas_call | solution.py:221
  37.6 3.4 %all-to-all-start.1 = ((f32[8,72,128]{2,1,0:T(8,128)}), f32[8,72,128]{2,1,0:T(8,128)S(1)}, u32[]{:S(2)}, u32[]{:S(2)}) async-start(f32[8,72,128]{2,1,0:T(8,128)} %question_pass.1), calls=%async_computation.1 | async-start | bytes 589824 | tf_op jit(solution)/shard_map/all_to_all | solution.py:387
  41.1 0.0 collective-permute-done.8
  41.1 0.0 collective-permute-done.7
  41.1 4.5 %collective-permute-start.10 = (bf16[128,256]{1,0:T(8,128)(2,1)S(1)}, bf16[128,256]{1,0:T(8,128)(2,1)S(1)}, u32[]{:S(2)}, u32[]{:S(2)}) collective-permute-start(bf16[128,256]{1,0:T(8,128)(2,1)S(1)} %select_select_fusion.1), channel_id=1, source_target_pairs={{0,40},{1,41},{2,42},{3,43},{4,44},{5,45},{6,46},{7,47},{8,48},{9,... | collective-permute-start | bytes 196616 | tf_op jit(solution)/shard_map/ppermute | solution.py:375
  45.6 0.0 collective-permute-start.9
  46.2 0.0 copy-start.5
  46.3 3.4 %collective-permute-done.10 = bf16[128,256]{1,0:T(8,128)(2,1)S(1)} collective-permute-done((bf16[128,256]{1,0:T(8,128)(2,1)S(1)}, bf16[128,256]{1,0:T(8,128)(2,1)S(1)}, u32[]{:S(2)}, u32[]{:S(2)}) %collective-permute-start.10) | collective-permute-done | bytes 65568 | tf_op jit(solution)/shard_map/ppermute | solution.py:375
  49.6 3.0 %collective-permute-done.9 = bf16[128,256]{1,0:T(8,128)(2,1)S(1)} collective-permute-done((bf16[128,256]{1,0:T(8,128)(2,1)S(1)}, bf16[128,256]{1,0:T(8,128)(2,1)S(1)}, u32[]{:S(2)}, u32[]{:S(2)}) %collective-permute-start.9) | collective-permute-done | bytes 65568 | tf_op jit(solution)/shard_map/ppermute | solution.py:375
  52.7 0.0 all-to-all-done.1.parts_ref
  52.7 1.5 %combine.1 = bf16[32,64,128]{2,1,0:T(8,128)(2,1)} custom-call(s32[1]{0:T(128)S(6)} %copy.19.limit_ref, f32[8,72,128]{2,1,0:T(8,128)S(1)} %all-to-all-done.1.parts_ref, bf16[128,256]{1,0:T(8,128)(2,1)S(1)} %select_select_fusion.refs_0_.piece_ref), custom_call_target="tpu_custom_call" | custom-call | tf_op jit(solution)/shard_map/combine/pallas_call | solution.py:262
  54.1 8.8 %all-to-all-start.2 = ((bf16[32,64,128]{2,1,0:T(8,128)(2,1)}), bf16[32,64,128]{2,1,0:T(8,128)(2,1)S(1)}, u32[]{:S(2)}, u32[]{:S(2)}) async-start(bf16[32,64,128]{2,1,0:T(8,128)(2,1)} %combine.1), calls=%async_computation.2 | async-start | bytes 1048576 | tf_op jit(solution)/shard_map/all_to_all | solution.py:394
  62.9 2.5 %collective-permute-start.13 = (bf16[128,256]{1,0:T(8,128)(2,1)S(1)}, bf16[128,256]{1,0:T(8,128)(2,1)S(1)}, u32[]{:S(2)}, u32[]{:S(2)}) collective-permute-start(bf16[128,256]{1,0:T(8,128)(2,1)S(1)} %select_select_fusion.refs_0_.piece_ref), channel_id=1, source_target_pairs={{0,6},{1,7},{2,0},{3,1},{4,2},{5,3},{6,4},{7,5},{8,14},{9,15},{10,... | collective-permute-start | bytes 196616 | tf_op jit(solution)/shard_map/ppermute | solution.py:372
  65.5 0.6 collective-permute-start.12
  66.0 0.6 collective-permute-start.11
  66.6 1.1 %collective-permute-done.13.refs_3_ = bf16[128,256]{1,0:T(8,128)(2,1)S(1)} collective-permute-done((bf16[128,256]{1,0:T(8,128)(2,1)S(1)}, bf16[128,256]{1,0:T(8,128)(2,1)S(1)}, u32[]{:S(2)}, u32[]{:S(2)}) %collective-permute-start.13) | collective-permute-done | bytes 65568 | tf_op jit(solution)/shard_map/ppermute | solution.py:372
  67.7 3.4 %collective-permute-done.12.refs_2_ = bf16[128,256]{1,0:T(8,128)(2,1)S(1)} collective-permute-done((bf16[128,256]{1,0:T(8,128)(2,1)S(1)}, bf16[128,256]{1,0:T(8,128)(2,1)S(1)}, u32[]{:S(2)}, u32[]{:S(2)}) %collective-permute-start.12) | collective-permute-done | bytes 65568 | tf_op jit(solution)/shard_map/ppermute | solution.py:372
  71.1 0.9 %collective-permute-done.11.refs_1_ = bf16[128,256]{1,0:T(8,128)(2,1)S(1)} collective-permute-done((bf16[128,256]{1,0:T(8,128)(2,1)S(1)}, bf16[128,256]{1,0:T(8,128)(2,1)S(1)}, u32[]{:S(2)}, u32[]{:S(2)}) %collective-permute-start.11) | collective-permute-done | bytes 65568 | tf_op jit(solution)/shard_map/ppermute | solution.py:372
  72.0 6.8 %encode.1 = (bf16[256,2048]{1,0:T(8,128)(2,1)}, bf16[256,256]{1,0:T(8,128)(2,1)}, bf16[256,256]{1,0:T(8,128)(2,1)}) custom-call(s32[64]{0:T(128)S(1)} %copy-done.4, s32[64]{0:T(128)S(1)} %copy-done.6, bf16[256,2048]{1,0:T(8,128)(2,1)S(1)} %copy-done.5, bf16[256,256]{1,0:T(8,128)(2,1)S(1)} %copy-done.2, bf16[256,256]{1,0:T(8,128)(2,1)S(1)} %copy-done.3, ...), custom_call_target="tpu_custom_call" | custom-call | flops 1100000000 | bytes 3500000 | tf_op jit(solution)/shard_map/encode/pallas_call | solution.py:310
  78.8 0.0 all-to-all-done.2.refs_0_
  78.8 0.9 %copy-done.1 = bf16[256,256]{1,0:T(8,128)(2,1)S(1)} copy-done((bf16[256,256]{1,0:T(8,128)(2,1)S(1)}, bf16[256,256]{1,0:T(8,128)(2,1)}, u32[]{:S(2)}) %copy-start.1) | copy-done | bytes 131096
  79.7 2.9 %collective-permute-start.14 = (bf16[32,64,128]{2,1,0:T(8,128)(2,1)S(1)}, bf16[32,64,128]{2,1,0:T(8,128)(2,1)S(1)}, u32[]{:S(2)}, u32[]{:S(2)}) collective-permute-start(bf16[32,64,128]{2,1,0:T(8,128)(2,1)S(1)} %gate.3.own_ref), channel_id=1, source_target_pairs={{0,1},{1,0},{2,3},{3,2},{4,5},{5,4},{6,7},{7,6},{8,9},{9,8},{10,11... | collective-permute-start | bytes 1572872 | tf_op jit(solution)/shard_map/ppermute | solution.py:369
  82.6 1.5 %collective-permute-done.14.other_ref = bf16[32,64,128]{2,1,0:T(8,128)(2,1)S(1)} collective-permute-done((bf16[32,64,128]{2,1,0:T(8,128)(2,1)S(1)}, bf16[32,64,128]{2,1,0:T(8,128)(2,1)S(1)}, u32[]{:S(2)}, u32[]{:S(2)}) %collective-permute-start.14) | collective-permute-done | bytes 524320 | tf_op jit(solution)/shard_map/ppermute | solution.py:369
  84.1 1.8 %assemble.1 = bf16[256,2048]{1,0:T(8,128)(2,1)} custom-call(bf16[32,64,128]{2,1,0:T(8,128)(2,1)S(1)} %gate.3.own_ref, bf16[32,64,128]{2,1,0:T(8,128)(2,1)S(1)} %collective-permute-done.14.other_ref), custom_call_target="tpu_custom_call" | custom-call | tf_op jit(solution)/shard_map/assemble/pallas_call | solution.py:354
  (13 shorter events, 0.0 us)
Async XLA Ops:
  2.3 14.3 %copy-start = (bf16[512,256]{1,0:T(8,128)(2,1)S(1)}, bf16[512,256]{1,0:T(8,128)(2,1)}, u32[]{:S(2)}) copy-start(bf16[512,256]{1,0:T(8,128)(2,1)} %join.1.refs_0_) | copy-start | bytes 786436
  2.3 22.2 %collective-permute-start.2 = (bf16[512,256]{1,0:T(8,128)(2,1)}, bf16[512,256]{1,0:T(8,128)(2,1)S(1)}, u32[]{:S(2)}, u32[]{:S(2)}) collective-permute-start(bf16[512,256]{1,0:T(8,128)(2,1)} %join.1.refs_0_), channel_id=1, source_target_pairs={{0,6},{1,7},{2,0},{3,1},{4,2},{5,3},{6,4},{7,5},{8,14},{9,15},{10,... | collective-permute-start | bytes 786440 | tf_op jit(solution)/shard_map/ppermute | solution.py:372
  6.0 18.6 %collective-permute-start.1 = (bf16[512,256]{1,0:T(8,128)(2,1)}, bf16[512,256]{1,0:T(8,128)(2,1)S(1)}, u32[]{:S(2)}, u32[]{:S(2)}) collective-permute-start(bf16[512,256]{1,0:T(8,128)(2,1)} %join.1.refs_0_), channel_id=1, source_target_pairs={{0,4},{1,5},{2,6},{3,7},{4,0},{5,1},{6,2},{7,3},{8,12},{9,13},{10,... | collective-permute-start | bytes 786440 | tf_op jit(solution)/shard_map/ppermute | solution.py:372
  6.3 18.2 %collective-permute-start = (bf16[512,256]{1,0:T(8,128)(2,1)}, bf16[512,256]{1,0:T(8,128)(2,1)S(1)}, u32[]{:S(2)}, u32[]{:S(2)}) collective-permute-start(bf16[512,256]{1,0:T(8,128)(2,1)} %join.1.refs_0_), channel_id=1, source_target_pairs={{0,2},{1,3},{2,4},{3,5},{4,6},{5,7},{6,0},{7,1},{8,10},{9,11},{10,... | collective-permute-start | bytes 786440 | tf_op jit(solution)/shard_map/ppermute | solution.py:372
  8.4 16.1 %all-to-all-start = ((bf16[8,32,256]{2,1,0:T(8,128)(2,1)}), bf16[8,32,256]{2,1,0:T(8,128)(2,1)S(1)}, u32[]{:S(2)}, u32[]{:S(2)}) async-start(bf16[8,32,256]{2,1,0:T(8,128)(2,1)} %repeat.1), calls=%async_computation | async-start | bytes 262144 | tf_op jit(solution)/shard_map/all_to_all | solution.py:382
  16.6 12.3 %collective-permute-start.3 = (bf16[512,256]{1,0:T(8,128)(2,1)S(1)}, bf16[512,256]{1,0:T(8,128)(2,1)S(1)}, u32[]{:S(2)}, u32[]{:S(2)}) collective-permute-start(bf16[512,256]{1,0:T(8,128)(2,1)S(1)} %copy-done), channel_id=1, source_target_pairs={{0,1},{1,0},{2,3},{3,2},{4,5},{5,4},{6,7},{7,6},{8,9},{9,8},{10,11... | collective-permute-start | bytes 786440 | tf_op jit(solution)/shard_map/ppermute | solution.py:369
  24.6 4.4 %collective-permute-start.4 = (bf16[512,256]{1,0:T(8,128)(2,1)S(1)}, bf16[512,256]{1,0:T(8,128)(2,1)S(1)}, u32[]{:S(2)}, u32[]{:S(2)}) collective-permute-start(bf16[512,256]{1,0:T(8,128)(2,1)S(1)} %get-tuple-element.10.refs_1_), channel_id=1, source_target_pairs={{0,1},{1,0},{2,3},{3,2},{4,5},{5,4},{6,7},{7,6},{8,9},{9,8},{10,11... | collective-permute-start | bytes 786440 | tf_op jit(solution)/shard_map/ppermute | solution.py:369
  27.6 1.5 %collective-permute-start.5 = (bf16[512,256]{1,0:T(8,128)(2,1)S(1)}, bf16[512,256]{1,0:T(8,128)(2,1)S(1)}, u32[]{:S(2)}, u32[]{:S(2)}) collective-permute-start(bf16[512,256]{1,0:T(8,128)(2,1)S(1)} %get-tuple-element.11.refs_2_), channel_id=1, source_target_pairs={{0,1},{1,0},{2,3},{3,2},{4,5},{5,4},{6,7},{7,6},{8,9},{9,8},{10,11... | collective-permute-start | bytes 786440 | tf_op jit(solution)/shard_map/ppermute | solution.py:369
  27.7 1.8 %collective-permute-start.6 = (bf16[512,256]{1,0:T(8,128)(2,1)S(1)}, bf16[512,256]{1,0:T(8,128)(2,1)S(1)}, u32[]{:S(2)}, u32[]{:S(2)}) collective-permute-start(bf16[512,256]{1,0:T(8,128)(2,1)S(1)} %get-tuple-element.12.refs_3_), channel_id=1, source_target_pairs={{0,1},{1,0},{2,3},{3,2},{4,5},{5,4},{6,7},{7,6},{8,9},{9,8},{10,11... | collective-permute-start | bytes 786440 | tf_op jit(solution)/shard_map/ppermute | solution.py:369
  28.1 0.7 copy-start.4
  28.9 2.8 %copy-start.6 = (s32[64]{0:T(128)S(1)}, s32[64]{0:T(128)}, u32[]{:S(2)}) copy-start(s32[64]{0:T(128)} %lengths_ref.3) | copy-start | bytes 772
  30.2 10.9 %collective-permute-start.8 = (bf16[128,256]{1,0:T(8,128)(2,1)S(1)}, bf16[128,256]{1,0:T(8,128)(2,1)S(1)}, u32[]{:S(2)}, u32[]{:S(2)}) collective-permute-start(bf16[128,256]{1,0:T(8,128)(2,1)S(1)} %pick.1), channel_id=1, source_target_pairs={{0,56},{1,57},{2,58},{3,59},{4,60},{5,61},{6,62},{7,63},{8,0},{9,1... | collective-permute-start | bytes 196616 | tf_op jit(solution)/shard_map/ppermute | solution.py:375
  30.6 10.5 %collective-permute-start.7 = (bf16[128,256]{1,0:T(8,128)(2,1)S(1)}, bf16[128,256]{1,0:T(8,128)(2,1)S(1)}, u32[]{:S(2)}, u32[]{:S(2)}) collective-permute-start(bf16[128,256]{1,0:T(8,128)(2,1)S(1)} %pick.1), channel_id=1, source_target_pairs={{0,8},{1,9},{2,10},{3,11},{4,12},{5,13},{6,14},{7,15},{8,16},{9,17... | collective-permute-start | bytes 196616 | tf_op jit(solution)/shard_map/ppermute | solution.py:375
  37.6 15.0 %all-to-all-start.1 = ((f32[8,72,128]{2,1,0:T(8,128)}), f32[8,72,128]{2,1,0:T(8,128)S(1)}, u32[]{:S(2)}, u32[]{:S(2)}) async-start(f32[8,72,128]{2,1,0:T(8,128)} %question_pass.1), calls=%async_computation.1 | async-start | bytes 589824 | tf_op jit(solution)/shard_map/all_to_all | solution.py:387
  41.1 8.5 %collective-permute-start.10 = (bf16[128,256]{1,0:T(8,128)(2,1)S(1)}, bf16[128,256]{1,0:T(8,128)(2,1)S(1)}, u32[]{:S(2)}, u32[]{:S(2)}) collective-permute-start(bf16[128,256]{1,0:T(8,128)(2,1)S(1)} %select_select_fusion.1), channel_id=1, source_target_pairs={{0,40},{1,41},{2,42},{3,43},{4,44},{5,45},{6,46},{7,47},{8,48},{9,... | collective-permute-start | bytes 196616 | tf_op jit(solution)/shard_map/ppermute | solution.py:375
  45.6 7.1 %collective-permute-start.9 = (bf16[128,256]{1,0:T(8,128)(2,1)S(1)}, bf16[128,256]{1,0:T(8,128)(2,1)S(1)}, u32[]{:S(2)}, u32[]{:S(2)}) collective-permute-start(bf16[128,256]{1,0:T(8,128)(2,1)S(1)} %select_select_fusion.1), channel_id=1, source_target_pairs={{0,24},{1,25},{2,26},{3,27},{4,28},{5,29},{6,30},{7,31},{8,32},{9,... | collective-permute-start | bytes 196616 | tf_op jit(solution)/shard_map/ppermute | solution.py:375
  46.2 25.7 %copy-start.5 = (bf16[256,2048]{1,0:T(8,128)(2,1)S(1)}, bf16[256,2048]{1,0:T(8,128)(2,1)}, u32[]{:S(2)}) copy-start(bf16[256,2048]{1,0:T(8,128)(2,1)} %q_ref.1) | copy-start | bytes 3145732
  54.1 17.8 %copy-start.2 = (bf16[256,256]{1,0:T(8,128)(2,1)S(1)}, bf16[256,256]{1,0:T(8,128)(2,1)}, u32[]{:S(2)}) copy-start(bf16[256,256]{1,0:T(8,128)(2,1)} %k_ref.3) | copy-start | bytes 393220
  54.1 17.8 %copy-start.3 = (bf16[256,256]{1,0:T(8,128)(2,1)S(1)}, bf16[256,256]{1,0:T(8,128)(2,1)}, u32[]{:S(2)}) copy-start(bf16[256,256]{1,0:T(8,128)(2,1)} %v_ref.3) | copy-start | bytes 393220
  54.1 24.6 %all-to-all-start.2 = ((bf16[32,64,128]{2,1,0:T(8,128)(2,1)}), bf16[32,64,128]{2,1,0:T(8,128)(2,1)S(1)}, u32[]{:S(2)}, u32[]{:S(2)}) async-start(bf16[32,64,128]{2,1,0:T(8,128)(2,1)} %combine.1), calls=%async_computation.2 | async-start | bytes 1048576 | tf_op jit(solution)/shard_map/all_to_all | solution.py:394
  62.9 4.8 %collective-permute-start.13 = (bf16[128,256]{1,0:T(8,128)(2,1)S(1)}, bf16[128,256]{1,0:T(8,128)(2,1)S(1)}, u32[]{:S(2)}, u32[]{:S(2)}) collective-permute-start(bf16[128,256]{1,0:T(8,128)(2,1)S(1)} %select_select_fusion.refs_0_.piece_ref), channel_id=1, source_target_pairs={{0,6},{1,7},{2,0},{3,1},{4,2},{5,3},{6,4},{7,5},{8,14},{9,15},{10,... | collective-permute-start | bytes 196616 | tf_op jit(solution)/shard_map/ppermute | solution.py:372
  65.5 5.6 %collective-permute-start.12 = (bf16[128,256]{1,0:T(8,128)(2,1)S(1)}, bf16[128,256]{1,0:T(8,128)(2,1)S(1)}, u32[]{:S(2)}, u32[]{:S(2)}) collective-permute-start(bf16[128,256]{1,0:T(8,128)(2,1)S(1)} %select_select_fusion.refs_0_.piece_ref), channel_id=1, source_target_pairs={{0,4},{1,5},{2,6},{3,7},{4,0},{5,1},{6,2},{7,3},{8,12},{9,13},{10,... | collective-permute-start | bytes 196616 | tf_op jit(solution)/shard_map/ppermute | solution.py:372
  66.0 5.9 %collective-permute-start.11 = (bf16[128,256]{1,0:T(8,128)(2,1)S(1)}, bf16[128,256]{1,0:T(8,128)(2,1)S(1)}, u32[]{:S(2)}, u32[]{:S(2)}) collective-permute-start(bf16[128,256]{1,0:T(8,128)(2,1)S(1)} %select_select_fusion.refs_0_.piece_ref), channel_id=1, source_target_pairs={{0,2},{1,3},{2,4},{3,5},{4,6},{5,7},{6,0},{7,1},{8,10},{9,11},{10,... | collective-permute-start | bytes 196616 | tf_op jit(solution)/shard_map/ppermute | solution.py:372
  78.8 0.9 %copy-start.1 = (bf16[256,256]{1,0:T(8,128)(2,1)S(1)}, bf16[256,256]{1,0:T(8,128)(2,1)}, u32[]{:S(2)}) copy-start(bf16[256,256]{1,0:T(8,128)(2,1)} %get-tuple-element.7.refs_1_) | copy-start | bytes 393220
  79.7 4.4 %collective-permute-start.14 = (bf16[32,64,128]{2,1,0:T(8,128)(2,1)S(1)}, bf16[32,64,128]{2,1,0:T(8,128)(2,1)S(1)}, u32[]{:S(2)}, u32[]{:S(2)}) collective-permute-start(bf16[32,64,128]{2,1,0:T(8,128)(2,1)S(1)} %gate.3.own_ref), channel_id=1, source_target_pairs={{0,1},{1,0},{2,3},{3,2},{4,5},{5,4},{6,7},{7,6},{8,9},{9,8},{10,11... | collective-permute-start | bytes 1572872 | tf_op jit(solution)/shard_map/ppermute | solution.py:369

commit v3 on v2

v3 whole, which is shorter than its diff:
```python
import functools
import math

import jax
import jax.numpy as jnp
from jax import lax
from jax.experimental import pallas as pl
from jax.experimental.pallas import tpu as pltpu
from jax.sharding import PartitionSpec as P

HD = 128
SC = HD ** (-0.5)
SC2 = SC * math.log2(math.e)
NZ, NY, NC = 8, 4, 2
BLK = 256
BF = jnp.bfloat16
F32 = jnp.float32
SMEM = pl.BlockSpec(memory_space=pltpu.SMEM)
VMEM = pl.BlockSpec(memory_space=pltpu.VMEM)
SMALL = pltpu.CompilerParams(vmem_limit_bytes=4 * 1024 * 1024)
PARAMS = pltpu.CompilerParams(vmem_limit_bytes=20 * 1024 * 1024)


def index_of(z, y, c):
    return (z * NY + y) * NC + c


def permutation(move):
    return [
        (index_of(z, y, c), index_of(*move(z, y, c)))
        for z in range(NZ)
        for y in range(NY)
        for c in range(NC)
    ]


Z_GROUPS = [[index_of(z, y, c) for z in range(NZ)] for y in range(NY) for c in range(NC)]
CHIP_GROUPS = [[index_of(z, y, c) for z in range(NZ) for y in range(NY)] for c in range(NC)]
OTHER_CORE = permutation(lambda z, y, c: (z, y, 1 - c))
Y_SHIFTS = [permutation(lambda z, y, c, d=d: (z, (y + d) % NY, c)) for d in range(NY)]
Z_SHIFTS = [permutation(lambda z, y, c, d=d: ((z + d) % NZ, y, c)) for d in range(NZ)]


def coordinates():
    place = lax.axis_index("ctx")
    return place // (NY * NC), (place // NC) % NY, place % NC


def sign_table():
    shape = (HD, HD)
    both = lax.broadcasted_iota(jnp.int32, shape, 0) & lax.broadcasted_iota(jnp.int32, shape, 1)
    both = both ^ (both >> 4)
    both = both ^ (both >> 2)
    both = both ^ (both >> 1)
    return (1 - 2 * (both & 1)).astype(F32).astype(BF)


def across(a, b):
    return lax.dot_general(a, b, (((1,), (1,)), ((), ())), preferred_element_type=F32)


def dot(a, b):
    return jnp.dot(a, b, preferred_element_type=F32)


def rotated(rows, table):
    return (dot(rows, table) * SC).astype(BF)


def join_kernel(k_ref, v_ref, k_other_ref, v_other_ref, both_ref):
    c = coordinates()[2]
    for head in range(NC):

        @pl.when(c == head)
        def _(head=head):
            lanes = slice(HD * head, HD * head + HD)
            for i, source in enumerate((k_ref, v_ref, k_other_ref, v_other_ref)):
                both_ref[BLK * i : BLK * i + BLK, :] = source[:, lanes]


def join(k, v, k_other, v_other):
    return pl.pallas_call(
        join_kernel,
        out_shape=jax.ShapeDtypeStruct((4 * BLK, HD), BF),
        in_specs=[VMEM] * 4,
        out_specs=VMEM,
        compiler_params=SMALL,
        name="join",
    )(k, v, k_other, v_other)


def repeat_kernel(own_ref, other_ref, send_ref, rows_ref):
    c = coordinates()[2]
    own, other = own_ref[...].astype(F32), other_ref[...].astype(F32)
    first, second = jnp.where(c == 0, own, other), jnp.where(c == 0, other, own)
    for at, source in enumerate((first, second)):
        for j in range(8):
            left, right = source[:, HD * j : HD * j + HD], source[:, HD * (8 + j) : HD * (9 + j)]
            rows_ref[8 * j + 4 * at : 8 * j + 4 * at + 4, :] = jnp.where(c == 0, left, right)
    rows = rows_ref[...].astype(BF)
    for i in range(NZ):
        send_ref[i] = rows


def repeat(own, other):
    return pl.pallas_call(
        repeat_kernel,
        out_shape=jax.ShapeDtypeStruct((NZ, 64, HD), BF),
        in_specs=[VMEM] * 2,
        out_specs=VMEM,
        scratch_shapes=[pltpu.VMEM((64, HD), F32)],
        compiler_params=SMALL,
        name="repeat",
    )(own, other)


def gate_kernel(*refs):
    pass


def gate(arrays, token):
    anywhere = pl.BlockSpec(memory_space=pl.ANY)
    return pl.pallas_call(
        gate_kernel,
        out_shape=[jax.ShapeDtypeStruct(x.shape, x.dtype) for x in arrays],
        in_specs=[anywhere] * (len(arrays) + 1),
        out_specs=[anywhere] * len(arrays),
        input_output_aliases={i: i for i in range(len(arrays))},
        compiler_params=pltpu.CompilerParams(vmem_limit_bytes=1024 * 1024),
        name="gate",
    )(*arrays, token)


def pick_kernel(anchor_ref, *refs):
    columns, out_ref, sems = refs[:NY], refs[NY], refs[NY + 1]
    z, y, c = coordinates()
    wanted = lax.rem(anchor_ref[0], NY * NC)
    rows = HD * lax.rem(y, 2)
    for which in range(8):
        core = c if which < NY else 1 - c
        place = NC * lax.rem(y + NY - which % NY, NY) + core

        @pl.when(place == wanted)
        def _(which=which):
            copies = []
            for i in range(2):
                first = pl.multiple_of(2 * BLK * (which // NY) + BLK * i + rows, HD)
                source = columns[which % NY].at[pl.ds(first, HD), :]
                target = out_ref.at[HD * i : HD * i + HD, :]
                copies.append(pltpu.make_async_copy(source, target, sems.at[i]))
            for copy in copies:
                copy.start()
            for copy in copies:
                copy.wait()


def pick(anchor_index, columns):
    anywhere = pl.BlockSpec(memory_space=pl.ANY)
    return pl.pallas_call(
        pick_kernel,
        out_shape=jax.ShapeDtypeStruct((BLK, HD), BF),
        in_specs=[SMEM] + [anywhere] * NY,
        out_specs=VMEM,
        scratch_shapes=[pltpu.SemaphoreType.DMA((2,))],
        compiler_params=pltpu.CompilerParams(vmem_limit_bytes=1024 * 1024),
        name="pick",
    )(anchor_index, *columns)


def thirds(x):
    high = x.astype(BF)
    rest = x - high.astype(F32)
    middle = rest.astype(BF)
    return high, middle, (rest - middle.astype(F32)).astype(BF)


def question_kernel(lengths_ref, got_ref, *refs):
    columns, send_ref = refs[:NY], refs[NY]
    z, y, c = coordinates()
    table = sign_table()
    lane = lax.broadcasted_iota(jnp.int32, (BLK, BLK), 1)
    ids = [index_of(z, lax.rem(y + NY - d, NY), c) for d in range(NY)]
    ids += [index_of(z, lax.rem(y + NY - d, NY), 1 - c) for d in range(NY)]
    q = rotated(got_ref[...].reshape(NZ * 64, HD), table)
    halves = [q[0:BLK], q[BLK : 2 * BLK]]
    tops, totals, sums = [None] * 2, [None] * 2, [None] * 2
    for which in range(8):
        column, first = columns[which % NY], 2 * BLK * (which // NY)
        k = rotated(column[first : first + BLK, :], table)
        v = rotated(column[first + BLK : first + 2 * BLK, :], table)
        ok = lane < lengths_ref[ids[which]]
        for i in range(2):
            part = jnp.where(ok, across(halves[i], k) * SC2, -jnp.inf)
            m = jnp.max(part, axis=1, keepdims=True)
            e = jnp.exp2(part - m)
            d = jnp.sum(e, axis=1, keepdims=True)
            n = dot(e.astype(BF), v)
            if which == 0:
                tops[i], totals[i], sums[i] = m, d, n
            else:
                new = jnp.maximum(tops[i], m)
                old_scale, scale = jnp.exp2(tops[i] - new), jnp.exp2(m - new)
                tops[i] = new
                totals[i] = totals[i] * old_scale + d * scale
                sums[i] = sums[i] * old_scale + n * scale
    lanes = lax.broadcasted_iota(jnp.int32, (HD, HD), 1)
    packed = jnp.zeros((HD, HD), F32)
    for i in range(4):
        rows = slice(HD * (i % 2), HD * (i % 2) + HD)
        packed = jnp.where(lanes == i, tops[i // 2][rows], packed)
        packed = jnp.where(lanes == 4 + i, totals[i // 2][rows], packed)
    tile = packed.T[0:8, :]
    for i in range(2):
        send_ref[4 * i : 4 * i + 4, 0:64, :] = sums[i].reshape(4, 64, HD)
    for i in range(NZ):
        send_ref[i, 64:72, :] = tile


def question_pass(lengths, got, columns):
    return pl.pallas_call(
        question_kernel,
        out_shape=jax.ShapeDtypeStruct((NZ, 72, HD), F32),
        in_specs=[SMEM] + [VMEM] * (1 + NY),
        out_specs=VMEM,
        compiler_params=PARAMS,
        cost_estimate=pl.CostEstimate(
            flops=900_000_000, bytes_accessed=2_500_000, transcendentals=1_100_000
        ),
        name="question_pass",
    )(lengths, got, *columns)


def combine_kernel(limit_ref, parts_ref, piece_ref, send_ref, columns_ref):
    z, y, c = coordinates()
    table = sign_table()
    tops = [parts_ref[s, pl.ds(64 + z // 2, 1), :] for s in range(NZ)]
    totals = [parts_ref[s, pl.ds(68 + z // 2, 1), :] for s in range(NZ)]
    square = jnp.concatenate(tops + totals + [jnp.zeros((HD - 16, HD), F32)], axis=0)
    columns_ref[...] = square.T
    columns = columns_ref[pl.ds(pl.multiple_of(z % 2 * 64, 64), 64), :]
    row = lax.broadcasted_iota(jnp.int32, (64, HD), 0)
    tops = [columns[:, s : s + 1] for s in range(NZ)]
    peak = functools.reduce(jnp.maximum, tops)
    total = jnp.zeros((64, 1), F32)
    summed = jnp.zeros((64, HD), F32)
    for s in range(NZ):
        scale = jnp.exp2(tops[s] - peak)
        total = total + scale * columns[:, NZ + s : NZ + s + 1]
        summed = summed + scale * parts_ref[s, 0:64, :]
    high, middle, low = thirds(summed / total)
    back = (dot(low, table) + dot(middle, table) + dot(high, table)) * SC
    position = (z * NY + y) * 8 + (row & 7)
    back = jnp.where(position < limit_ref[0], back, 0.0).astype(BF)
    for i in range(NZ * NY):
        send_ref[i] = back


def combine(limit, parts, piece):
    return pl.pallas_call(
        combine_kernel,
        out_shape=jax.ShapeDtypeStruct((NZ * NY, 64, HD), BF),
        in_specs=[SMEM, VMEM, pl.BlockSpec(memory_space=pl.ANY)],
        out_specs=VMEM,
        scratch_shapes=[pltpu.VMEM((HD, HD), F32)],
        compiler_params=SMALL,
        name="combine",
    )(limit, parts, piece)


def encode_kernel(anchor_ref, lengths_ref, q_ref, k_ref, v_ref, *refs):
    pieces = refs[:4]
    mixed_ref, krot_ref, vrot_ref, token_ref, far_k_ref, far_v_ref = refs[4:]
    z, y, c = coordinates()
    place = index_of(z, y, c)
    anchor = anchor_ref[0]
    k, v = k_ref[...], v_ref[...]
    table = sign_table()
    krot_ref[...] = rotated(k, table)
    vrot_ref[...] = rotated(v, table)
    token_ref[...] = jnp.zeros_like(token_ref)
    g = pl.program_id(0)
    for core in range(2):

        @pl.when((g == c) == (core == 0))
        def _(core=core):
            for i in range(2):
                at = pl.multiple_of(HD * lax.rem(y + i, 2), HD)
                far_k_ref[pl.ds(at, HD), :] = pieces[2 * core + i][0:HD, :]
                far_v_ref[pl.ds(at, HD), :] = pieces[2 * core + i][HD : 2 * HD, :]

    far_k, far_v = far_k_ref[...], far_v_ref[...]
    far_len = jnp.where(place == anchor, 0, lengths_ref[anchor])
    own_len = lengths_ref[place]
    query = lax.broadcasted_iota(jnp.int32, (BLK, BLK), 0)
    key = lax.broadcasted_iota(jnp.int32, (BLK, BLK), 1)
    far_ok = key < far_len
    own_ok = (key <= query) & (key < own_len)
    for j in range(8):
        q = q_ref[:, HD * j : HD * j + HD]
        s_far = jnp.where(far_ok, across(q, far_k) * SC2, -jnp.inf)
        s_own = jnp.where(own_ok, across(q, k) * SC2, -jnp.inf)
        top = jnp.max(jnp.maximum(s_far, s_own), axis=1, keepdims=True)
        e_far = jnp.exp2(s_far - top)
        e_own = jnp.exp2(s_own - top)
        total = jnp.sum(e_far + e_own, axis=1, keepdims=True)
        summed = dot(e_far.astype(BF), far_v) + dot(e_own.astype(BF), v)
        mixed_ref[:, HD * j : HD * j + HD] = (summed / total).astype(BF)


def encode(anchor_index, lengths, q, k, v, pieces):
    heads = pl.BlockSpec((BLK, 8 * HD), lambda g: (0, g))
    group = pl.BlockSpec((BLK, HD), lambda g: (0, g))
    token = pl.BlockSpec((8, HD), lambda g: (0, 0))
    return pl.pallas_call(
        encode_kernel,
        grid=(2,),
        out_shape=(
            jax.ShapeDtypeStruct(q.shape, BF),
            jax.ShapeDtypeStruct(k.shape, BF),
            jax.ShapeDtypeStruct(v.shape, BF),
            jax.ShapeDtypeStruct((8, HD), F32),
        ),
        in_specs=[SMEM, SMEM, heads, group, group] + [VMEM] * 4,
        out_specs=(heads, group, group, token),
        scratch_shapes=[pltpu.VMEM((BLK, HD), BF), pltpu.VMEM((BLK, HD), BF)],
        compiler_params=PARAMS,
        cost_estimate=pl.CostEstimate(
            flops=1_100_000_000, bytes_accessed=3_500_000, transcendentals=2_100_000
        ),
        name="encode",
    )(anchor_index, lengths, q, k, v, *pieces)


def assemble_kernel(own_ref, other_ref, out_ref):
    c = coordinates()[2]
    for pair in range(4):
        sources = []
        for i in (2 * pair, 2 * pair + 1):
            own, other = own_ref[i].astype(F32), other_ref[i].astype(F32)
            sources.append((jnp.where(c == 0, own, other), jnp.where(c == 0, other, own)))
        rows = slice(16 * pair, 16 * pair + 16)
        for g in range(2):
            for j in range(8):
                parts = [source[g][8 * j : 8 * j + 8] for source in sources]
                lanes = slice(HD * (8 * g + j), HD * (8 * g + j) + HD)
                out_ref[rows, lanes] = jnp.concatenate(parts, axis=0).astype(BF)


def assemble(own, other):
    part = pl.BlockSpec((8, 64, HD), lambda i: (i, 0, 0))
    return pl.pallas_call(
        assemble_kernel,
        grid=(4,),
        out_shape=jax.ShapeDtypeStruct((256, 2048), BF),
        in_specs=[part] * 2,
        out_specs=pl.BlockSpec((64, 2048), lambda i: (i, 0)),
        compiler_params=PARAMS,
        name="assemble",
    )(own, other)


def on_device(
    context_q, context_k, context_v, question, block_lengths, anchor_index, question_length
):
    def swap(x):
        return lax.ppermute(x, "ctx", OTHER_CORE)

    def along_y(x):
        return [x] + [lax.ppermute(x, "ctx", Y_SHIFTS[d]) for d in range(1, NY)]

    def along_z(x, d):
        return lax.ppermute(x, "ctx", Z_SHIFTS[d]), lax.ppermute(x, "ctx", Z_SHIFTS[NZ - d])

    def with_other_core(parts):
        return parts + [swap(x) for x in parts]

    columns = along_y(join(context_k, context_v, swap(context_k), swap(context_v)))
    spread_rows = repeat(question, swap(question))
    got = lax.all_to_all(spread_rows, "ctx", 0, 0, axis_index_groups=Z_GROUPS)
    columns = [columns[0], *gate(columns[1:], got)]
    piece = pick(anchor_index, columns)
    below, above = along_z(piece, 1)
    send = question_pass(block_lengths, got, columns)
    parts = lax.all_to_all(send, "ctx", 0, 0, axis_index_groups=Z_GROUPS)
    distance = (lax.axis_index("ctx") // (NY * NC) - anchor_index[0] // (NY * NC)) & (NZ - 1)
    piece = jnp.where(distance == 1, below, jnp.where(distance == NZ - 1, above, piece))
    below, above = along_z(piece, 3)
    near = (distance < 2) | (distance == NZ - 1)
    piece = jnp.where(near, piece, jnp.where(distance < 5, below, above))
    spread = combine(question_length, parts, piece)
    own = lax.all_to_all(spread, "ctx", 0, 0, axis_index_groups=CHIP_GROUPS)
    pieces = [piece, lax.ppermute(piece, "ctx", Y_SHIFTS[1])]
    mixed, key_cache, value_cache, token = encode(
        anchor_index,
        block_lengths,
        context_q,
        context_k,
        context_v,
        pieces + [swap(x) for x in pieces],
    )
    (own,) = gate([own], token)
    answer = assemble(own, swap(own))
    return mixed, key_cache, value_cache, answer


def solution(mesh):
    placed = (
        P("ctx", "heads"),
        P("ctx", "heads"),
        P("ctx", "heads"),
        P("ctx", "heads"),
        P(),
        P(),
        P(),
    )
    return jax.shard_map(
        on_device,
        mesh=mesh,
        in_specs=placed,
        out_specs=(P("ctx", "heads"), P("ctx", "heads"), P("ctx", "heads"), P(None, "heads")),
        check_vma=False,
    )
```

time: 86.4 us -> 81 us (0.937)
  Pallas kernels: 19.7 us -> 15.9 us
  starting transfers between devices: 43.1 us -> 41.5 us
  local copies, waits for them, and re-layouts: 1.58 us -> 2.48 us
  waiting for transfers between devices: 19.9 us -> 19 us
    ppermute x6 -> x3, starting transfers between devices: 8.35 us -> 2.12 us  [along_y(): return [x] + [lax.ppermute(x, 'ctx', Y_SHIFTS[d]) for d in range(1, NY)]]
    ppermute x5 -> x6, starting transfers between devices: 8.34 us -> 14 us  [swap(): return lax.ppermute(x, 'ctx', OTHER_CORE)]
    ppermute x6 -> x3, waiting for transfers between devices: 5.37 us -> 0.01 us  [along_y(): return [x] + [lax.ppermute(x, 'ctx', Y_SHIFTS[d]) for d in range(1, NY)]]
    all_to_all x1, starting transfers between devices: 8.79 us -> 5.87 us  [on_device(): own = lax.all_to_all(spread, 'ctx', 0, 0, axis_index_groups=CHIP_GROUPS)]
    ppermute x5 -> x6, waiting for transfers between devices: 2.08 us -> 4.73 us  [swap(): return lax.ppermute(x, 'ctx', OTHER_CORE)]
    ppermute x2, waiting for transfers between devices: 3.02 us -> 5.61 us  [along_z(): lax.ppermute(x, 'ctx', Z_SHIFTS[d])]
    pallas_call x3, Pallas kernels: 3.8 us -> 1.45 us  [the longest x1 0.72 us: pick(): pl.pallas_call(pick_kernel, out_shape=jax.ShapeDtypeStruct((BLK, HD), BF)...]
    ppermute x2, waiting for transfers between devices: 3.37 us -> 1.55 us  [along_z(): lax.ppermute(x, 'ctx', Z_SHIFTS[NZ - d])]
  transfers between devices with their start and end apart: 18 -> 17, of which waited for: 9 -> 8; matrix products, arithmetic and copies ran while one was open for 0% -> 0% of each run, Pallas kernels for 16% -> 15%
where the time goes in v3:
time: 81 us; the launch traced here: 80.5 us
  starting transfers between devices  41.5 us (51%)
  waiting for transfers between devices  19 us (23%)
  Pallas kernels  15.9 us (20%)
  local copies, waits for them, and re-layouts  2.48 us (3%)
  between operations  1.58 us (2%)
    ppermute x6, starting transfers between devices, swap(): return lax.ppermute(x, 'ctx', OTHER_CORE)  14 us
    all_to_all x1, starting transfers between devices, on_device(): got = lax.all_to_all(spread_rows, 'ctx', 0, 0, axis_index_groups=Z_GROUPS)  8.19 us
    all_to_all x1, waiting for transfers between devices, on_device(): got = lax.all_to_all(spread_rows, 'ctx', 0, 0, axis_index_groups=Z_GROUPS)  7.09 us
    pallas_call x1, Pallas kernels, encode(): pl.pallas_call(encode_kernel, grid=(2,), out_shape=(jax.ShapeDtypeStruct(...  7.04 us
    all_to_all x1, starting transfers between devices, on_device(): own = lax.all_to_all(spread, 'ctx', 0, 0, axis_index_groups=CHIP_GROUPS)  5.87 us
    ppermute x2, starting transfers between devices, along_z(): lax.ppermute(x, 'ctx', Z_SHIFTS[NZ - d])  5.8 us
    ppermute x2, waiting for transfers between devices, along_z(): lax.ppermute(x, 'ctx', Z_SHIFTS[d])  5.61 us
    ppermute x6, waiting for transfers between devices, swap(): return lax.ppermute(x, 'ctx', OTHER_CORE)  4.73 us
  transfers between devices with their start and end apart: 17, of which 8 were waited for; matrix products, arithmetic and copies ran while one was open for 0% of the time, Pallas kernels for 15%

profile of v3, /device:TPU:1, one launch (start us, length us, event | category | flops | bytes accessed | tf_op | source)
XLA Modules:
  0.0 80.5 jit_solution(5775308992967879279)
XLA Ops:
  0.6 3.3 %collective-permute-start = (bf16[256,256]{1,0:T(8,128)(2,1)}, bf16[256,256]{1,0:T(8,128)(2,1)S(1)}, u32[]{:S(2)}, u32[]{:S(2)}) collective-permute-start(bf16[256,256]{1,0:T(8,128)(2,1)} %k_ref.3), channel_id=1, source_target_pairs={{0,1},{1,0},{2,3},{3,2},{4,5},{5,4},{6,7},{7,6},{8,9},{9,8},{10,11... | collective-permute-start | bytes 393224 | tf_op jit(solution)/shard_map/ppermute | solution.py:366
  4.0 0.1 collective-permute-start.1
  4.1 1.1 %collective-permute-done.k_other_ref = bf16[256,256]{1,0:T(8,128)(2,1)S(1)} collective-permute-done((bf16[256,256]{1,0:T(8,128)(2,1)}, bf16[256,256]{1,0:T(8,128)(2,1)S(1)}, u32[]{:S(2)}, u32[]{:S(2)}) %collective-permute-start) | collective-permute-done | bytes 131104 | tf_op jit(solution)/shard_map/ppermute | solution.py:366
  5.2 0.4 collective-permute-done.1.v_other_ref
  5.5 0.9 %copy-done = bf16[256,256]{1,0:T(8,128)(2,1)S(1)} copy-done((bf16[256,256]{1,0:T(8,128)(2,1)S(1)}, bf16[256,256]{1,0:T(8,128)(2,1)}, u32[]{:S(2)}) %copy-start) | copy-done | bytes 131096
  6.4 0.9 %copy-done.2 = bf16[256,256]{1,0:T(8,128)(2,1)S(1)} copy-done((bf16[256,256]{1,0:T(8,128)(2,1)S(1)}, bf16[256,256]{1,0:T(8,128)(2,1)}, u32[]{:S(2)}) %copy-start.2) | copy-done | bytes 131096
  7.4 1.1 %collective-permute-start.4 = (bf16[1024,128]{1,0:T(8,128)(2,1)S(1)}, bf16[1024,128]{1,0:T(8,128)(2,1)S(1)}, u32[]{:S(2)}, u32[]{:S(2)}) collective-permute-start(bf16[1024,128]{1,0:T(8,128)(2,1)S(1)} %join.1.refs_0_), channel_id=1, source_target_pairs={{0,6},{1,7},{2,0},{3,1},{4,2},{5,3},{6,4},{7,5},{8,14},{9,15},{10,... | collective-permute-start | bytes 786440 | tf_op jit(solution)/shard_map/ppermute | solution.py:369
  8.5 0.3 collective-permute-start.3
  8.8 0.7 collective-permute-start.2
  9.5 0.0 copy-done.4
  9.5 1.0 %collective-permute-start.5 = (bf16[4,2048]{1,0:T(4,128)(2,1)S(1)}, bf16[4,2048]{1,0:T(4,128)(2,1)S(1)}, u32[]{:S(2)}, u32[]{:S(2)}) collective-permute-start(bf16[4,2048]{1,0:T(4,128)(2,1)S(1)} %copy-done.4), channel_id=1, source_target_pairs={{0,1},{1,0},{2,3},{3,2},{4,5},{5,4},{6,7},{7,6},{8,9},{9,8},{10,11... | collective-permute-start | bytes 49160 | tf_op jit(solution)/shard_map/ppermute | solution.py:366
  10.5 0.8 %collective-permute-done.5.other_ref = bf16[4,2048]{1,0:T(4,128)(2,1)S(1)} collective-permute-done((bf16[4,2048]{1,0:T(4,128)(2,1)S(1)}, bf16[4,2048]{1,0:T(4,128)(2,1)S(1)}, u32[]{:S(2)}, u32[]{:S(2)}) %collective-permute-start.5) | collective-permute-done | bytes 16416 | tf_op jit(solution)/shard_map/ppermute | solution.py:366
  11.4 0.7 repeat.1
  12.1 8.2 %all-to-all-start = ((bf16[8,64,128]{2,1,0:T(8,128)(2,1)}), bf16[8,64,128]{2,1,0:T(8,128)(2,1)S(1)}, u32[]{:S(2)}, u32[]{:S(2)}) async-start(bf16[8,64,128]{2,1,0:T(8,128)(2,1)} %repeat.1), calls=%async_computation | async-start | bytes 262144 | tf_op jit(solution)/shard_map/all_to_all | solution.py:379
  20.2 0.7 copy-done.5
  21.1 7.1 %all-to-all-done.refs_3_.got_ref = bf16[8,64,128]{2,1,0:T(8,128)(2,1)S(1)} async-done(((bf16[8,64,128]{2,1,0:T(8,128)(2,1)}), bf16[8,64,128]{2,1,0:T(8,128)(2,1)S(1)}, u32[]{:S(2)}, u32[]{:S(2)}) %all-to-all-start) | async-done | bytes 131104 | tf_op jit(solution)/shard_map/all_to_all | solution.py:379
  28.2 0.0 collective-permute-done.4.refs_2_
  28.2 0.0 collective-permute-done.3.refs_1_
  28.2 0.0 collective-permute-done.2.refs_0_
  28.2 0.0 copy-start.7
  28.2 0.7 pick.1
  28.9 1.3 %collective-permute-start.7 = (bf16[256,128]{1,0:T(8,128)(2,1)S(1)}, bf16[256,128]{1,0:T(8,128)(2,1)S(1)}, u32[]{:S(2)}, u32[]{:S(2)}) collective-permute-start(bf16[256,128]{1,0:T(8,128)(2,1)S(1)} %pick.1), channel_id=1, source_target_pairs={{0,56},{1,57},{2,58},{3,59},{4,60},{5,61},{6,62},{7,63},{8,0},{9,1... | collective-permute-start | bytes 196616 | tf_op jit(solution)/shard_map/ppermute | solution.py:372
  30.2 0.3 collective-permute-start.6
  30.5 0.0 copy-done.7
  30.5 4.3 %question_pass.1 = f32[8,72,128]{2,1,0:T(8,128)} custom-call(s32[64]{0:T(128)S(1)} %copy-done.7, bf16[8,64,128]{2,1,0:T(8,128)(2,1)S(1)} %all-to-all-done.refs_3_.got_ref, bf16[1024,128]{1,0:T(8,128)(2,1)S(1)} %join.1.refs_0_, bf16[1024,128]{1,0:T(8,128)(2,1)S(1)} %get-tuple-element.11.refs_1_, bf16[1024,128]{1,0:T(8,128)(2,1)S(1)} %get-tuple-element.12.refs_2_, ...), custom_call_target="tpu_custom_call" | custom-call | flops 900000000 | bytes 2500000 | tf_op jit(solution)/shard_map/question_pass/pallas_call | solution.py:220
  34.8 3.8 %all-to-all-start.1 = ((f32[8,72,128]{2,1,0:T(8,128)}), f32[8,72,128]{2,1,0:T(8,128)S(1)}, u32[]{:S(2)}, u32[]{:S(2)}) async-start(f32[8,72,128]{2,1,0:T(8,128)} %question_pass.1), calls=%async_computation.1 | async-start | bytes 589824 | tf_op jit(solution)/shard_map/all_to_all | solution.py:384
  38.6 0.0 collective-permute-done.7
  38.6 0.0 collective-permute-done.6
  38.6 4.5 %collective-permute-start.9 = (bf16[256,128]{1,0:T(8,128)(2,1)S(1)}, bf16[256,128]{1,0:T(8,128)(2,1)S(1)}, u32[]{:S(2)}, u32[]{:S(2)}) collective-permute-start(bf16[256,128]{1,0:T(8,128)(2,1)S(1)} %select_select_fusion.1), channel_id=1, source_target_pairs={{0,40},{1,41},{2,42},{3,43},{4,44},{5,45},{6,46},{7,47},{8,48},{9,... | collective-permute-start | bytes 196616 | tf_op jit(solution)/shard_map/ppermute | solution.py:372
  43.1 0.0 collective-permute-start.8
  43.8 0.0 copy-start.6
  43.8 1.5 %collective-permute-done.9 = bf16[256,128]{1,0:T(8,128)(2,1)S(1)} collective-permute-done((bf16[256,128]{1,0:T(8,128)(2,1)S(1)}, bf16[256,128]{1,0:T(8,128)(2,1)S(1)}, u32[]{:S(2)}, u32[]{:S(2)}) %collective-permute-start.9) | collective-permute-done | bytes 65568 | tf_op jit(solution)/shard_map/ppermute | solution.py:372
  45.4 5.6 %collective-permute-done.8 = bf16[256,128]{1,0:T(8,128)(2,1)S(1)} collective-permute-done((bf16[256,128]{1,0:T(8,128)(2,1)S(1)}, bf16[256,128]{1,0:T(8,128)(2,1)S(1)}, u32[]{:S(2)}, u32[]{:S(2)}) %collective-permute-start.8) | collective-permute-done | bytes 65568 | tf_op jit(solution)/shard_map/ppermute | solution.py:372
  51.0 0.0 all-to-all-done.1.parts_ref
  51.0 1.5 %combine.1 = bf16[32,64,128]{2,1,0:T(8,128)(2,1)} custom-call(s32[1]{0:T(128)S(6)} %copy.19.limit_ref, f32[8,72,128]{2,1,0:T(8,128)S(1)} %all-to-all-done.1.parts_ref, bf16[256,128]{1,0:T(8,128)(2,1)S(1)} %select_select_fusion.refs_0_.piece_ref), custom_call_target="tpu_custom_call" | custom-call | tf_op jit(solution)/shard_map/combine/pallas_call | solution.py:259
  52.5 5.9 %all-to-all-start.2 = ((bf16[32,64,128]{2,1,0:T(8,128)(2,1)}), bf16[32,64,128]{2,1,0:T(8,128)(2,1)S(1)}, u32[]{:S(2)}, u32[]{:S(2)}) async-start(bf16[32,64,128]{2,1,0:T(8,128)(2,1)} %combine.1), calls=%async_computation.2 | async-start | bytes 1048576 | tf_op jit(solution)/shard_map/all_to_all | solution.py:391
  58.4 1.5 %collective-permute-start.10 = (bf16[256,128]{1,0:T(8,128)(2,1)S(1)}, bf16[256,128]{1,0:T(8,128)(2,1)S(1)}, u32[]{:S(2)}, u32[]{:S(2)}) collective-permute-start(bf16[256,128]{1,0:T(8,128)(2,1)S(1)} %select_select_fusion.refs_0_.piece_ref), channel_id=1, source_target_pairs={{0,2},{1,3},{2,4},{3,5},{4,6},{5,7},{6,0},{7,1},{8,10},{9,11},{10,... | collective-permute-start | bytes 196616 | tf_op jit(solution)/shard_map/ppermute | solution.py:392
  59.9 3.7 %collective-permute-start.11 = (bf16[256,128]{1,0:T(8,128)(2,1)S(1)}, bf16[256,128]{1,0:T(8,128)(2,1)S(1)}, u32[]{:S(2)}, u32[]{:S(2)}) collective-permute-start(bf16[256,128]{1,0:T(8,128)(2,1)S(1)} %select_select_fusion.refs_0_.piece_ref), channel_id=1, source_target_pairs={{0,1},{1,0},{2,3},{3,2},{4,5},{5,4},{6,7},{7,6},{8,9},{9,8},{10,11... | collective-permute-start | bytes 196616 | tf_op jit(solution)/shard_map/ppermute | solution.py:366
  63.5 0.0 collective-permute-done.10.refs_1_
  63.5 4.5 %collective-permute-start.12 = (bf16[256,128]{1,0:T(8,128)(2,1)S(1)}, bf16[256,128]{1,0:T(8,128)(2,1)S(1)}, u32[]{:S(2)}, u32[]{:S(2)}) collective-permute-start(bf16[256,128]{1,0:T(8,128)(2,1)S(1)} %collective-permute-done.10.refs_1_), channel_id=1, source_target_pairs={{0,1},{1,0},{2,3},{3,2},{4,5},{5,4},{6,7},{7,6},{8,9},{9,8},{10,11... | collective-permute-start | bytes 196616 | tf_op jit(solution)/shard_map/ppermute | solution.py:366
  68.1 0.0 collective-permute-done.11.refs_2_
  68.1 0.9 %collective-permute-done.12.refs_3_ = bf16[256,128]{1,0:T(8,128)(2,1)S(1)} collective-permute-done((bf16[256,128]{1,0:T(8,128)(2,1)S(1)}, bf16[256,128]{1,0:T(8,128)(2,1)S(1)}, u32[]{:S(2)}, u32[]{:S(2)}) %collective-permute-start.12) | collective-permute-done | bytes 65568 | tf_op jit(solution)/shard_map/ppermute | solution.py:366
  69.0 0.0 copy-done.3
  69.0 7.0 %encode.1 = (bf16[256,2048]{1,0:T(8,128)(2,1)}, bf16[256,256]{1,0:T(8,128)(2,1)}, bf16[256,256]{1,0:T(8,128)(2,1)}, f32[8,128]{1,0:T(8,128)S(1)}) custom-call(s32[64]{0:T(128)S(1)} %copy-done.5, s32[64]{0:T(128)S(1)} %copy-done.7, bf16[256,2048]{1,0:T(8,128)(2,1)S(1)} %copy-done.6, bf16[256,256]{1,0:T(8,128)(2,1)S(1)} %copy-done.1, ...), custom_call_target="tpu_custom_call" | custom-call | flops 1100000000 | bytes 3500000 | tf_op jit(solution)/shard_map/encode/pallas_call | solution.py:314
  76.0 0.0 all-to-all-done.2.refs_0_
  76.0 1.4 %collective-permute-start.13 = (bf16[32,64,128]{2,1,0:T(8,128)(2,1)S(1)}, bf16[32,64,128]{2,1,0:T(8,128)(2,1)S(1)}, u32[]{:S(2)}, u32[]{:S(2)}) collective-permute-start(bf16[32,64,128]{2,1,0:T(8,128)(2,1)S(1)} %gate.3.own_ref), channel_id=1, source_target_pairs={{0,1},{1,0},{2,3},{3,2},{4,5},{5,4},{6,7},{7,6},{8,9},{9,8},{10,11... | collective-permute-start | bytes 1572872 | tf_op jit(solution)/shard_map/ppermute | solution.py:366
  77.4 1.5 %collective-permute-done.13.other_ref = bf16[32,64,128]{2,1,0:T(8,128)(2,1)S(1)} collective-permute-done((bf16[32,64,128]{2,1,0:T(8,128)(2,1)S(1)}, bf16[32,64,128]{2,1,0:T(8,128)(2,1)S(1)}, u32[]{:S(2)}, u32[]{:S(2)}) %collective-permute-start.13) | collective-permute-done | bytes 524320 | tf_op jit(solution)/shard_map/ppermute | solution.py:366
  78.9 1.6 %assemble.1 = bf16[256,2048]{1,0:T(8,128)(2,1)} custom-call(bf16[32,64,128]{2,1,0:T(8,128)(2,1)S(1)} %gate.3.own_ref, bf16[32,64,128]{2,1,0:T(8,128)(2,1)S(1)} %collective-permute-done.13.other_ref), custom_call_target="tpu_custom_call" | custom-call | tf_op jit(solution)/shard_map/assemble/pallas_call | solution.py:351
  (13 shorter events, 0.1 us)
Async XLA Ops:
  0.6 4.5 %collective-permute-start = (bf16[256,256]{1,0:T(8,128)(2,1)}, bf16[256,256]{1,0:T(8,128)(2,1)S(1)}, u32[]{:S(2)}, u32[]{:S(2)}) collective-permute-start(bf16[256,256]{1,0:T(8,128)(2,1)} %k_ref.3), channel_id=1, source_target_pairs={{0,1},{1,0},{2,3},{3,2},{4,5},{5,4},{6,7},{7,6},{8,9},{9,8},{10,11... | collective-permute-start | bytes 393224 | tf_op jit(solution)/shard_map/ppermute | solution.py:366
  4.0 1.6 %collective-permute-start.1 = (bf16[256,256]{1,0:T(8,128)(2,1)}, bf16[256,256]{1,0:T(8,128)(2,1)S(1)}, u32[]{:S(2)}, u32[]{:S(2)}) collective-permute-start(bf16[256,256]{1,0:T(8,128)(2,1)} %v_ref.3), channel_id=1, source_target_pairs={{0,1},{1,0},{2,3},{3,2},{4,5},{5,4},{6,7},{7,6},{8,9},{9,8},{10,11... | collective-permute-start | bytes 393224 | tf_op jit(solution)/shard_map/ppermute | solution.py:366
  5.5 0.9 %copy-start = (bf16[256,256]{1,0:T(8,128)(2,1)S(1)}, bf16[256,256]{1,0:T(8,128)(2,1)}, u32[]{:S(2)}) copy-start(bf16[256,256]{1,0:T(8,128)(2,1)} %k_ref.3) | copy-start | bytes 393220
  6.4 0.9 %copy-start.2 = (bf16[256,256]{1,0:T(8,128)(2,1)S(1)}, bf16[256,256]{1,0:T(8,128)(2,1)}, u32[]{:S(2)}) copy-start(bf16[256,256]{1,0:T(8,128)(2,1)} %v_ref.3) | copy-start | bytes 393220
  7.3 2.2 %copy-start.4 = (bf16[4,2048]{1,0:T(4,128)(2,1)S(1)}, bf16[4,2048]{1,0:T(4,128)(2,1)}, u32[]{:S(2)}) copy-start(bf16[4,2048]{1,0:T(4,128)(2,1)} %own_ref.1) | copy-start | bytes 49156
  7.4 20.8 %collective-permute-start.4 = (bf16[1024,128]{1,0:T(8,128)(2,1)S(1)}, bf16[1024,128]{1,0:T(8,128)(2,1)S(1)}, u32[]{:S(2)}, u32[]{:S(2)}) collective-permute-start(bf16[1024,128]{1,0:T(8,128)(2,1)S(1)} %join.1.refs_0_), channel_id=1, source_target_pairs={{0,6},{1,7},{2,0},{3,1},{4,2},{5,3},{6,4},{7,5},{8,14},{9,15},{10,... | collective-permute-start | bytes 786440 | tf_op jit(solution)/shard_map/ppermute | solution.py:369
  8.5 19.7 %collective-permute-start.3 = (bf16[1024,128]{1,0:T(8,128)(2,1)S(1)}, bf16[1024,128]{1,0:T(8,128)(2,1)S(1)}, u32[]{:S(2)}, u32[]{:S(2)}) collective-permute-start(bf16[1024,128]{1,0:T(8,128)(2,1)S(1)} %join.1.refs_0_), channel_id=1, source_target_pairs={{0,4},{1,5},{2,6},{3,7},{4,0},{5,1},{6,2},{7,3},{8,12},{9,13},{10,... | collective-permute-start | bytes 786440 | tf_op jit(solution)/shard_map/ppermute | solution.py:369
  8.8 19.4 %collective-permute-start.2 = (bf16[1024,128]{1,0:T(8,128)(2,1)S(1)}, bf16[1024,128]{1,0:T(8,128)(2,1)S(1)}, u32[]{:S(2)}, u32[]{:S(2)}) collective-permute-start(bf16[1024,128]{1,0:T(8,128)(2,1)S(1)} %join.1.refs_0_), channel_id=1, source_target_pairs={{0,2},{1,3},{2,4},{3,5},{4,6},{5,7},{6,0},{7,1},{8,10},{9,11},{10,... | collective-permute-start | bytes 786440 | tf_op jit(solution)/shard_map/ppermute | solution.py:369
  9.5 1.9 %collective-permute-start.5 = (bf16[4,2048]{1,0:T(4,128)(2,1)S(1)}, bf16[4,2048]{1,0:T(4,128)(2,1)S(1)}, u32[]{:S(2)}, u32[]{:S(2)}) collective-permute-start(bf16[4,2048]{1,0:T(4,128)(2,1)S(1)} %copy-done.4), channel_id=1, source_target_pairs={{0,1},{1,0},{2,3},{3,2},{4,5},{5,4},{6,7},{7,6},{8,9},{9,8},{10,11... | collective-permute-start | bytes 49160 | tf_op jit(solution)/shard_map/ppermute | solution.py:366
  12.1 16.1 %all-to-all-start = ((bf16[8,64,128]{2,1,0:T(8,128)(2,1)}), bf16[8,64,128]{2,1,0:T(8,128)(2,1)S(1)}, u32[]{:S(2)}, u32[]{:S(2)}) async-start(bf16[8,64,128]{2,1,0:T(8,128)(2,1)} %repeat.1), calls=%async_computation | async-start | bytes 262144 | tf_op jit(solution)/shard_map/all_to_all | solution.py:379
  20.2 0.7 copy-start.5
  28.2 2.3 %copy-start.7 = (s32[64]{0:T(128)S(1)}, s32[64]{0:T(128)}, u32[]{:S(2)}) copy-start(s32[64]{0:T(128)} %lengths_ref.3) | copy-start | bytes 772
  28.9 9.6 %collective-permute-start.7 = (bf16[256,128]{1,0:T(8,128)(2,1)S(1)}, bf16[256,128]{1,0:T(8,128)(2,1)S(1)}, u32[]{:S(2)}, u32[]{:S(2)}) collective-permute-start(bf16[256,128]{1,0:T(8,128)(2,1)S(1)} %pick.1), channel_id=1, source_target_pairs={{0,56},{1,57},{2,58},{3,59},{4,60},{5,61},{6,62},{7,63},{8,0},{9,1... | collective-permute-start | bytes 196616 | tf_op jit(solution)/shard_map/ppermute | solution.py:372
  30.2 8.4 %collective-permute-start.6 = (bf16[256,128]{1,0:T(8,128)(2,1)S(1)}, bf16[256,128]{1,0:T(8,128)(2,1)S(1)}, u32[]{:S(2)}, u32[]{:S(2)}) collective-permute-start(bf16[256,128]{1,0:T(8,128)(2,1)S(1)} %pick.1), channel_id=1, source_target_pairs={{0,8},{1,9},{2,10},{3,11},{4,12},{5,13},{6,14},{7,15},{8,16},{9,17... | collective-permute-start | bytes 196616 | tf_op jit(solution)/shard_map/ppermute | solution.py:372
  34.8 16.2 %all-to-all-start.1 = ((f32[8,72,128]{2,1,0:T(8,128)}), f32[8,72,128]{2,1,0:T(8,128)S(1)}, u32[]{:S(2)}, u32[]{:S(2)}) async-start(f32[8,72,128]{2,1,0:T(8,128)} %question_pass.1), calls=%async_computation.1 | async-start | bytes 589824 | tf_op jit(solution)/shard_map/all_to_all | solution.py:384
  38.6 6.8 %collective-permute-start.9 = (bf16[256,128]{1,0:T(8,128)(2,1)S(1)}, bf16[256,128]{1,0:T(8,128)(2,1)S(1)}, u32[]{:S(2)}, u32[]{:S(2)}) collective-permute-start(bf16[256,128]{1,0:T(8,128)(2,1)S(1)} %select_select_fusion.1), channel_id=1, source_target_pairs={{0,40},{1,41},{2,42},{3,43},{4,44},{5,45},{6,46},{7,47},{8,48},{9,... | collective-permute-start | bytes 196616 | tf_op jit(solution)/shard_map/ppermute | solution.py:372
  43.1 7.8 %collective-permute-start.8 = (bf16[256,128]{1,0:T(8,128)(2,1)S(1)}, bf16[256,128]{1,0:T(8,128)(2,1)S(1)}, u32[]{:S(2)}, u32[]{:S(2)}) collective-permute-start(bf16[256,128]{1,0:T(8,128)(2,1)S(1)} %select_select_fusion.1), channel_id=1, source_target_pairs={{0,24},{1,25},{2,26},{3,27},{4,28},{5,29},{6,30},{7,31},{8,32},{9,... | collective-permute-start | bytes 196616 | tf_op jit(solution)/shard_map/ppermute | solution.py:372
  43.8 25.2 %copy-start.6 = (bf16[256,2048]{1,0:T(8,128)(2,1)S(1)}, bf16[256,2048]{1,0:T(8,128)(2,1)}, u32[]{:S(2)}) copy-start(bf16[256,2048]{1,0:T(8,128)(2,1)} %q_ref.1) | copy-start | bytes 3145732
  52.5 16.5 %copy-start.1 = (bf16[256,256]{1,0:T(8,128)(2,1)S(1)}, bf16[256,256]{1,0:T(8,128)(2,1)}, u32[]{:S(2)}) copy-start(bf16[256,256]{1,0:T(8,128)(2,1)} %k_ref.3) | copy-start | bytes 393220
  52.5 16.5 %copy-start.3 = (bf16[256,256]{1,0:T(8,128)(2,1)S(1)}, bf16[256,256]{1,0:T(8,128)(2,1)}, u32[]{:S(2)}) copy-start(bf16[256,256]{1,0:T(8,128)(2,1)} %v_ref.3) | copy-start | bytes 393220
  52.5 23.5 %all-to-all-start.2 = ((bf16[32,64,128]{2,1,0:T(8,128)(2,1)}), bf16[32,64,128]{2,1,0:T(8,128)(2,1)S(1)}, u32[]{:S(2)}, u32[]{:S(2)}) async-start(bf16[32,64,128]{2,1,0:T(8,128)(2,1)} %combine.1), calls=%async_computation.2 | async-start | bytes 1048576 | tf_op jit(solution)/shard_map/all_to_all | solution.py:391
  58.4 5.2 %collective-permute-start.10 = (bf16[256,128]{1,0:T(8,128)(2,1)S(1)}, bf16[256,128]{1,0:T(8,128)(2,1)S(1)}, u32[]{:S(2)}, u32[]{:S(2)}) collective-permute-start(bf16[256,128]{1,0:T(8,128)(2,1)S(1)} %select_select_fusion.refs_0_.piece_ref), channel_id=1, source_target_pairs={{0,2},{1,3},{2,4},{3,5},{4,6},{5,7},{6,0},{7,1},{8,10},{9,11},{10,... | collective-permute-start | bytes 196616 | tf_op jit(solution)/shard_map/ppermute | solution.py:392
  59.9 8.2 %collective-permute-start.11 = (bf16[256,128]{1,0:T(8,128)(2,1)S(1)}, bf16[256,128]{1,0:T(8,128)(2,1)S(1)}, u32[]{:S(2)}, u32[]{:S(2)}) collective-permute-start(bf16[256,128]{1,0:T(8,128)(2,1)S(1)} %select_select_fusion.refs_0_.piece_ref), channel_id=1, source_target_pairs={{0,1},{1,0},{2,3},{3,2},{4,5},{5,4},{6,7},{7,6},{8,9},{9,8},{10,11... | collective-permute-start | bytes 196616 | tf_op jit(solution)/shard_map/ppermute | solution.py:366
  63.5 5.4 %collective-permute-start.12 = (bf16[256,128]{1,0:T(8,128)(2,1)S(1)}, bf16[256,128]{1,0:T(8,128)(2,1)S(1)}, u32[]{:S(2)}, u32[]{:S(2)}) collective-permute-start(bf16[256,128]{1,0:T(8,128)(2,1)S(1)} %collective-permute-done.10.refs_1_), channel_id=1, source_target_pairs={{0,1},{1,0},{2,3},{3,2},{4,5},{5,4},{6,7},{7,6},{8,9},{9,8},{10,11... | collective-permute-start | bytes 196616 | tf_op jit(solution)/shard_map/ppermute | solution.py:366
  76.0 2.9 %collective-permute-start.13 = (bf16[32,64,128]{2,1,0:T(8,128)(2,1)S(1)}, bf16[32,64,128]{2,1,0:T(8,128)(2,1)S(1)}, u32[]{:S(2)}, u32[]{:S(2)}) collective-permute-start(bf16[32,64,128]{2,1,0:T(8,128)(2,1)S(1)} %gate.3.own_ref), channel_id=1, source_target_pairs={{0,1},{1,0},{2,3},{3,2},{4,5},{5,4},{6,7},{7,6},{8,9},{9,8},{10,11... | collective-permute-start | bytes 1572872 | tf_op jit(solution)/shard_map/ppermute | solution.py:366

commit v4 on v3

--- a/solution.py
+++ b/solution.py
@@ -37,6 +37,8 @@
 Z_GROUPS = [[index_of(z, y, c) for z in range(NZ)] for y in range(NY) for c in range(NC)]
 CHIP_GROUPS = [[index_of(z, y, c) for z in range(NZ) for y in range(NY)] for c in range(NC)]
 OTHER_CORE = permutation(lambda z, y, c: (z, y, 1 - c))
+Y_PARTNER = permutation(lambda z, y, c: (z, y ^ 1, c))
+DIAGONAL = permutation(lambda z, y, c: (z, y ^ 1, 1 - c))
 Y_SHIFTS = [permutation(lambda z, y, c, d=d: (z, (y + d) % NY, c)) for d in range(NY)]
 Z_SHIFTS = [permutation(lambda z, y, c, d=d: ((z + d) % NZ, y, c)) for d in range(NZ)]
 
@@ -67,26 +69,49 @@
     return (dot(rows, table) * SC).astype(BF)
 
 
-def join_kernel(k_ref, v_ref, k_other_ref, v_other_ref, both_ref):
+def halve_kernel(k_ref, v_ref, mine_ref):
     c = coordinates()[2]
     for head in range(NC):
 
         @pl.when(c == head)
         def _(head=head):
             lanes = slice(HD * head, HD * head + HD)
-            for i, source in enumerate((k_ref, v_ref, k_other_ref, v_other_ref)):
-                both_ref[BLK * i : BLK * i + BLK, :] = source[:, lanes]
-
-
-def join(k, v, k_other, v_other):
+            mine_ref[0:BLK, :] = k_ref[:, lanes]
+            mine_ref[BLK : 2 * BLK, :] = v_ref[:, lanes]
+
+
+def halve(k, v):
+    return pl.pallas_call(
+        halve_kernel,
+        out_shape=jax.ShapeDtypeStruct((2 * BLK, HD), BF),
+        in_specs=[VMEM] * 2,
+        out_specs=VMEM,
+        compiler_params=SMALL,
+        name="halve",
+    )(k, v)
+
+
+def join_kernel(mine_ref, k_ref, v_ref, early_ref, both_ref):
+    c = coordinates()[2]
+    both_ref[0 : 2 * BLK, :] = mine_ref[...]
+    for head in range(NC):
+
+        @pl.when(c == head)
+        def _(head=head):
+            lanes = slice(HD * head, HD * head + HD)
+            both_ref[2 * BLK : 3 * BLK, :] = k_ref[:, lanes]
+            both_ref[3 * BLK : 4 * BLK, :] = v_ref[:, lanes]
+
+
+def join(mine, k_other, v_other, early):
     return pl.pallas_call(
         join_kernel,
         out_shape=jax.ShapeDtypeStruct((4 * BLK, HD), BF),
-        in_specs=[VMEM] * 4,
+        in_specs=[VMEM] * 3 + [pl.BlockSpec(memory_space=pl.ANY)],
         out_specs=VMEM,
         compiler_params=SMALL,
         name="join",
-    )(k, v, k_other, v_other)
+    )(mine, k_other, v_other, early)
 
 
 def repeat_kernel(own_ref, other_ref, send_ref, rows_ref):
@@ -132,7 +157,7 @@
 
 
 def pick_kernel(anchor_ref, *refs):
-    columns, out_ref, sems = refs[:NY], refs[NY], refs[NY + 1]
+    columns, out_ref = refs[:NY], refs[NY]
     z, y, c = coordinates()
     wanted = lax.rem(anchor_ref[0], NY * NC)
     rows = HD * lax.rem(y, 2)
@@ -142,27 +167,18 @@
 
         @pl.when(place == wanted)
         def _(which=which):
-            copies = []
             for i in range(2):
                 first = pl.multiple_of(2 * BLK * (which // NY) + BLK * i + rows, HD)
-                source = columns[which % NY].at[pl.ds(first, HD), :]
-                target = out_ref.at[HD * i : HD * i + HD, :]
-                copies.append(pltpu.make_async_copy(source, target, sems.at[i]))
-            for copy in copies:
-                copy.start()
-            for copy in copies:
-                copy.wait()
+                out_ref[HD * i : HD * i + HD, :] = columns[which % NY][pl.ds(first, HD), :]
 
 
 def pick(anchor_index, columns):
-    anywhere = pl.BlockSpec(memory_space=pl.ANY)
     return pl.pallas_call(
         pick_kernel,
         out_shape=jax.ShapeDtypeStruct((BLK, HD), BF),
-        in_specs=[SMEM] + [anywhere] * NY,
-        out_specs=VMEM,
-        scratch_shapes=[pltpu.SemaphoreType.DMA((2,))],
-        compiler_params=pltpu.CompilerParams(vmem_limit_bytes=1024 * 1024),
+        in_specs=[SMEM] + [VMEM] * NY,
+        out_specs=VMEM,
+        compiler_params=SMALL,
         name="pick",
     )(anchor_index, *columns)
 
@@ -251,6 +267,7 @@
     back = (dot(low, table) + dot(middle, table) + dot(high, table)) * SC
     position = (z * NY + y) * 8 + (row & 7)
     back = jnp.where(position < limit_ref[0], back, 0.0).astype(BF)
+    back = back.astype(F32).reshape(8, 8, HD).astype(BF)
     for i in range(NZ * NY):
         send_ref[i] = back
 
@@ -258,7 +275,7 @@
 def combine(limit, parts, piece):
     return pl.pallas_call(
         combine_kernel,
-        out_shape=jax.ShapeDtypeStruct((NZ * NY, 64, HD), BF),
+        out_shape=jax.ShapeDtypeStruct((NZ * NY, 8, 8, HD), BF),
         in_specs=[SMEM, VMEM, pl.BlockSpec(memory_space=pl.ANY)],
         out_specs=VMEM,
         scratch_shapes=[pltpu.VMEM((HD, HD), F32)],
@@ -331,32 +348,32 @@
     )(anchor_index, lengths, q, k, v, *pieces)
 
 
-def assemble_kernel(own_ref, other_ref, out_ref):
+def assemble_kernel(part_ref, *refs, own):
+    out_ref, sems = refs[-2:]
     c = coordinates()[2]
-    for pair in range(4):
-        sources = []
-        for i in (2 * pair, 2 * pair + 1):
-            own, other = own_ref[i].astype(F32), other_ref[i].astype(F32)
-            sources.append((jnp.where(c == 0, own, other), jnp.where(c == 0, other, own)))
-        rows = slice(16 * pair, 16 * pair + 16)
-        for g in range(2):
-            for j in range(8):
-                parts = [source[g][8 * j : 8 * j + 8] for source in sources]
-                lanes = slice(HD * (8 * g + j), HD * (8 * g + j) + HD)
-                out_ref[rows, lanes] = jnp.concatenate(parts, axis=0).astype(BF)
-
-
-def assemble(own, other):
-    part = pl.BlockSpec((8, 64, HD), lambda i: (i, 0, 0))
-    return pl.pallas_call(
-        assemble_kernel,
-        grid=(4,),
-        out_shape=jax.ShapeDtypeStruct((256, 2048), BF),
-        in_specs=[part] * 2,
-        out_specs=pl.BlockSpec((64, 2048), lambda i: (i, 0)),
-        compiler_params=PARAMS,
+    head = c if own else 1 - c
+    copies = []
+    for j in range(8):
+        lanes = pl.ds(pl.multiple_of(HD * (8 * head + j), HD), HD)
+        copies.append(pltpu.make_async_copy(part_ref.at[:, j], out_ref.at[:, :, lanes], sems.at[j]))
+    for copy in copies:
+        copy.start()
+    for copy in copies:
+        copy.wait()
+
+
+def assemble(part, out=None):
+    anywhere = pl.BlockSpec(memory_space=pl.ANY)
+    return pl.pallas_call(
+        functools.partial(assemble_kernel, own=out is None),
+        out_shape=jax.ShapeDtypeStruct((32, 8, 2048), BF),
+        in_specs=[anywhere] * (1 if out is None else 2),
+        out_specs=anywhere,
+        scratch_shapes=[pltpu.SemaphoreType.DMA((8,))],
+        input_output_aliases={} if out is None else {1: 0},
+        compiler_params=SMALL,
         name="assemble",
-    )(own, other)
+    )(part, *([] if out is None else [out]))
 
 
 def on_device(
@@ -374,8 +391,10 @@
     def with_other_core(parts):
         return parts + [swap(x) for x in parts]
 
-    columns = along_y(join(context_k, context_v, swap(context_k), swap(context_v)))
-    spread_rows = repeat(question, swap(question))
+    mine = halve(context_k, context_v)
+    other_question = swap(question)
+    columns = along_y(join(mine, swap(context_k), swap(context_v), other_question))
+    spread_rows = repeat(question, other_question)
     got = lax.all_to_all(spread_rows, "ctx", 0, 0, axis_index_groups=Z_GROUPS)
     columns = [columns[0], *gate(columns[1:], got)]
     piece = pick(anchor_index, columns)
@@ -389,17 +408,18 @@
     piece = jnp.where(near, piece, jnp.where(distance < 5, below, above))
     spread = combine(question_length, parts, piece)
     own = lax.all_to_all(spread, "ctx", 0, 0, axis_index_groups=CHIP_GROUPS)
-    pieces = [piece, lax.ppermute(piece, "ctx", Y_SHIFTS[1])]
+    pieces = [piece, lax.ppermute(piece, "ctx", Y_PARTNER)]
+    pieces = pieces + [swap(piece), lax.ppermute(piece, "ctx", DIAGONAL)]
     mixed, key_cache, value_cache, token = encode(
         anchor_index,
         block_lengths,
         context_q,
         context_k,
         context_v,
-        pieces + [swap(x) for x in pieces],
+        pieces,
     )
     (own,) = gate([own], token)
-    answer = assemble(own, swap(own))
+    answer = assemble(swap(own), assemble(own)).reshape(256, 2048)
     return mixed, key_cache, value_cache, answer
 
 

time: 81 us -> 79.4 us (0.980)
  starting transfers between devices: 41.5 us -> 37.8 us
  waiting for transfers between devices: 19 us -> 21 us
    ppermute x6 -> x5, starting transfers between devices: 14 us -> 6.27 us  [swap(): return lax.ppermute(x, 'ctx', OTHER_CORE)]
    ppermute x1 -> x2, waiting for transfers between devices: 0.01 us -> 5.43 us  [the longest x1 4.79 us: on_device(): pieces = pieces + [swap(piece), lax.ppermute(piece, 'ctx', DIAGONAL)]]
    ppermute x6 -> x5, waiting for transfers between devices: 4.73 us -> 0.69 us  [swap(): return lax.ppermute(x, 'ctx', OTHER_CORE)]
    ppermute x1 -> x2, starting transfers between devices: 1.49 us -> 3.88 us  [the longest x1 3.48 us: on_device(): pieces = pieces + [swap(piece), lax.ppermute(piece, 'ctx', DIAGONAL)]]
    ppermute x2, starting transfers between devices: 5.8 us -> 7.69 us  [along_z(): lax.ppermute(x, 'ctx', Z_SHIFTS[NZ - d])]
    pallas_call x2 -> x4, Pallas kernels: 3.13 us -> 3.22 us  [the longest x2 1.69 us: assemble(): pl.pallas_call(functools.partial(assemble_kernel, own=out is None), out_s...]
  transfers between devices with their start and end apart: 17 -> 17, of which waited for: 8 -> 6; matrix products, arithmetic and copies ran while one was open for 0% -> 0% of each run, Pallas kernels for 15% -> 16%
where the time goes in v4:
time: 79.4 us; the launch traced here: 79 us
  starting transfers between devices  37.8 us (48%)
  waiting for transfers between devices  21 us (26%)
  Pallas kernels  15.9 us (20%)
  local copies, waits for them, and re-layouts  2.49 us (3%)
  between operations  1.78 us (2%)
    all_to_all x1, starting transfers between devices, on_device(): got = lax.all_to_all(spread_rows, 'ctx', 0, 0, axis_index_groups=Z_GROUPS)  8.19 us
    ppermute x2, starting transfers between devices, along_z(): lax.ppermute(x, 'ctx', Z_SHIFTS[NZ - d])  7.69 us
    all_to_all x1, waiting for transfers between devices, on_device(): got = lax.all_to_all(spread_rows, 'ctx', 0, 0, axis_index_groups=Z_GROUPS)  7.07 us
    pallas_call x1, Pallas kernels, encode(): pl.pallas_call(encode_kernel, grid=(2,), out_shape=(jax.ShapeDtypeStruct(...  7.05 us
    ppermute x5, starting transfers between devices, swap(): return lax.ppermute(x, 'ctx', OTHER_CORE)  6.27 us
    ppermute x2, waiting for transfers between devices, along_z(): lax.ppermute(x, 'ctx', Z_SHIFTS[d])  5.58 us
    all_to_all x1, starting transfers between devices, on_device(): own = lax.all_to_all(spread, 'ctx', 0, 0, axis_index_groups=CHIP_GROUPS)  5.58 us
    ppermute x1, waiting for transfers between devices, on_device(): pieces = pieces + [swap(piece), lax.ppermute(piece, 'ctx', DIAGONAL)]  4.79 us
  transfers between devices with their start and end apart: 17, of which 6 were waited for; matrix products, arithmetic and copies ran while one was open for 0% of the time, Pallas kernels for 16%

profile of v4, /device:TPU:1, one launch (start us, length us, event | category | flops | bytes accessed | tf_op | source)
XLA Modules:
  0.0 79.0 jit_solution(12407796303272420865)
XLA Ops:
  0.6 3.3 %collective-permute-start = (bf16[256,256]{1,0:T(8,128)(2,1)}, bf16[256,256]{1,0:T(8,128)(2,1)S(1)}, u32[]{:S(2)}, u32[]{:S(2)}) collective-permute-start(bf16[256,256]{1,0:T(8,128)(2,1)} %k_ref.3), channel_id=1, source_target_pairs={{0,1},{1,0},{2,3},{3,2},{4,5},{5,4},{6,7},{7,6},{8,9},{9,8},{10,11... | collective-permute-start | bytes 393224 | tf_op jit(solution)/shard_map/ppermute | solution.py:383
  4.0 0.1 collective-permute-start.1
  4.1 0.4 collective-permute-start.2
  4.5 0.9 %copy-done = bf16[256,256]{1,0:T(8,128)(2,1)S(1)} copy-done((bf16[256,256]{1,0:T(8,128)(2,1)S(1)}, bf16[256,256]{1,0:T(8,128)(2,1)}, u32[]{:S(2)}) %copy-start) | copy-done | bytes 131096
  5.4 0.9 %copy-done.2 = bf16[256,256]{1,0:T(8,128)(2,1)S(1)} copy-done((bf16[256,256]{1,0:T(8,128)(2,1)S(1)}, bf16[256,256]{1,0:T(8,128)(2,1)}, u32[]{:S(2)}) %copy-start.2) | copy-done | bytes 131096
  6.3 0.0 copy-start.4
  6.3 0.0 collective-permute-done.2.early_ref.other_ref
  6.3 0.0 collective-permute-done.k_ref
  6.3 0.0 collective-permute-done.1.v_ref
  6.4 1.1 %collective-permute-start.5 = (bf16[1024,128]{1,0:T(8,128)(2,1)S(1)}, bf16[1024,128]{1,0:T(8,128)(2,1)S(1)}, u32[]{:S(2)}, u32[]{:S(2)}) collective-permute-start(bf16[1024,128]{1,0:T(8,128)(2,1)S(1)} %join.1.refs_0_), channel_id=1, source_target_pairs={{0,6},{1,7},{2,0},{3,1},{4,2},{5,3},{6,4},{7,5},{8,14},{9,15},{10,... | collective-permute-start | bytes 786440 | tf_op jit(solution)/shard_map/ppermute | solution.py:386
  7.5 0.3 collective-permute-start.4
  7.9 0.7 collective-permute-start.3
  8.5 0.7 repeat.1
  9.2 8.2 %all-to-all-start = ((bf16[8,64,128]{2,1,0:T(8,128)(2,1)}), bf16[8,64,128]{2,1,0:T(8,128)(2,1)S(1)}, u32[]{:S(2)}, u32[]{:S(2)}) async-start(bf16[8,64,128]{2,1,0:T(8,128)(2,1)} %repeat.1), calls=%async_computation | async-start | bytes 262144 | tf_op jit(solution)/shard_map/all_to_all | solution.py:398
  17.4 0.7 copy-done.5
  18.2 7.1 %all-to-all-done.refs_3_.got_ref = bf16[8,64,128]{2,1,0:T(8,128)(2,1)S(1)} async-done(((bf16[8,64,128]{2,1,0:T(8,128)(2,1)}), bf16[8,64,128]{2,1,0:T(8,128)(2,1)S(1)}, u32[]{:S(2)}, u32[]{:S(2)}) %all-to-all-start) | async-done | bytes 131104 | tf_op jit(solution)/shard_map/all_to_all | solution.py:398
  25.3 0.0 collective-permute-done.5.refs_2_
  25.3 0.0 collective-permute-done.4.refs_1_
  25.3 0.0 collective-permute-done.3.refs_0_
  25.3 0.0 copy-start.7
  25.4 0.6 pick.1
  26.0 3.2 %collective-permute-start.7 = (bf16[256,128]{1,0:T(8,128)(2,1)S(1)}, bf16[256,128]{1,0:T(8,128)(2,1)S(1)}, u32[]{:S(2)}, u32[]{:S(2)}) collective-permute-start(bf16[256,128]{1,0:T(8,128)(2,1)S(1)} %pick.1), channel_id=1, source_target_pairs={{0,56},{1,57},{2,58},{3,59},{4,60},{5,61},{6,62},{7,63},{8,0},{9,1... | collective-permute-start | bytes 196616 | tf_op jit(solution)/shard_map/ppermute | solution.py:389
  29.1 0.0 collective-permute-start.6
  29.1 4.3 %question_pass.1 = f32[8,72,128]{2,1,0:T(8,128)} custom-call(s32[64]{0:T(128)S(1)} %copy-done.7, bf16[8,64,128]{2,1,0:T(8,128)(2,1)S(1)} %all-to-all-done.refs_3_.got_ref, bf16[1024,128]{1,0:T(8,128)(2,1)S(1)} %join.1.refs_0_, bf16[1024,128]{1,0:T(8,128)(2,1)S(1)} %get-tuple-element.11.refs_1_, bf16[1024,128]{1,0:T(8,128)(2,1)S(1)} %get-tuple-element.12.refs_2_, ...), custom_call_target="tpu_custom_call" | custom-call | flops 900000000 | bytes 2500000 | tf_op jit(solution)/shard_map/question_pass/pallas_call | solution.py:236
  33.4 4.1 %all-to-all-start.1 = ((f32[8,72,128]{2,1,0:T(8,128)}), f32[8,72,128]{2,1,0:T(8,128)S(1)}, u32[]{:S(2)}, u32[]{:S(2)}) async-start(f32[8,72,128]{2,1,0:T(8,128)} %question_pass.1), calls=%async_computation.1 | async-start | bytes 589824 | tf_op jit(solution)/shard_map/all_to_all | solution.py:403
  37.5 0.0 collective-permute-done.7
  37.5 0.0 collective-permute-done.6
  37.5 4.5 %collective-permute-start.9 = (bf16[256,128]{1,0:T(8,128)(2,1)S(1)}, bf16[256,128]{1,0:T(8,128)(2,1)S(1)}, u32[]{:S(2)}, u32[]{:S(2)}) collective-permute-start(bf16[256,128]{1,0:T(8,128)(2,1)S(1)} %select_select_fusion.1), channel_id=1, source_target_pairs={{0,40},{1,41},{2,42},{3,43},{4,44},{5,45},{6,46},{7,47},{8,48},{9,... | collective-permute-start | bytes 196616 | tf_op jit(solution)/shard_map/ppermute | solution.py:389
  42.1 0.0 collective-permute-start.8
  42.7 0.0 copy-start.6
  42.8 2.2 %collective-permute-done.9 = bf16[256,128]{1,0:T(8,128)(2,1)S(1)} collective-permute-done((bf16[256,128]{1,0:T(8,128)(2,1)S(1)}, bf16[256,128]{1,0:T(8,128)(2,1)S(1)}, u32[]{:S(2)}, u32[]{:S(2)}) %collective-permute-start.9) | collective-permute-done | bytes 65568 | tf_op jit(solution)/shard_map/ppermute | solution.py:389
  44.9 5.6 %collective-permute-done.8 = bf16[256,128]{1,0:T(8,128)(2,1)S(1)} collective-permute-done((bf16[256,128]{1,0:T(8,128)(2,1)S(1)}, bf16[256,128]{1,0:T(8,128)(2,1)S(1)}, u32[]{:S(2)}, u32[]{:S(2)}) %collective-permute-start.8) | collective-permute-done | bytes 65568 | tf_op jit(solution)/shard_map/ppermute | solution.py:389
  50.5 0.0 all-to-all-done.1.parts_ref
  50.5 1.5 %combine.1 = bf16[32,8,8,128]{3,2,1,0:T(8,128)(2,1)} custom-call(s32[1]{0:T(128)S(6)} %copy.21.limit_ref, f32[8,72,128]{2,1,0:T(8,128)S(1)} %all-to-all-done.1.parts_ref, bf16[256,128]{1,0:T(8,128)(2,1)S(1)} %select_select_fusion.refs_0_.piece_ref), custom_call_target="tpu_custom_call" | custom-call | tf_op jit(solution)/shard_map/combine/pallas_call | solution.py:276
  52.0 5.6 %all-to-all-start.2 = ((bf16[32,8,8,128]{3,2,1,0:T(8,128)(2,1)}), bf16[32,8,8,128]{3,2,1,0:T(8,128)(2,1)S(1)}, u32[]{:S(2)}, u32[]{:S(2)}) async-start(bf16[32,8,8,128]{3,2,1,0:T(8,128)(2,1)} %combine.1), calls=%async_computation.2 | async-start | bytes 1048576 | tf_op jit(solution)/shard_map/all_to_all | solution.py:410
  57.6 3.5 %collective-permute-start.12 = (bf16[256,128]{1,0:T(8,128)(2,1)S(1)}, bf16[256,128]{1,0:T(8,128)(2,1)S(1)}, u32[]{:S(2)}, u32[]{:S(2)}) collective-permute-start(bf16[256,128]{1,0:T(8,128)(2,1)S(1)} %select_select_fusion.refs_0_.piece_ref), channel_id=1, source_target_pairs={{0,3},{1,2},{2,1},{3,0},{4,7},{5,6},{6,5},{7,4},{8,11},{9,10},{10,... | collective-permute-start | bytes 196616 | tf_op jit(solution)/shard_map/ppermute | solution.py:412
  61.1 0.0 collective-permute-start.11
  61.1 0.4 collective-permute-start.10
  61.5 4.8 %collective-permute-done.12.refs_3_ = bf16[256,128]{1,0:T(8,128)(2,1)S(1)} collective-permute-done((bf16[256,128]{1,0:T(8,128)(2,1)S(1)}, bf16[256,128]{1,0:T(8,128)(2,1)S(1)}, u32[]{:S(2)}, u32[]{:S(2)}) %collective-permute-start.12) | collective-permute-done | bytes 65568 | tf_op jit(solution)/shard_map/ppermute | solution.py:412
  66.3 0.0 collective-permute-done.11.refs_2_
  66.3 0.6 collective-permute-done.10.refs_1_
  66.9 0.0 copy-done.3
  67.0 7.1 %encode.1 = (bf16[256,2048]{1,0:T(8,128)(2,1)}, bf16[256,256]{1,0:T(8,128)(2,1)}, bf16[256,256]{1,0:T(8,128)(2,1)}, f32[8,128]{1,0:T(8,128)S(1)}) custom-call(s32[64]{0:T(128)S(1)} %copy-done.5, s32[64]{0:T(128)S(1)} %copy-done.7, bf16[256,2048]{1,0:T(8,128)(2,1)S(1)} %copy-done.6, bf16[256,256]{1,0:T(8,128)(2,1)S(1)} %copy-done.1, ...), custom_call_target="tpu_custom_call" | custom-call | flops 1100000000 | bytes 3500000 | tf_op jit(solution)/shard_map/encode/pallas_call | solution.py:331
  74.0 0.0 all-to-all-done.2.refs_0_
  74.0 2.4 %collective-permute-start.13 = (bf16[32,8,8,128]{3,2,1,0:T(8,128)(2,1)S(1)}, bf16[32,8,8,128]{3,2,1,0:T(8,128)(2,1)S(1)}, u32[]{:S(2)}, u32[]{:S(2)}) collective-permute-start(bf16[32,8,8,128]{3,2,1,0:T(8,128)(2,1)S(1)} %gate.3.part_ref), channel_id=1, source_target_pairs={{0,1},{1,0},{2,3},{3,2},{4,5},{5,4},{6,7},{7,6},{8,9},{9,8},{10,11... | collective-permute-start | bytes 1572872 | tf_op jit(solution)/shard_map/ppermute | solution.py:383
  76.4 0.8 %assemble.2.refs_0_ = bf16[32,8,2048]{2,1,0:T(8,128)(2,1)} custom-call(bf16[32,8,8,128]{3,2,1,0:T(8,128)(2,1)S(1)} %gate.3.part_ref), custom_call_target="tpu_custom_call" | custom-call | tf_op jit(solution)/shard_map/assemble/pallas_call | solution.py:367
  77.3 0.7 collective-permute-done.13.part_ref
  78.0 0.8 %assemble.3 = bf16[32,8,2048]{2,1,0:T(8,128)(2,1)} custom-call(bf16[32,8,8,128]{3,2,1,0:T(8,128)(2,1)S(1)} %collective-permute-done.13.part_ref, bf16[32,8,2048]{2,1,0:T(8,128)(2,1)} %assemble.2.refs_0_), custom_call_target="tpu_custom_call", output_to_operand_aliasing={{}: (1, {})} | custom-call | tf_op jit(solution)/shard_map/assemble/pallas_call | solution.py:367
  (15 shorter events, 0.1 us)
Async XLA Ops:
  0.6 5.7 %collective-permute-start = (bf16[256,256]{1,0:T(8,128)(2,1)}, bf16[256,256]{1,0:T(8,128)(2,1)S(1)}, u32[]{:S(2)}, u32[]{:S(2)}) collective-permute-start(bf16[256,256]{1,0:T(8,128)(2,1)} %k_ref.3), channel_id=1, source_target_pairs={{0,1},{1,0},{2,3},{3,2},{4,5},{5,4},{6,7},{7,6},{8,9},{9,8},{10,11... | collective-permute-start | bytes 393224 | tf_op jit(solution)/shard_map/ppermute | solution.py:383
  4.0 2.4 %collective-permute-start.1 = (bf16[256,256]{1,0:T(8,128)(2,1)}, bf16[256,256]{1,0:T(8,128)(2,1)S(1)}, u32[]{:S(2)}, u32[]{:S(2)}) collective-permute-start(bf16[256,256]{1,0:T(8,128)(2,1)} %v_ref.3), channel_id=1, source_target_pairs={{0,1},{1,0},{2,3},{3,2},{4,5},{5,4},{6,7},{7,6},{8,9},{9,8},{10,11... | collective-permute-start | bytes 393224 | tf_op jit(solution)/shard_map/ppermute | solution.py:383
  4.1 2.3 %collective-permute-start.2 = (bf16[4,2048]{1,0:T(4,128)(2,1)}, bf16[4,2048]{1,0:T(4,128)(2,1)S(1)}, u32[]{:S(2)}, u32[]{:S(2)}) collective-permute-start(bf16[4,2048]{1,0:T(4,128)(2,1)} %own_ref.1), channel_id=1, source_target_pairs={{0,1},{1,0},{2,3},{3,2},{4,5},{5,4},{6,7},{7,6},{8,9},{9,8},{10,11... | collective-permute-start | bytes 49160 | tf_op jit(solution)/shard_map/ppermute | solution.py:383
  4.5 0.9 %copy-start = (bf16[256,256]{1,0:T(8,128)(2,1)S(1)}, bf16[256,256]{1,0:T(8,128)(2,1)}, u32[]{:S(2)}) copy-start(bf16[256,256]{1,0:T(8,128)(2,1)} %k_ref.3) | copy-start | bytes 393220
  5.4 0.9 %copy-start.2 = (bf16[256,256]{1,0:T(8,128)(2,1)S(1)}, bf16[256,256]{1,0:T(8,128)(2,1)}, u32[]{:S(2)}) copy-start(bf16[256,256]{1,0:T(8,128)(2,1)} %v_ref.3) | copy-start | bytes 393220
  6.3 2.2 %copy-start.4 = (bf16[4,2048]{1,0:T(4,128)(2,1)S(1)}, bf16[4,2048]{1,0:T(4,128)(2,1)}, u32[]{:S(2)}) copy-start(bf16[4,2048]{1,0:T(4,128)(2,1)} %own_ref.1) | copy-start | bytes 49156
  6.4 18.9 %collective-permute-start.5 = (bf16[1024,128]{1,0:T(8,128)(2,1)S(1)}, bf16[1024,128]{1,0:T(8,128)(2,1)S(1)}, u32[]{:S(2)}, u32[]{:S(2)}) collective-permute-start(bf16[1024,128]{1,0:T(8,128)(2,1)S(1)} %join.1.refs_0_), channel_id=1, source_target_pairs={{0,6},{1,7},{2,0},{3,1},{4,2},{5,3},{6,4},{7,5},{8,14},{9,15},{10,... | collective-permute-start | bytes 786440 | tf_op jit(solution)/shard_map/ppermute | solution.py:386
  7.5 17.8 %collective-permute-start.4 = (bf16[1024,128]{1,0:T(8,128)(2,1)S(1)}, bf16[1024,128]{1,0:T(8,128)(2,1)S(1)}, u32[]{:S(2)}, u32[]{:S(2)}) collective-permute-start(bf16[1024,128]{1,0:T(8,128)(2,1)S(1)} %join.1.refs_0_), channel_id=1, source_target_pairs={{0,4},{1,5},{2,6},{3,7},{4,0},{5,1},{6,2},{7,3},{8,12},{9,13},{10,... | collective-permute-start | bytes 786440 | tf_op jit(solution)/shard_map/ppermute | solution.py:386
  7.9 17.5 %collective-permute-start.3 = (bf16[1024,128]{1,0:T(8,128)(2,1)S(1)}, bf16[1024,128]{1,0:T(8,128)(2,1)S(1)}, u32[]{:S(2)}, u32[]{:S(2)}) collective-permute-start(bf16[1024,128]{1,0:T(8,128)(2,1)S(1)} %join.1.refs_0_), channel_id=1, source_target_pairs={{0,2},{1,3},{2,4},{3,5},{4,6},{5,7},{6,0},{7,1},{8,10},{9,11},{10,... | collective-permute-start | bytes 786440 | tf_op jit(solution)/shard_map/ppermute | solution.py:386
  9.2 16.1 %all-to-all-start = ((bf16[8,64,128]{2,1,0:T(8,128)(2,1)}), bf16[8,64,128]{2,1,0:T(8,128)(2,1)S(1)}, u32[]{:S(2)}, u32[]{:S(2)}) async-start(bf16[8,64,128]{2,1,0:T(8,128)(2,1)} %repeat.1), calls=%async_computation | async-start | bytes 262144 | tf_op jit(solution)/shard_map/all_to_all | solution.py:398
  17.4 0.7 copy-start.5
  25.3 3.8 %copy-start.7 = (s32[64]{0:T(128)S(1)}, s32[64]{0:T(128)}, u32[]{:S(2)}) copy-start(s32[64]{0:T(128)} %lengths_ref.3) | copy-start | bytes 772
  26.0 11.5 %collective-permute-start.7 = (bf16[256,128]{1,0:T(8,128)(2,1)S(1)}, bf16[256,128]{1,0:T(8,128)(2,1)S(1)}, u32[]{:S(2)}, u32[]{:S(2)}) collective-permute-start(bf16[256,128]{1,0:T(8,128)(2,1)S(1)} %pick.1), channel_id=1, source_target_pairs={{0,56},{1,57},{2,58},{3,59},{4,60},{5,61},{6,62},{7,63},{8,0},{9,1... | collective-permute-start | bytes 196616 | tf_op jit(solution)/shard_map/ppermute | solution.py:389
  29.1 8.4 %collective-permute-start.6 = (bf16[256,128]{1,0:T(8,128)(2,1)S(1)}, bf16[256,128]{1,0:T(8,128)(2,1)S(1)}, u32[]{:S(2)}, u32[]{:S(2)}) collective-permute-start(bf16[256,128]{1,0:T(8,128)(2,1)S(1)} %pick.1), channel_id=1, source_target_pairs={{0,8},{1,9},{2,10},{3,11},{4,12},{5,13},{6,14},{7,15},{8,16},{9,17... | collective-permute-start | bytes 196616 | tf_op jit(solution)/shard_map/ppermute | solution.py:389
  33.4 17.1 %all-to-all-start.1 = ((f32[8,72,128]{2,1,0:T(8,128)}), f32[8,72,128]{2,1,0:T(8,128)S(1)}, u32[]{:S(2)}, u32[]{:S(2)}) async-start(f32[8,72,128]{2,1,0:T(8,128)} %question_pass.1), calls=%async_computation.1 | async-start | bytes 589824 | tf_op jit(solution)/shard_map/all_to_all | solution.py:403
  37.5 7.4 %collective-permute-start.9 = (bf16[256,128]{1,0:T(8,128)(2,1)S(1)}, bf16[256,128]{1,0:T(8,128)(2,1)S(1)}, u32[]{:S(2)}, u32[]{:S(2)}) collective-permute-start(bf16[256,128]{1,0:T(8,128)(2,1)S(1)} %select_select_fusion.1), channel_id=1, source_target_pairs={{0,40},{1,41},{2,42},{3,43},{4,44},{5,45},{6,46},{7,47},{8,48},{9,... | collective-permute-start | bytes 196616 | tf_op jit(solution)/shard_map/ppermute | solution.py:389
  42.1 8.4 %collective-permute-start.8 = (bf16[256,128]{1,0:T(8,128)(2,1)S(1)}, bf16[256,128]{1,0:T(8,128)(2,1)S(1)}, u32[]{:S(2)}, u32[]{:S(2)}) collective-permute-start(bf16[256,128]{1,0:T(8,128)(2,1)S(1)} %select_select_fusion.1), channel_id=1, source_target_pairs={{0,24},{1,25},{2,26},{3,27},{4,28},{5,29},{6,30},{7,31},{8,32},{9,... | collective-permute-start | bytes 196616 | tf_op jit(solution)/shard_map/ppermute | solution.py:389
  42.7 24.2 %copy-start.6 = (bf16[256,2048]{1,0:T(8,128)(2,1)S(1)}, bf16[256,2048]{1,0:T(8,128)(2,1)}, u32[]{:S(2)}) copy-start(bf16[256,2048]{1,0:T(8,128)(2,1)} %q_ref.1) | copy-start | bytes 3145732
  52.0 14.9 %copy-start.1 = (bf16[256,256]{1,0:T(8,128)(2,1)S(1)}, bf16[256,256]{1,0:T(8,128)(2,1)}, u32[]{:S(2)}) copy-start(bf16[256,256]{1,0:T(8,128)(2,1)} %k_ref.3) | copy-start | bytes 393220
  52.0 14.9 %copy-start.3 = (bf16[256,256]{1,0:T(8,128)(2,1)S(1)}, bf16[256,256]{1,0:T(8,128)(2,1)}, u32[]{:S(2)}) copy-start(bf16[256,256]{1,0:T(8,128)(2,1)} %v_ref.3) | copy-start | bytes 393220
  52.0 22.0 %all-to-all-start.2 = ((bf16[32,8,8,128]{3,2,1,0:T(8,128)(2,1)}), bf16[32,8,8,128]{3,2,1,0:T(8,128)(2,1)S(1)}, u32[]{:S(2)}, u32[]{:S(2)}) async-start(bf16[32,8,8,128]{3,2,1,0:T(8,128)(2,1)} %combine.1), calls=%async_computation.2 | async-start | bytes 1048576 | tf_op jit(solution)/shard_map/all_to_all | solution.py:410
  57.6 8.7 %collective-permute-start.12 = (bf16[256,128]{1,0:T(8,128)(2,1)S(1)}, bf16[256,128]{1,0:T(8,128)(2,1)S(1)}, u32[]{:S(2)}, u32[]{:S(2)}) collective-permute-start(bf16[256,128]{1,0:T(8,128)(2,1)S(1)} %select_select_fusion.refs_0_.piece_ref), channel_id=1, source_target_pairs={{0,3},{1,2},{2,1},{3,0},{4,7},{5,6},{6,5},{7,4},{8,11},{9,10},{10,... | collective-permute-start | bytes 196616 | tf_op jit(solution)/shard_map/ppermute | solution.py:412
  61.1 5.2 %collective-permute-start.11 = (bf16[256,128]{1,0:T(8,128)(2,1)S(1)}, bf16[256,128]{1,0:T(8,128)(2,1)S(1)}, u32[]{:S(2)}, u32[]{:S(2)}) collective-permute-start(bf16[256,128]{1,0:T(8,128)(2,1)S(1)} %select_select_fusion.refs_0_.piece_ref), channel_id=1, source_target_pairs={{0,1},{1,0},{2,3},{3,2},{4,5},{5,4},{6,7},{7,6},{8,9},{9,8},{10,11... | collective-permute-start | bytes 196616 | tf_op jit(solution)/shard_map/ppermute | solution.py:383
  61.1 5.8 %collective-permute-start.10 = (bf16[256,128]{1,0:T(8,128)(2,1)S(1)}, bf16[256,128]{1,0:T(8,128)(2,1)S(1)}, u32[]{:S(2)}, u32[]{:S(2)}) collective-permute-start(bf16[256,128]{1,0:T(8,128)(2,1)S(1)} %select_select_fusion.refs_0_.piece_ref), channel_id=1, source_target_pairs={{0,2},{1,3},{2,0},{3,1},{4,6},{5,7},{6,4},{7,5},{8,10},{9,11},{10,... | collective-permute-start | bytes 196616 | tf_op jit(solution)/shard_map/ppermute | solution.py:411
  74.0 4.0 %collective-permute-start.13 = (bf16[32,8,8,128]{3,2,1,0:T(8,128)(2,1)S(1)}, bf16[32,8,8,128]{3,2,1,0:T(8,128)(2,1)S(1)}, u32[]{:S(2)}, u32[]{:S(2)}) collective-permute-start(bf16[32,8,8,128]{3,2,1,0:T(8,128)(2,1)S(1)} %gate.3.part_ref), channel_id=1, source_target_pairs={{0,1},{1,0},{2,3},{3,2},{4,5},{5,4},{6,7},{7,6},{8,9},{9,8},{10,11... | collective-permute-start | bytes 1572872 | tf_op jit(solution)/shard_map/ppermute | solution.py:383

commit v5 on v4

--- a/solution.py
+++ b/solution.py
@@ -39,7 +39,7 @@
 OTHER_CORE = permutation(lambda z, y, c: (z, y, 1 - c))
 Y_PARTNER = permutation(lambda z, y, c: (z, y ^ 1, c))
 DIAGONAL = permutation(lambda z, y, c: (z, y ^ 1, 1 - c))
-Y_SHIFTS = [permutation(lambda z, y, c, d=d: (z, (y + d) % NY, c)) for d in range(NY)]
+Y_MOVES = [permutation(lambda z, y, c, d=d: (z, y ^ d, c)) for d in range(NY)]
 Z_SHIFTS = [permutation(lambda z, y, c, d=d: ((z + d) % NZ, y, c)) for d in range(NZ)]
 
 
@@ -67,28 +67,6 @@
 
 def rotated(rows, table):
     return (dot(rows, table) * SC).astype(BF)
-
-
-def halve_kernel(k_ref, v_ref, mine_ref):
-    c = coordinates()[2]
-    for head in range(NC):
-
-        @pl.when(c == head)
-        def _(head=head):
-            lanes = slice(HD * head, HD * head + HD)
-            mine_ref[0:BLK, :] = k_ref[:, lanes]
-            mine_ref[BLK : 2 * BLK, :] = v_ref[:, lanes]
-
-
-def halve(k, v):
-    return pl.pallas_call(
-        halve_kernel,
-        out_shape=jax.ShapeDtypeStruct((2 * BLK, HD), BF),
-        in_specs=[VMEM] * 2,
-        out_specs=VMEM,
-        compiler_params=SMALL,
-        name="halve",
-    )(k, v)
 
 
 def join_kernel(mine_ref, k_ref, v_ref, early_ref, both_ref):
@@ -163,7 +141,7 @@
     rows = HD * lax.rem(y, 2)
     for which in range(8):
         core = c if which < NY else 1 - c
-        place = NC * lax.rem(y + NY - which % NY, NY) + core
+        place = NC * (y ^ which % NY) + core
 
         @pl.when(place == wanted)
         def _(which=which):
@@ -195,30 +173,33 @@
     z, y, c = coordinates()
     table = sign_table()
     lane = lax.broadcasted_iota(jnp.int32, (BLK, BLK), 1)
-    ids = [index_of(z, lax.rem(y + NY - d, NY), c) for d in range(NY)]
-    ids += [index_of(z, lax.rem(y + NY - d, NY), 1 - c) for d in range(NY)]
+    ids = [index_of(z, y ^ d, c) for d in range(NY)]
+    ids += [index_of(z, y ^ d, 1 - c) for d in range(NY)]
     q = rotated(got_ref[...].reshape(NZ * 64, HD), table)
-    halves = [q[0:BLK], q[BLK : 2 * BLK]]
-    tops, totals, sums = [None] * 2, [None] * 2, [None] * 2
-    for which in range(8):
-        column, first = columns[which % NY], 2 * BLK * (which // NY)
-        k = rotated(column[first : first + BLK, :], table)
-        v = rotated(column[first + BLK : first + 2 * BLK, :], table)
-        ok = lane < lengths_ref[ids[which]]
-        for i in range(2):
-            part = jnp.where(ok, across(halves[i], k) * SC2, -jnp.inf)
+    turned = [rotated(column[...], table) for column in columns]
+    tops, totals, sums = [], [], []
+    for i in range(2):
+        chunk = q[BLK * i : BLK * i + BLK]
+        top = total = summed = None
+        for which in range(8):
+            column, first = turned[which % NY], 2 * BLK * (which // NY)
+            k, v = column[first : first + BLK], column[first + BLK : first + 2 * BLK]
+            part = jnp.where(lane < lengths_ref[ids[which]], across(chunk, k) * SC2, -jnp.inf)
             m = jnp.max(part, axis=1, keepdims=True)
             e = jnp.exp2(part - m)
             d = jnp.sum(e, axis=1, keepdims=True)
             n = dot(e.astype(BF), v)
             if which == 0:
-                tops[i], totals[i], sums[i] = m, d, n
+                top, total, summed = m, d, n
             else:
-                new = jnp.maximum(tops[i], m)
-                old_scale, scale = jnp.exp2(tops[i] - new), jnp.exp2(m - new)
-                tops[i] = new
-                totals[i] = totals[i] * old_scale + d * scale
-                sums[i] = sums[i] * old_scale + n * scale
+                new = jnp.maximum(top, m)
+                old_scale, scale = jnp.exp2(top - new), jnp.exp2(m - new)
+                top = new
+                total = total * old_scale + d * scale
+                summed = summed * old_scale + n * scale
+        tops.append(top)
+        totals.append(total)
+        sums.append(summed)
     lanes = lax.broadcasted_iota(jnp.int32, (HD, HD), 1)
     packed = jnp.zeros((HD, HD), F32)
     for i in range(4):
@@ -251,19 +232,17 @@
     table = sign_table()
     tops = [parts_ref[s, pl.ds(64 + z // 2, 1), :] for s in range(NZ)]
     totals = [parts_ref[s, pl.ds(68 + z // 2, 1), :] for s in range(NZ)]
-    square = jnp.concatenate(tops + totals + [jnp.zeros((HD - 16, HD), F32)], axis=0)
+    tops, totals = jnp.concatenate(tops, axis=0), jnp.concatenate(totals, axis=0)
+    weights = jnp.exp2(tops - jnp.max(tops, axis=0, keepdims=True))
+    weights = weights / jnp.sum(weights * totals, axis=0, keepdims=True)
+    square = jnp.concatenate([weights, jnp.zeros((HD - NZ, HD), F32)], axis=0)
     columns_ref[...] = square.T
     columns = columns_ref[pl.ds(pl.multiple_of(z % 2 * 64, 64), 64), :]
     row = lax.broadcasted_iota(jnp.int32, (64, HD), 0)
-    tops = [columns[:, s : s + 1] for s in range(NZ)]
-    peak = functools.reduce(jnp.maximum, tops)
-    total = jnp.zeros((64, 1), F32)
-    summed = jnp.zeros((64, HD), F32)
+    result = jnp.zeros((64, HD), F32)
     for s in range(NZ):
-        scale = jnp.exp2(tops[s] - peak)
-        total = total + scale * columns[:, NZ + s : NZ + s + 1]
-        summed = summed + scale * parts_ref[s, 0:64, :]
-    high, middle, low = thirds(summed / total)
+        result = result + columns[:, s : s + 1] * parts_ref[s, 0:64, :]
+    high, middle, low = thirds(result)
     back = (dot(low, table) + dot(middle, table) + dot(high, table)) * SC
     position = (z * NY + y) * 8 + (row & 7)
     back = jnp.where(position < limit_ref[0], back, 0.0).astype(BF)
@@ -383,7 +362,7 @@
         return lax.ppermute(x, "ctx", OTHER_CORE)
 
     def along_y(x):
-        return [x] + [lax.ppermute(x, "ctx", Y_SHIFTS[d]) for d in range(1, NY)]
+        return [x] + [lax.ppermute(x, "ctx", Y_MOVES[d]) for d in range(1, NY)]
 
     def along_z(x, d):
         return lax.ppermute(x, "ctx", Z_SHIFTS[d]), lax.ppermute(x, "ctx", Z_SHIFTS[NZ - d])
@@ -391,7 +370,9 @@
     def with_other_core(parts):
         return parts + [swap(x) for x in parts]
 
-    mine = halve(context_k, context_v)
+    first_lane = lax.axis_index("ctx") % NC * HD
+    halves = [lax.dynamic_slice_in_dim(x, first_lane, HD, 1) for x in (context_k, context_v)]
+    mine = jnp.concatenate(halves, axis=0)
     other_question = swap(question)
     columns = along_y(join(mine, swap(context_k), swap(context_v), other_question))
     spread_rows = repeat(question, other_question)

time: 79.4 us -> 77.6 us (0.977)
  starting transfers between devices: 37.8 us -> 35.9 us
  waiting for transfers between devices: 21 us -> 22.7 us
  local copies, waits for them, and re-layouts: 2.49 us -> 1.56 us
    ppermute x2, starting transfers between devices: 7.69 us -> 4.8 us  [along_z(): lax.ppermute(x, 'ctx', Z_SHIFTS[NZ - d])]
    unnamed x16 -> x12, local copies, waits for them, and re-layouts: 2.49 us -> 0.68 us
    all_to_all x1, starting transfers between devices: 8.19 us -> 6.61 us  [on_device(): got = lax.all_to_all(spread_rows, 'ctx', 0, 0, axis_index_groups=Z_GROUPS)]
    ppermute x3, starting transfers between devices: 2.14 us -> 3.34 us  [along_y(): return [x] + [lax.ppermute(x, 'ctx', Y_MOVES[d]) for d in range(1, NY)]]
    ppermute x2, starting transfers between devices: 0.01 us -> 1.2 us  [along_z(): lax.ppermute(x, 'ctx', Z_SHIFTS[d])]
    ppermute x1, starting transfers between devices: 3.48 us -> 4.66 us  [on_device(): pieces = pieces + [swap(piece), lax.ppermute(piece, 'ctx', DIAGONAL)]]
    ppermute x5, starting transfers between devices: 6.27 us -> 5.33 us  [swap(): return lax.ppermute(x, 'ctx', OTHER_CORE)]
    dynamic_slice x0 -> x1, local copies, waits for them, and re-layouts: none -> 0.88 us  [on_device(): lax.dynamic_slice_in_dim(x, first_lane, HD, 1)]
  transfers between devices with their start and end apart: 17 -> 17, of which waited for: 6 -> 8; matrix products, arithmetic and copies ran while one was open for 0% -> 1% of each run, Pallas kernels for 16% -> 16%
where the time goes in v5:
time: 77.6 us; the launch traced here: 77.2 us
  starting transfers between devices  35.9 us (46%)
  waiting for transfers between devices  22.7 us (29%)
  Pallas kernels  15.3 us (20%)
  between operations  1.78 us (2%)
  local copies, waits for them, and re-layouts  1.56 us (2%)
    all_to_all x1, waiting for transfers between devices, on_device(): got = lax.all_to_all(spread_rows, 'ctx', 0, 0, axis_index_groups=Z_GROUPS)  7.2 us
    pallas_call x1, Pallas kernels, encode(): pl.pallas_call(encode_kernel, grid=(2,), out_shape=(jax.ShapeDtypeStruct(...  7.06 us
    all_to_all x1, starting transfers between devices, on_device(): got = lax.all_to_all(spread_rows, 'ctx', 0, 0, axis_index_groups=Z_GROUPS)  6.61 us
    all_to_all x1, starting transfers between devices, on_device(): own = lax.all_to_all(spread, 'ctx', 0, 0, axis_index_groups=CHIP_GROUPS)  6.28 us
    ppermute x2, waiting for transfers between devices, along_z(): lax.ppermute(x, 'ctx', Z_SHIFTS[d])  6.08 us
    ppermute x5, starting transfers between devices, swap(): return lax.ppermute(x, 'ctx', OTHER_CORE)  5.33 us
    ppermute x1, waiting for transfers between devices, on_device(): pieces = pieces + [swap(piece), lax.ppermute(piece, 'ctx', DIAGONAL)]  5.29 us
    ppermute x2, starting transfers between devices, along_z(): lax.ppermute(x, 'ctx', Z_SHIFTS[NZ - d])  4.8 us
  transfers between devices with their start and end apart: 17, of which 8 were waited for; matrix products, arithmetic and copies ran while one was open for 1% of the time, Pallas kernels for 16%

profile of v5, /device:TPU:1, one launch (start us, length us, event | category | flops | bytes accessed | tf_op | source)
XLA Modules:
  0.0 77.2 jit_solution(683459392491944695)
XLA Ops:
  0.6 3.3 %collective-permute-start.2 = (bf16[4,2048]{1,0:T(4,128)(2,1)}, bf16[4,2048]{1,0:T(4,128)(2,1)S(1)}, u32[]{:S(2)}, u32[]{:S(2)}) collective-permute-start(bf16[4,2048]{1,0:T(4,128)(2,1)} %own_ref.1), channel_id=1, source_target_pairs={{0,1},{1,0},{2,3},{3,2},{4,5},{5,4},{6,7},{7,6},{8,9},{9,8},{10,11... | collective-permute-start | bytes 49160 | tf_op jit(solution)/shard_map/ppermute | solution.py:362
  4.0 0.1 collective-permute-start
  4.1 0.4 collective-permute-start.1
  4.5 0.9 %constant_dynamic-slice_fusion = (bf16[256,128]{1,0:T(8,128)(2,1)S(1)}, bf16[256,128]{1,0:T(8,128)(2,1)S(1)}) fusion(bf16[256,256]{1,0:T(8,128)(2,1)} %v_ref.1, s32[]{:T(128)S(6)} %select_n.49, bf16[256,256]{1,0:T(8,128)(2,1)} %k_ref.1), kind=kLoop, calls=%fused_computation.3 | loop fusion | bytes 262148 | tf_op jit(solution)/shard_map/dynamic_slice | solution.py:374
  5.4 0.0 copy-start.2
  5.4 0.0 collective-permute-done.2.early_ref.other_ref
  5.4 0.1 collective-permute-done.k_ref
  5.5 0.2 collective-permute-done.1.v_ref
  5.7 1.1 %collective-permute-start.5 = (bf16[1024,128]{1,0:T(8,128)(2,1)S(1)}, bf16[1024,128]{1,0:T(8,128)(2,1)S(1)}, u32[]{:S(2)}, u32[]{:S(2)}) collective-permute-start(bf16[1024,128]{1,0:T(8,128)(2,1)S(1)} %join.1.refs_0_), channel_id=1, source_target_pairs={{0,6},{1,7},{2,4},{3,5},{4,2},{5,3},{6,0},{7,1},{8,14},{9,15},{10,... | collective-permute-start | bytes 786440 | tf_op jit(solution)/shard_map/ppermute | solution.py:365
  6.8 0.3 collective-permute-start.4
  7.2 1.9 %collective-permute-start.3 = (bf16[1024,128]{1,0:T(8,128)(2,1)S(1)}, bf16[1024,128]{1,0:T(8,128)(2,1)S(1)}, u32[]{:S(2)}, u32[]{:S(2)}) collective-permute-start(bf16[1024,128]{1,0:T(8,128)(2,1)S(1)} %join.1.refs_0_), channel_id=1, source_target_pairs={{0,2},{1,3},{2,0},{3,1},{4,6},{5,7},{6,4},{7,5},{8,10},{9,11},{10,... | collective-permute-start | bytes 786440 | tf_op jit(solution)/shard_map/ppermute | solution.py:365
  9.1 0.0 copy-done.2
  9.1 0.7 repeat.1
  9.8 6.6 %all-to-all-start = ((bf16[8,64,128]{2,1,0:T(8,128)(2,1)}), bf16[8,64,128]{2,1,0:T(8,128)(2,1)S(1)}, u32[]{:S(2)}, u32[]{:S(2)}) async-start(bf16[8,64,128]{2,1,0:T(8,128)(2,1)} %repeat.1), calls=%async_computation | async-start | bytes 262144 | tf_op jit(solution)/shard_map/all_to_all | solution.py:379
  16.4 0.7 copy-done.3
  17.2 7.2 %all-to-all-done.refs_3_.got_ref = bf16[8,64,128]{2,1,0:T(8,128)(2,1)S(1)} async-done(((bf16[8,64,128]{2,1,0:T(8,128)(2,1)}), bf16[8,64,128]{2,1,0:T(8,128)(2,1)S(1)}, u32[]{:S(2)}, u32[]{:S(2)}) %all-to-all-start) | async-done | bytes 131104 | tf_op jit(solution)/shard_map/all_to_all | solution.py:379
  24.4 0.0 collective-permute-done.5.refs_2_
  24.4 0.0 collective-permute-done.4.refs_1_
  24.4 0.0 collective-permute-done.3.refs_0_
  24.4 0.0 copy-start.5
  24.4 0.6 pick.1
  25.1 0.3 collective-permute-start.7
  25.4 1.2 %collective-permute-start.6 = (bf16[256,128]{1,0:T(8,128)(2,1)S(1)}, bf16[256,128]{1,0:T(8,128)(2,1)S(1)}, u32[]{:S(2)}, u32[]{:S(2)}) collective-permute-start(bf16[256,128]{1,0:T(8,128)(2,1)S(1)} %pick.1), channel_id=1, source_target_pairs={{0,8},{1,9},{2,10},{3,11},{4,12},{5,13},{6,14},{7,15},{8,16},{9,17... | collective-permute-start | bytes 196616 | tf_op jit(solution)/shard_map/ppermute | solution.py:368
  26.6 3.9 %question_pass.1 = f32[8,72,128]{2,1,0:T(8,128)} custom-call(s32[64]{0:T(128)S(1)} %copy-done.5, bf16[8,64,128]{2,1,0:T(8,128)(2,1)S(1)} %all-to-all-done.refs_3_.got_ref, bf16[1024,128]{1,0:T(8,128)(2,1)S(1)} %join.1.refs_0_, bf16[1024,128]{1,0:T(8,128)(2,1)S(1)} %get-tuple-element.11.refs_1_, bf16[1024,128]{1,0:T(8,128)(2,1)S(1)} %get-tuple-element.12.refs_2_, ...), custom_call_target="tpu_custom_call" | custom-call | flops 900000000 | bytes 2500000 | tf_op jit(solution)/shard_map/question_pass/pallas_call | solution.py:217
  30.5 3.4 %all-to-all-start.1 = ((f32[8,72,128]{2,1,0:T(8,128)}), f32[8,72,128]{2,1,0:T(8,128)S(1)}, u32[]{:S(2)}, u32[]{:S(2)}) async-start(f32[8,72,128]{2,1,0:T(8,128)} %question_pass.1), calls=%async_computation.1 | async-start | bytes 589824 | tf_op jit(solution)/shard_map/all_to_all | solution.py:384
  33.9 0.0 collective-permute-done.7
  33.9 0.0 collective-permute-done.6
  34.0 4.5 %collective-permute-start.9 = (bf16[256,128]{1,0:T(8,128)(2,1)S(1)}, bf16[256,128]{1,0:T(8,128)(2,1)S(1)}, u32[]{:S(2)}, u32[]{:S(2)}) collective-permute-start(bf16[256,128]{1,0:T(8,128)(2,1)S(1)} %select_select_fusion.1), channel_id=1, source_target_pairs={{0,40},{1,41},{2,42},{3,43},{4,44},{5,45},{6,46},{7,47},{8,48},{9,... | collective-permute-start | bytes 196616 | tf_op jit(solution)/shard_map/ppermute | solution.py:368
  38.4 0.0 collective-permute-start.8
  39.1 0.0 copy-start.4
  39.1 2.2 %collective-permute-done.9 = bf16[256,128]{1,0:T(8,128)(2,1)S(1)} collective-permute-done((bf16[256,128]{1,0:T(8,128)(2,1)S(1)}, bf16[256,128]{1,0:T(8,128)(2,1)S(1)}, u32[]{:S(2)}, u32[]{:S(2)}) %collective-permute-start.9) | collective-permute-done | bytes 65568 | tf_op jit(solution)/shard_map/ppermute | solution.py:368
  41.3 6.1 %collective-permute-done.8 = bf16[256,128]{1,0:T(8,128)(2,1)S(1)} collective-permute-done((bf16[256,128]{1,0:T(8,128)(2,1)S(1)}, bf16[256,128]{1,0:T(8,128)(2,1)S(1)}, u32[]{:S(2)}, u32[]{:S(2)}) %collective-permute-start.8) | collective-permute-done | bytes 65568 | tf_op jit(solution)/shard_map/ppermute | solution.py:368
  47.4 0.0 all-to-all-done.1.parts_ref
  47.4 1.3 %combine.1 = bf16[32,8,8,128]{3,2,1,0:T(8,128)(2,1)} custom-call(s32[1]{0:T(128)S(6)} %copy.21.limit_ref, f32[8,72,128]{2,1,0:T(8,128)S(1)} %all-to-all-done.1.parts_ref, bf16[256,128]{1,0:T(8,128)(2,1)S(1)} %select_select_fusion.refs_0_.piece_ref), custom_call_target="tpu_custom_call" | custom-call | tf_op jit(solution)/shard_map/combine/pallas_call | solution.py:255
  48.7 6.3 %all-to-all-start.2 = ((bf16[32,8,8,128]{3,2,1,0:T(8,128)(2,1)}), bf16[32,8,8,128]{3,2,1,0:T(8,128)(2,1)S(1)}, u32[]{:S(2)}, u32[]{:S(2)}) async-start(bf16[32,8,8,128]{3,2,1,0:T(8,128)(2,1)} %combine.1), calls=%async_computation.2 | async-start | bytes 1048576 | tf_op jit(solution)/shard_map/all_to_all | solution.py:391
  55.0 4.7 %collective-permute-start.12 = (bf16[256,128]{1,0:T(8,128)(2,1)S(1)}, bf16[256,128]{1,0:T(8,128)(2,1)S(1)}, u32[]{:S(2)}, u32[]{:S(2)}) collective-permute-start(bf16[256,128]{1,0:T(8,128)(2,1)S(1)} %select_select_fusion.refs_0_.piece_ref), channel_id=1, source_target_pairs={{0,3},{1,2},{2,1},{3,0},{4,7},{5,6},{6,5},{7,4},{8,11},{9,10},{10,... | collective-permute-start | bytes 196616 | tf_op jit(solution)/shard_map/ppermute | solution.py:393
  59.7 0.0 collective-permute-start.11
  59.7 0.2 collective-permute-start.10
  59.9 5.3 %collective-permute-done.12.refs_3_ = bf16[256,128]{1,0:T(8,128)(2,1)S(1)} collective-permute-done((bf16[256,128]{1,0:T(8,128)(2,1)S(1)}, bf16[256,128]{1,0:T(8,128)(2,1)S(1)}, u32[]{:S(2)}, u32[]{:S(2)}) %collective-permute-start.12) | collective-permute-done | bytes 65568 | tf_op jit(solution)/shard_map/ppermute | solution.py:393
  65.2 0.0 collective-permute-done.11.refs_2_
  65.2 0.9 %collective-permute-done.10.refs_1_ = bf16[256,128]{1,0:T(8,128)(2,1)S(1)} collective-permute-done((bf16[256,128]{1,0:T(8,128)(2,1)S(1)}, bf16[256,128]{1,0:T(8,128)(2,1)S(1)}, u32[]{:S(2)}, u32[]{:S(2)}) %collective-permute-start.10) | collective-permute-done | bytes 65568 | tf_op jit(solution)/shard_map/ppermute | solution.py:392
  66.1 0.0 copy-done
  66.1 7.1 %encode.1 = (bf16[256,2048]{1,0:T(8,128)(2,1)}, bf16[256,256]{1,0:T(8,128)(2,1)}, bf16[256,256]{1,0:T(8,128)(2,1)}, f32[8,128]{1,0:T(8,128)S(1)}) custom-call(s32[64]{0:T(128)S(1)} %copy-done.3, s32[64]{0:T(128)S(1)} %copy-done.5, bf16[256,2048]{1,0:T(8,128)(2,1)S(1)} %copy-done.4, bf16[256,256]{1,0:T(8,128)(2,1)S(1)} %copy-done, ...), custom_call_target="tpu_custom_call" | custom-call | flops 1100000000 | bytes 3500000 | tf_op jit(solution)/shard_map/encode/pallas_call | solution.py:310
  73.1 0.0 all-to-all-done.2.refs_0_
  73.1 1.5 %collective-permute-start.13 = (bf16[32,8,8,128]{3,2,1,0:T(8,128)(2,1)S(1)}, bf16[32,8,8,128]{3,2,1,0:T(8,128)(2,1)S(1)}, u32[]{:S(2)}, u32[]{:S(2)}) collective-permute-start(bf16[32,8,8,128]{3,2,1,0:T(8,128)(2,1)S(1)} %gate.3.part_ref), channel_id=1, source_target_pairs={{0,1},{1,0},{2,3},{3,2},{4,5},{5,4},{6,7},{7,6},{8,9},{9,8},{10,11... | collective-permute-start | bytes 1572872 | tf_op jit(solution)/shard_map/ppermute | solution.py:362
  74.6 0.8 %assemble.2.refs_0_ = bf16[32,8,2048]{2,1,0:T(8,128)(2,1)} custom-call(bf16[32,8,8,128]{3,2,1,0:T(8,128)(2,1)S(1)} %gate.3.part_ref), custom_call_target="tpu_custom_call" | custom-call | tf_op jit(solution)/shard_map/assemble/pallas_call | solution.py:346
  75.5 0.7 collective-permute-done.13.part_ref
  76.2 0.8 %assemble.3 = bf16[32,8,2048]{2,1,0:T(8,128)(2,1)} custom-call(bf16[32,8,8,128]{3,2,1,0:T(8,128)(2,1)S(1)} %collective-permute-done.13.part_ref, bf16[32,8,2048]{2,1,0:T(8,128)(2,1)} %assemble.2.refs_0_), custom_call_target="tpu_custom_call", output_to_operand_aliasing={{}: (1, {})} | custom-call | tf_op jit(solution)/shard_map/assemble/pallas_call | solution.py:346
  (12 shorter events, 0.1 us)
Async XLA Ops:
  0.6 4.8 %collective-permute-start.2 = (bf16[4,2048]{1,0:T(4,128)(2,1)}, bf16[4,2048]{1,0:T(4,128)(2,1)S(1)}, u32[]{:S(2)}, u32[]{:S(2)}) collective-permute-start(bf16[4,2048]{1,0:T(4,128)(2,1)} %own_ref.1), channel_id=1, source_target_pairs={{0,1},{1,0},{2,3},{3,2},{4,5},{5,4},{6,7},{7,6},{8,9},{9,8},{10,11... | collective-permute-start | bytes 49160 | tf_op jit(solution)/shard_map/ppermute | solution.py:362
  4.0 1.6 %collective-permute-start = (bf16[256,256]{1,0:T(8,128)(2,1)}, bf16[256,256]{1,0:T(8,128)(2,1)S(1)}, u32[]{:S(2)}, u32[]{:S(2)}) collective-permute-start(bf16[256,256]{1,0:T(8,128)(2,1)} %k_ref.1), channel_id=1, source_target_pairs={{0,1},{1,0},{2,3},{3,2},{4,5},{5,4},{6,7},{7,6},{8,9},{9,8},{10,11... | collective-permute-start | bytes 393224 | tf_op jit(solution)/shard_map/ppermute | solution.py:362
  4.1 1.6 %collective-permute-start.1 = (bf16[256,256]{1,0:T(8,128)(2,1)}, bf16[256,256]{1,0:T(8,128)(2,1)S(1)}, u32[]{:S(2)}, u32[]{:S(2)}) collective-permute-start(bf16[256,256]{1,0:T(8,128)(2,1)} %v_ref.1), channel_id=1, source_target_pairs={{0,1},{1,0},{2,3},{3,2},{4,5},{5,4},{6,7},{7,6},{8,9},{9,8},{10,11... | collective-permute-start | bytes 393224 | tf_op jit(solution)/shard_map/ppermute | solution.py:362
  5.4 3.7 %copy-start.2 = (bf16[4,2048]{1,0:T(4,128)(2,1)S(1)}, bf16[4,2048]{1,0:T(4,128)(2,1)}, u32[]{:S(2)}) copy-start(bf16[4,2048]{1,0:T(4,128)(2,1)} %own_ref.1) | copy-start | bytes 49156
  5.7 18.7 %collective-permute-start.5 = (bf16[1024,128]{1,0:T(8,128)(2,1)S(1)}, bf16[1024,128]{1,0:T(8,128)(2,1)S(1)}, u32[]{:S(2)}, u32[]{:S(2)}) collective-permute-start(bf16[1024,128]{1,0:T(8,128)(2,1)S(1)} %join.1.refs_0_), channel_id=1, source_target_pairs={{0,6},{1,7},{2,4},{3,5},{4,2},{5,3},{6,0},{7,1},{8,14},{9,15},{10,... | collective-permute-start | bytes 786440 | tf_op jit(solution)/shard_map/ppermute | solution.py:365
  6.8 17.6 %collective-permute-start.4 = (bf16[1024,128]{1,0:T(8,128)(2,1)S(1)}, bf16[1024,128]{1,0:T(8,128)(2,1)S(1)}, u32[]{:S(2)}, u32[]{:S(2)}) collective-permute-start(bf16[1024,128]{1,0:T(8,128)(2,1)S(1)} %join.1.refs_0_), channel_id=1, source_target_pairs={{0,4},{1,5},{2,6},{3,7},{4,0},{5,1},{6,2},{7,3},{8,12},{9,13},{10,... | collective-permute-start | bytes 786440 | tf_op jit(solution)/shard_map/ppermute | solution.py:365
  7.2 17.2 %collective-permute-start.3 = (bf16[1024,128]{1,0:T(8,128)(2,1)S(1)}, bf16[1024,128]{1,0:T(8,128)(2,1)S(1)}, u32[]{:S(2)}, u32[]{:S(2)}) collective-permute-start(bf16[1024,128]{1,0:T(8,128)(2,1)S(1)} %join.1.refs_0_), channel_id=1, source_target_pairs={{0,2},{1,3},{2,0},{3,1},{4,6},{5,7},{6,4},{7,5},{8,10},{9,11},{10,... | collective-permute-start | bytes 786440 | tf_op jit(solution)/shard_map/ppermute | solution.py:365
  9.8 14.6 %all-to-all-start = ((bf16[8,64,128]{2,1,0:T(8,128)(2,1)}), bf16[8,64,128]{2,1,0:T(8,128)(2,1)S(1)}, u32[]{:S(2)}, u32[]{:S(2)}) async-start(bf16[8,64,128]{2,1,0:T(8,128)(2,1)} %repeat.1), calls=%async_computation | async-start | bytes 262144 | tf_op jit(solution)/shard_map/all_to_all | solution.py:379
  16.4 0.7 copy-start.3
  24.4 2.2 %copy-start.5 = (s32[64]{0:T(128)S(1)}, s32[64]{0:T(128)}, u32[]{:S(2)}) copy-start(s32[64]{0:T(128)} %lengths_ref.3) | copy-start | bytes 772
  25.1 8.9 %collective-permute-start.7 = (bf16[256,128]{1,0:T(8,128)(2,1)S(1)}, bf16[256,128]{1,0:T(8,128)(2,1)S(1)}, u32[]{:S(2)}, u32[]{:S(2)}) collective-permute-start(bf16[256,128]{1,0:T(8,128)(2,1)S(1)} %pick.1), channel_id=1, source_target_pairs={{0,56},{1,57},{2,58},{3,59},{4,60},{5,61},{6,62},{7,63},{8,0},{9,1... | collective-permute-start | bytes 196616 | tf_op jit(solution)/shard_map/ppermute | solution.py:368
  25.4 8.5 %collective-permute-start.6 = (bf16[256,128]{1,0:T(8,128)(2,1)S(1)}, bf16[256,128]{1,0:T(8,128)(2,1)S(1)}, u32[]{:S(2)}, u32[]{:S(2)}) collective-permute-start(bf16[256,128]{1,0:T(8,128)(2,1)S(1)} %pick.1), channel_id=1, source_target_pairs={{0,8},{1,9},{2,10},{3,11},{4,12},{5,13},{6,14},{7,15},{8,16},{9,17... | collective-permute-start | bytes 196616 | tf_op jit(solution)/shard_map/ppermute | solution.py:368
  30.5 16.9 %all-to-all-start.1 = ((f32[8,72,128]{2,1,0:T(8,128)}), f32[8,72,128]{2,1,0:T(8,128)S(1)}, u32[]{:S(2)}, u32[]{:S(2)}) async-start(f32[8,72,128]{2,1,0:T(8,128)} %question_pass.1), calls=%async_computation.1 | async-start | bytes 589824 | tf_op jit(solution)/shard_map/all_to_all | solution.py:384
  34.0 7.3 %collective-permute-start.9 = (bf16[256,128]{1,0:T(8,128)(2,1)S(1)}, bf16[256,128]{1,0:T(8,128)(2,1)S(1)}, u32[]{:S(2)}, u32[]{:S(2)}) collective-permute-start(bf16[256,128]{1,0:T(8,128)(2,1)S(1)} %select_select_fusion.1), channel_id=1, source_target_pairs={{0,40},{1,41},{2,42},{3,43},{4,44},{5,45},{6,46},{7,47},{8,48},{9,... | collective-permute-start | bytes 196616 | tf_op jit(solution)/shard_map/ppermute | solution.py:368
  38.4 9.0 %collective-permute-start.8 = (bf16[256,128]{1,0:T(8,128)(2,1)S(1)}, bf16[256,128]{1,0:T(8,128)(2,1)S(1)}, u32[]{:S(2)}, u32[]{:S(2)}) collective-permute-start(bf16[256,128]{1,0:T(8,128)(2,1)S(1)} %select_select_fusion.1), channel_id=1, source_target_pairs={{0,24},{1,25},{2,26},{3,27},{4,28},{5,29},{6,30},{7,31},{8,32},{9,... | collective-permute-start | bytes 196616 | tf_op jit(solution)/shard_map/ppermute | solution.py:368
  39.1 27.0 %copy-start.4 = (bf16[256,2048]{1,0:T(8,128)(2,1)S(1)}, bf16[256,2048]{1,0:T(8,128)(2,1)}, u32[]{:S(2)}) copy-start(bf16[256,2048]{1,0:T(8,128)(2,1)} %q_ref.1) | copy-start | bytes 3145732
  48.7 17.3 %copy-start = (bf16[256,256]{1,0:T(8,128)(2,1)S(1)}, bf16[256,256]{1,0:T(8,128)(2,1)}, u32[]{:S(2)}) copy-start(bf16[256,256]{1,0:T(8,128)(2,1)} %k_ref.1) | copy-start | bytes 393220
  48.7 17.3 %copy-start.1 = (bf16[256,256]{1,0:T(8,128)(2,1)S(1)}, bf16[256,256]{1,0:T(8,128)(2,1)}, u32[]{:S(2)}) copy-start(bf16[256,256]{1,0:T(8,128)(2,1)} %v_ref.1) | copy-start | bytes 393220
  48.7 24.4 %all-to-all-start.2 = ((bf16[32,8,8,128]{3,2,1,0:T(8,128)(2,1)}), bf16[32,8,8,128]{3,2,1,0:T(8,128)(2,1)S(1)}, u32[]{:S(2)}, u32[]{:S(2)}) async-start(bf16[32,8,8,128]{3,2,1,0:T(8,128)(2,1)} %combine.1), calls=%async_computation.2 | async-start | bytes 1048576 | tf_op jit(solution)/shard_map/all_to_all | solution.py:391
  55.0 10.2 %collective-permute-start.12 = (bf16[256,128]{1,0:T(8,128)(2,1)S(1)}, bf16[256,128]{1,0:T(8,128)(2,1)S(1)}, u32[]{:S(2)}, u32[]{:S(2)}) collective-permute-start(bf16[256,128]{1,0:T(8,128)(2,1)S(1)} %select_select_fusion.refs_0_.piece_ref), channel_id=1, source_target_pairs={{0,3},{1,2},{2,1},{3,0},{4,7},{5,6},{6,5},{7,4},{8,11},{9,10},{10,... | collective-permute-start | bytes 196616 | tf_op jit(solution)/shard_map/ppermute | solution.py:393
  59.7 5.5 %collective-permute-start.11 = (bf16[256,128]{1,0:T(8,128)(2,1)S(1)}, bf16[256,128]{1,0:T(8,128)(2,1)S(1)}, u32[]{:S(2)}, u32[]{:S(2)}) collective-permute-start(bf16[256,128]{1,0:T(8,128)(2,1)S(1)} %select_select_fusion.refs_0_.piece_ref), channel_id=1, source_target_pairs={{0,1},{1,0},{2,3},{3,2},{4,5},{5,4},{6,7},{7,6},{8,9},{9,8},{10,11... | collective-permute-start | bytes 196616 | tf_op jit(solution)/shard_map/ppermute | solution.py:362
  59.7 6.4 %collective-permute-start.10 = (bf16[256,128]{1,0:T(8,128)(2,1)S(1)}, bf16[256,128]{1,0:T(8,128)(2,1)S(1)}, u32[]{:S(2)}, u32[]{:S(2)}) collective-permute-start(bf16[256,128]{1,0:T(8,128)(2,1)S(1)} %select_select_fusion.refs_0_.piece_ref), channel_id=1, source_target_pairs={{0,2},{1,3},{2,0},{3,1},{4,6},{5,7},{6,4},{7,5},{8,10},{9,11},{10,... | collective-permute-start | bytes 196616 | tf_op jit(solution)/shard_map/ppermute | solution.py:392
  73.1 3.0 %collective-permute-start.13 = (bf16[32,8,8,128]{3,2,1,0:T(8,128)(2,1)S(1)}, bf16[32,8,8,128]{3,2,1,0:T(8,128)(2,1)S(1)}, u32[]{:S(2)}, u32[]{:S(2)}) collective-permute-start(bf16[32,8,8,128]{3,2,1,0:T(8,128)(2,1)S(1)} %gate.3.part_ref), channel_id=1, source_target_pairs={{0,1},{1,0},{2,3},{3,2},{4,5},{5,4},{6,7},{7,6},{8,9},{9,8},{10,11... | collective-permute-start | bytes 1572872 | tf_op jit(solution)/shard_map/ppermute | solution.py:362

commit v6 on v5

--- a/solution.py
+++ b/solution.py
@@ -34,8 +34,9 @@
     ]
 
 
-Z_GROUPS = [[index_of(z, y, c) for z in range(NZ)] for y in range(NY) for c in range(NC)]
-CHIP_GROUPS = [[index_of(z, y, c) for z in range(NZ) for y in range(NY)] for c in range(NC)]
+Z_ORDER = (0, 2, 4, 6, 1, 3, 5, 7)
+Z_GROUPS = [[index_of(z, y, c) for z in Z_ORDER] for y in range(NY) for c in range(NC)]
+CHIP_GROUPS = [[index_of(z, y, c) for y in range(NY) for z in Z_ORDER] for c in range(NC)]
 OTHER_CORE = permutation(lambda z, y, c: (z, y, 1 - c))
 Y_PARTNER = permutation(lambda z, y, c: (z, y ^ 1, c))
 DIAGONAL = permutation(lambda z, y, c: (z, y ^ 1, 1 - c))
@@ -230,14 +231,15 @@
 def combine_kernel(limit_ref, parts_ref, piece_ref, send_ref, columns_ref):
     z, y, c = coordinates()
     table = sign_table()
-    tops = [parts_ref[s, pl.ds(64 + z // 2, 1), :] for s in range(NZ)]
-    totals = [parts_ref[s, pl.ds(68 + z // 2, 1), :] for s in range(NZ)]
+    rank = z % 2 * 4 + z // 2
+    tops = [parts_ref[s, pl.ds(64 + rank // 2, 1), :] for s in range(NZ)]
+    totals = [parts_ref[s, pl.ds(68 + rank // 2, 1), :] for s in range(NZ)]
     tops, totals = jnp.concatenate(tops, axis=0), jnp.concatenate(totals, axis=0)
     weights = jnp.exp2(tops - jnp.max(tops, axis=0, keepdims=True))
     weights = weights / jnp.sum(weights * totals, axis=0, keepdims=True)
     square = jnp.concatenate([weights, jnp.zeros((HD - NZ, HD), F32)], axis=0)
     columns_ref[...] = square.T
-    columns = columns_ref[pl.ds(pl.multiple_of(z % 2 * 64, 64), 64), :]
+    columns = columns_ref[pl.ds(pl.multiple_of(rank % 2 * 64, 64), 64), :]
     row = lax.broadcasted_iota(jnp.int32, (64, HD), 0)
     result = jnp.zeros((64, HD), F32)
     for s in range(NZ):
@@ -245,8 +247,8 @@
     high, middle, low = thirds(result)
     back = (dot(low, table) + dot(middle, table) + dot(high, table)) * SC
     position = (z * NY + y) * 8 + (row & 7)
-    back = jnp.where(position < limit_ref[0], back, 0.0).astype(BF)
-    back = back.astype(F32).reshape(8, 8, HD).astype(BF)
+    back = jnp.where(position < limit_ref[0], back, 0.0)
+    back = jnp.concatenate([back[8 * j : 8 * j + 8] for j in range(8)], axis=1).astype(BF)
     for i in range(NZ * NY):
         send_ref[i] = back
 
@@ -254,7 +256,7 @@
 def combine(limit, parts, piece):
     return pl.pallas_call(
         combine_kernel,
-        out_shape=jax.ShapeDtypeStruct((NZ * NY, 8, 8, HD), BF),
+        out_shape=jax.ShapeDtypeStruct((NZ * NY, 8, 1024), BF),
         in_specs=[SMEM, VMEM, pl.BlockSpec(memory_space=pl.ANY)],
         out_specs=VMEM,
         scratch_shapes=[pltpu.VMEM((HD, HD), F32)],
@@ -330,11 +332,13 @@
 def assemble_kernel(part_ref, *refs, own):
     out_ref, sems = refs[-2:]
     c = coordinates()[2]
-    head = c if own else 1 - c
+    lanes = pl.ds(pl.multiple_of(1024 * (c if own else 1 - c), 1024), 1024)
     copies = []
-    for j in range(8):
-        lanes = pl.ds(pl.multiple_of(HD * (8 * head + j), HD), HD)
-        copies.append(pltpu.make_async_copy(part_ref.at[:, j], out_ref.at[:, :, lanes], sems.at[j]))
+    for y in range(NY):
+        for odd in range(2):
+            source = part_ref.at[pl.ds(NZ * y + 4 * odd, 4)]
+            target = out_ref.at[:, odd, y, :, lanes]
+            copies.append(pltpu.make_async_copy(source, target, sems.at[y, odd]))
     for copy in copies:
         copy.start()
     for copy in copies:
@@ -345,10 +349,10 @@
     anywhere = pl.BlockSpec(memory_space=pl.ANY)
     return pl.pallas_call(
         functools.partial(assemble_kernel, own=out is None),
-        out_shape=jax.ShapeDtypeStruct((32, 8, 2048), BF),
+        out_shape=jax.ShapeDtypeStruct((NZ // 2, 2, NY, 8, 2048), BF),
         in_specs=[anywhere] * (1 if out is None else 2),
         out_specs=anywhere,
-        scratch_shapes=[pltpu.SemaphoreType.DMA((8,))],
+        scratch_shapes=[pltpu.SemaphoreType.DMA((NY, 2))],
         input_output_aliases={} if out is None else {1: 0},
         compiler_params=SMALL,
         name="assemble",

time: 77.6 us -> 75.6 us (0.974)
  waiting for transfers between devices: 22.7 us -> 21 us
    ppermute x1, waiting for transfers between devices: 5.29 us -> 3.69 us  [on_device(): pieces = pieces + [swap(piece), lax.ppermute(piece, 'ctx', DIAGONAL)]]
    ppermute x2, starting transfers between devices: 4.8 us -> 5.88 us  [along_z(): lax.ppermute(x, 'ctx', Z_SHIFTS[NZ - d])]
    all_to_all x1, waiting for transfers between devices: 7.2 us -> 6.2 us  [on_device(): got = lax.all_to_all(spread_rows, 'ctx', 0, 0, axis_index_groups=Z_GROUPS)]
    ppermute x2, starting transfers between devices: 1.2 us -> 0.3 us  [along_z(): lax.ppermute(x, 'ctx', Z_SHIFTS[d])]
    all_to_all x1, starting transfers between devices: 6.28 us -> 5.5 us  [on_device(): own = lax.all_to_all(spread, 'ctx', 0, 0, axis_index_groups=CHIP_GROUPS)]
  transfers between devices with their start and end apart: 17 -> 17, of which waited for: 8 -> 8; matrix products, arithmetic and copies ran while one was open for 1% -> 1% of each run, Pallas kernels for 16% -> 17%
where the time goes in v6:
time: 75.6 us; the launch traced here: 75 us
  starting transfers between devices  35.3 us (47%)
  waiting for transfers between devices  21 us (28%)
  Pallas kernels  15.3 us (20%)
  between operations  1.77 us (2%)
  local copies, waits for them, and re-layouts  1.56 us (2%)
    pallas_call x1, Pallas kernels, encode(): pl.pallas_call(encode_kernel, grid=(2,), out_shape=(jax.ShapeDtypeStruct(...  7.05 us
    ppermute x2, waiting for transfers between devices, along_z(): lax.ppermute(x, 'ctx', Z_SHIFTS[d])  6.78 us
    all_to_all x1, starting transfers between devices, on_device(): got = lax.all_to_all(spread_rows, 'ctx', 0, 0, axis_index_groups=Z_GROUPS)  6.61 us
    all_to_all x1, waiting for transfers between devices, on_device(): got = lax.all_to_all(spread_rows, 'ctx', 0, 0, axis_index_groups=Z_GROUPS)  6.2 us
    ppermute x2, starting transfers between devices, along_z(): lax.ppermute(x, 'ctx', Z_SHIFTS[NZ - d])  5.88 us
    all_to_all x1, starting transfers between devices, on_device(): own = lax.all_to_all(spread, 'ctx', 0, 0, axis_index_groups=CHIP_GROUPS)  5.5 us
    ppermute x5, starting transfers between devices, swap(): return lax.ppermute(x, 'ctx', OTHER_CORE)  4.96 us
    ppermute x1, starting transfers between devices, on_device(): pieces = pieces + [swap(piece), lax.ppermute(piece, 'ctx', DIAGONAL)]  4.7 us
  transfers between devices with their start and end apart: 17, of which 8 were waited for; matrix products, arithmetic and copies ran while one was open for 1% of the time, Pallas kernels for 17%

profile of v6, /device:TPU:1, one launch (start us, length us, event | category | flops | bytes accessed | tf_op | source)
XLA Modules:
  0.0 75.0 jit_solution(15831534011281163157)
XLA Ops:
  0.6 3.3 %collective-permute-start.2 = (bf16[4,2048]{1,0:T(4,128)(2,1)}, bf16[4,2048]{1,0:T(4,128)(2,1)S(1)}, u32[]{:S(2)}, u32[]{:S(2)}) collective-permute-start(bf16[4,2048]{1,0:T(4,128)(2,1)} %own_ref.1), channel_id=1, source_target_pairs={{0,1},{1,0},{2,3},{3,2},{4,5},{5,4},{6,7},{7,6},{8,9},{9,8},{10,11... | collective-permute-start | bytes 49160 | tf_op jit(solution)/shard_map/ppermute | solution.py:366
  4.0 0.1 collective-permute-start
  4.1 0.4 collective-permute-start.1
  4.5 0.9 %constant_dynamic-slice_fusion = (bf16[256,128]{1,0:T(8,128)(2,1)S(1)}, bf16[256,128]{1,0:T(8,128)(2,1)S(1)}) fusion(bf16[256,256]{1,0:T(8,128)(2,1)} %v_ref.1, s32[]{:T(128)S(6)} %select_n.49, bf16[256,256]{1,0:T(8,128)(2,1)} %k_ref.1), kind=kLoop, calls=%fused_computation.3 | loop fusion | bytes 262148 | tf_op jit(solution)/shard_map/dynamic_slice | solution.py:378
  5.4 0.0 copy-start.2
  5.4 0.0 collective-permute-done.2.early_ref.other_ref
  5.4 0.1 collective-permute-done.k_ref
  5.5 0.2 collective-permute-done.1.v_ref
  5.7 1.1 %collective-permute-start.5 = (bf16[1024,128]{1,0:T(8,128)(2,1)S(1)}, bf16[1024,128]{1,0:T(8,128)(2,1)S(1)}, u32[]{:S(2)}, u32[]{:S(2)}) collective-permute-start(bf16[1024,128]{1,0:T(8,128)(2,1)S(1)} %join.1.refs_0_), channel_id=1, source_target_pairs={{0,6},{1,7},{2,4},{3,5},{4,2},{5,3},{6,0},{7,1},{8,14},{9,15},{10,... | collective-permute-start | bytes 786440 | tf_op jit(solution)/shard_map/ppermute | solution.py:369
  6.8 0.3 collective-permute-start.4
  7.2 1.9 %collective-permute-start.3 = (bf16[1024,128]{1,0:T(8,128)(2,1)S(1)}, bf16[1024,128]{1,0:T(8,128)(2,1)S(1)}, u32[]{:S(2)}, u32[]{:S(2)}) collective-permute-start(bf16[1024,128]{1,0:T(8,128)(2,1)S(1)} %join.1.refs_0_), channel_id=1, source_target_pairs={{0,2},{1,3},{2,0},{3,1},{4,6},{5,7},{6,4},{7,5},{8,10},{9,11},{10,... | collective-permute-start | bytes 786440 | tf_op jit(solution)/shard_map/ppermute | solution.py:369
  9.1 0.0 copy-done.2
  9.1 0.7 repeat.1
  9.8 6.6 %all-to-all-start = ((bf16[8,64,128]{2,1,0:T(8,128)(2,1)}), bf16[8,64,128]{2,1,0:T(8,128)(2,1)S(1)}, u32[]{:S(2)}, u32[]{:S(2)}) async-start(bf16[8,64,128]{2,1,0:T(8,128)(2,1)} %repeat.1), calls=%async_computation | async-start | bytes 262144 | tf_op jit(solution)/shard_map/all_to_all | solution.py:383
  16.4 0.7 copy-done.3
  17.2 6.2 %all-to-all-done.refs_3_.got_ref = bf16[8,64,128]{2,1,0:T(8,128)(2,1)S(1)} async-done(((bf16[8,64,128]{2,1,0:T(8,128)(2,1)}), bf16[8,64,128]{2,1,0:T(8,128)(2,1)S(1)}, u32[]{:S(2)}, u32[]{:S(2)}) %all-to-all-start) | async-done | bytes 131104 | tf_op jit(solution)/shard_map/all_to_all | solution.py:383
  23.4 0.0 collective-permute-done.5.refs_2_
  23.4 0.0 collective-permute-done.4.refs_1_
  23.4 0.0 collective-permute-done.3.refs_0_
  23.4 0.0 copy-start.5
  23.5 0.6 pick.1
  24.1 1.3 %collective-permute-start.7 = (bf16[256,128]{1,0:T(8,128)(2,1)S(1)}, bf16[256,128]{1,0:T(8,128)(2,1)S(1)}, u32[]{:S(2)}, u32[]{:S(2)}) collective-permute-start(bf16[256,128]{1,0:T(8,128)(2,1)S(1)} %pick.1), channel_id=1, source_target_pairs={{0,56},{1,57},{2,58},{3,59},{4,60},{5,61},{6,62},{7,63},{8,0},{9,1... | collective-permute-start | bytes 196616 | tf_op jit(solution)/shard_map/ppermute | solution.py:372
  25.4 0.3 collective-permute-start.6
  25.7 3.9 %question_pass.1 = f32[8,72,128]{2,1,0:T(8,128)} custom-call(s32[64]{0:T(128)S(1)} %copy-done.5, bf16[8,64,128]{2,1,0:T(8,128)(2,1)S(1)} %all-to-all-done.refs_3_.got_ref, bf16[1024,128]{1,0:T(8,128)(2,1)S(1)} %join.1.refs_0_, bf16[1024,128]{1,0:T(8,128)(2,1)S(1)} %get-tuple-element.11.refs_1_, bf16[1024,128]{1,0:T(8,128)(2,1)S(1)} %get-tuple-element.12.refs_2_, ...), custom_call_target="tpu_custom_call" | custom-call | flops 900000000 | bytes 2500000 | tf_op jit(solution)/shard_map/question_pass/pallas_call | solution.py:218
  29.6 3.8 %all-to-all-start.1 = ((f32[8,72,128]{2,1,0:T(8,128)}), f32[8,72,128]{2,1,0:T(8,128)S(1)}, u32[]{:S(2)}, u32[]{:S(2)}) async-start(f32[8,72,128]{2,1,0:T(8,128)} %question_pass.1), calls=%async_computation.1 | async-start | bytes 589824 | tf_op jit(solution)/shard_map/all_to_all | solution.py:388
  33.4 0.0 collective-permute-done.7
  33.4 0.0 collective-permute-done.6
  33.4 4.5 %collective-permute-start.9 = (bf16[256,128]{1,0:T(8,128)(2,1)S(1)}, bf16[256,128]{1,0:T(8,128)(2,1)S(1)}, u32[]{:S(2)}, u32[]{:S(2)}) collective-permute-start(bf16[256,128]{1,0:T(8,128)(2,1)S(1)} %select_select_fusion.1), channel_id=1, source_target_pairs={{0,40},{1,41},{2,42},{3,43},{4,44},{5,45},{6,46},{7,47},{8,48},{9,... | collective-permute-start | bytes 196616 | tf_op jit(solution)/shard_map/ppermute | solution.py:372
  38.0 0.0 collective-permute-start.8
  38.6 0.0 copy-start.4
  38.6 1.9 %collective-permute-done.9 = bf16[256,128]{1,0:T(8,128)(2,1)S(1)} collective-permute-done((bf16[256,128]{1,0:T(8,128)(2,1)S(1)}, bf16[256,128]{1,0:T(8,128)(2,1)S(1)}, u32[]{:S(2)}, u32[]{:S(2)}) %collective-permute-start.9) | collective-permute-done | bytes 65568 | tf_op jit(solution)/shard_map/ppermute | solution.py:372
  40.5 6.8 %collective-permute-done.8 = bf16[256,128]{1,0:T(8,128)(2,1)S(1)} collective-permute-done((bf16[256,128]{1,0:T(8,128)(2,1)S(1)}, bf16[256,128]{1,0:T(8,128)(2,1)S(1)}, u32[]{:S(2)}, u32[]{:S(2)}) %collective-permute-start.8) | collective-permute-done | bytes 65568 | tf_op jit(solution)/shard_map/ppermute | solution.py:372
  47.3 0.0 all-to-all-done.1.parts_ref
  47.3 1.3 %combine.1 = bf16[32,8,1024]{2,1,0:T(8,128)(2,1)} custom-call(s32[1]{0:T(128)S(6)} %copy.21.limit_ref, f32[8,72,128]{2,1,0:T(8,128)S(1)} %all-to-all-done.1.parts_ref, bf16[256,128]{1,0:T(8,128)(2,1)S(1)} %select_select_fusion.refs_0_.piece_ref), custom_call_target="tpu_custom_call" | custom-call | tf_op jit(solution)/shard_map/combine/pallas_call | solution.py:257
  48.7 5.5 %all-to-all-start.2 = ((bf16[32,8,1024]{2,1,0:T(8,128)(2,1)}), bf16[32,8,1024]{2,1,0:T(8,128)(2,1)S(1)}, u32[]{:S(2)}, u32[]{:S(2)}) async-start(bf16[32,8,1024]{2,1,0:T(8,128)(2,1)} %combine.1), calls=%async_computation.2 | async-start | bytes 1048576 | tf_op jit(solution)/shard_map/all_to_all | solution.py:395
  54.2 4.7 %collective-permute-start.12 = (bf16[256,128]{1,0:T(8,128)(2,1)S(1)}, bf16[256,128]{1,0:T(8,128)(2,1)S(1)}, u32[]{:S(2)}, u32[]{:S(2)}) collective-permute-start(bf16[256,128]{1,0:T(8,128)(2,1)S(1)} %select_select_fusion.refs_0_.piece_ref), channel_id=1, source_target_pairs={{0,3},{1,2},{2,1},{3,0},{4,7},{5,6},{6,5},{7,4},{8,11},{9,10},{10,... | collective-permute-start | bytes 196616 | tf_op jit(solution)/shard_map/ppermute | solution.py:397
  58.9 0.0 collective-permute-start.11
  58.9 0.2 collective-permute-start.10
  59.1 3.7 %collective-permute-done.12.refs_3_ = bf16[256,128]{1,0:T(8,128)(2,1)S(1)} collective-permute-done((bf16[256,128]{1,0:T(8,128)(2,1)S(1)}, bf16[256,128]{1,0:T(8,128)(2,1)S(1)}, u32[]{:S(2)}, u32[]{:S(2)}) %collective-permute-start.12) | collective-permute-done | bytes 65568 | tf_op jit(solution)/shard_map/ppermute | solution.py:397
  62.8 0.0 collective-permute-done.11.refs_2_
  62.8 1.5 %collective-permute-done.10.refs_1_ = bf16[256,128]{1,0:T(8,128)(2,1)S(1)} collective-permute-done((bf16[256,128]{1,0:T(8,128)(2,1)S(1)}, bf16[256,128]{1,0:T(8,128)(2,1)S(1)}, u32[]{:S(2)}, u32[]{:S(2)}) %collective-permute-start.10) | collective-permute-done | bytes 65568 | tf_op jit(solution)/shard_map/ppermute | solution.py:396
  64.2 0.0 copy-done
  64.3 7.1 %encode.1 = (bf16[256,2048]{1,0:T(8,128)(2,1)}, bf16[256,256]{1,0:T(8,128)(2,1)}, bf16[256,256]{1,0:T(8,128)(2,1)}, f32[8,128]{1,0:T(8,128)S(1)}) custom-call(s32[64]{0:T(128)S(1)} %copy-done.3, s32[64]{0:T(128)S(1)} %copy-done.5, bf16[256,2048]{1,0:T(8,128)(2,1)S(1)} %copy-done.4, bf16[256,256]{1,0:T(8,128)(2,1)S(1)} %copy-done, ...), custom_call_target="tpu_custom_call" | custom-call | flops 1100000000 | bytes 3500000 | tf_op jit(solution)/shard_map/encode/pallas_call | solution.py:312
  71.3 0.0 all-to-all-done.2.refs_0_
  71.3 1.1 %collective-permute-start.13 = (bf16[32,8,1024]{2,1,0:T(8,128)(2,1)S(1)}, bf16[32,8,1024]{2,1,0:T(8,128)(2,1)S(1)}, u32[]{:S(2)}, u32[]{:S(2)}) collective-permute-start(bf16[32,8,1024]{2,1,0:T(8,128)(2,1)S(1)} %gate.3.part_ref), channel_id=1, source_target_pairs={{0,1},{1,0},{2,3},{3,2},{4,5},{5,4},{6,7},{7,6},{8,9},{9,8},{10,11... | collective-permute-start | bytes 1572872 | tf_op jit(solution)/shard_map/ppermute | solution.py:366
  72.4 0.8 %assemble.2.refs_0_ = bf16[4,2,4,8,2048]{4,3,2,1,0:T(8,128)(2,1)} custom-call(bf16[32,8,1024]{2,1,0:T(8,128)(2,1)S(1)} %gate.3.part_ref), custom_call_target="tpu_custom_call" | custom-call | tf_op jit(solution)/shard_map/assemble/pallas_call | solution.py:350
  73.3 0.7 collective-permute-done.13.part_ref
  74.0 0.8 %assemble.3 = bf16[4,2,4,8,2048]{4,3,2,1,0:T(8,128)(2,1)} custom-call(bf16[32,8,1024]{2,1,0:T(8,128)(2,1)S(1)} %collective-permute-done.13.part_ref, bf16[4,2,4,8,2048]{4,3,2,1,0:T(8,128)(2,1)} %assemble.2.refs_0_), custom_call_target="tpu_custom_call", output_to_operand_aliasing={{}: (1, {})} | custom-call | tf_op jit(solution)/shard_map/assemble/pallas_call | solution.py:350
  (12 shorter events, 0.1 us)
Async XLA Ops:
  0.6 4.8 %collective-permute-start.2 = (bf16[4,2048]{1,0:T(4,128)(2,1)}, bf16[4,2048]{1,0:T(4,128)(2,1)S(1)}, u32[]{:S(2)}, u32[]{:S(2)}) collective-permute-start(bf16[4,2048]{1,0:T(4,128)(2,1)} %own_ref.1), channel_id=1, source_target_pairs={{0,1},{1,0},{2,3},{3,2},{4,5},{5,4},{6,7},{7,6},{8,9},{9,8},{10,11... | collective-permute-start | bytes 49160 | tf_op jit(solution)/shard_map/ppermute | solution.py:366
  4.0 1.6 %collective-permute-start = (bf16[256,256]{1,0:T(8,128)(2,1)}, bf16[256,256]{1,0:T(8,128)(2,1)S(1)}, u32[]{:S(2)}, u32[]{:S(2)}) collective-permute-start(bf16[256,256]{1,0:T(8,128)(2,1)} %k_ref.1), channel_id=1, source_target_pairs={{0,1},{1,0},{2,3},{3,2},{4,5},{5,4},{6,7},{7,6},{8,9},{9,8},{10,11... | collective-permute-start | bytes 393224 | tf_op jit(solution)/shard_map/ppermute | solution.py:366
  4.1 1.6 %collective-permute-start.1 = (bf16[256,256]{1,0:T(8,128)(2,1)}, bf16[256,256]{1,0:T(8,128)(2,1)S(1)}, u32[]{:S(2)}, u32[]{:S(2)}) collective-permute-start(bf16[256,256]{1,0:T(8,128)(2,1)} %v_ref.1), channel_id=1, source_target_pairs={{0,1},{1,0},{2,3},{3,2},{4,5},{5,4},{6,7},{7,6},{8,9},{9,8},{10,11... | collective-permute-start | bytes 393224 | tf_op jit(solution)/shard_map/ppermute | solution.py:366
  5.4 3.7 %copy-start.2 = (bf16[4,2048]{1,0:T(4,128)(2,1)S(1)}, bf16[4,2048]{1,0:T(4,128)(2,1)}, u32[]{:S(2)}) copy-start(bf16[4,2048]{1,0:T(4,128)(2,1)} %own_ref.1) | copy-start | bytes 49156
  5.7 17.7 %collective-permute-start.5 = (bf16[1024,128]{1,0:T(8,128)(2,1)S(1)}, bf16[1024,128]{1,0:T(8,128)(2,1)S(1)}, u32[]{:S(2)}, u32[]{:S(2)}) collective-permute-start(bf16[1024,128]{1,0:T(8,128)(2,1)S(1)} %join.1.refs_0_), channel_id=1, source_target_pairs={{0,6},{1,7},{2,4},{3,5},{4,2},{5,3},{6,0},{7,1},{8,14},{9,15},{10,... | collective-permute-start | bytes 786440 | tf_op jit(solution)/shard_map/ppermute | solution.py:369
  6.8 16.6 %collective-permute-start.4 = (bf16[1024,128]{1,0:T(8,128)(2,1)S(1)}, bf16[1024,128]{1,0:T(8,128)(2,1)S(1)}, u32[]{:S(2)}, u32[]{:S(2)}) collective-permute-start(bf16[1024,128]{1,0:T(8,128)(2,1)S(1)} %join.1.refs_0_), channel_id=1, source_target_pairs={{0,4},{1,5},{2,6},{3,7},{4,0},{5,1},{6,2},{7,3},{8,12},{9,13},{10,... | collective-permute-start | bytes 786440 | tf_op jit(solution)/shard_map/ppermute | solution.py:369
  7.2 16.2 %collective-permute-start.3 = (bf16[1024,128]{1,0:T(8,128)(2,1)S(1)}, bf16[1024,128]{1,0:T(8,128)(2,1)S(1)}, u32[]{:S(2)}, u32[]{:S(2)}) collective-permute-start(bf16[1024,128]{1,0:T(8,128)(2,1)S(1)} %join.1.refs_0_), channel_id=1, source_target_pairs={{0,2},{1,3},{2,0},{3,1},{4,6},{5,7},{6,4},{7,5},{8,10},{9,11},{10,... | collective-permute-start | bytes 786440 | tf_op jit(solution)/shard_map/ppermute | solution.py:369
  9.8 13.6 %all-to-all-start = ((bf16[8,64,128]{2,1,0:T(8,128)(2,1)}), bf16[8,64,128]{2,1,0:T(8,128)(2,1)S(1)}, u32[]{:S(2)}, u32[]{:S(2)}) async-start(bf16[8,64,128]{2,1,0:T(8,128)(2,1)} %repeat.1), calls=%async_computation | async-start | bytes 262144 | tf_op jit(solution)/shard_map/all_to_all | solution.py:383
  16.4 0.7 copy-start.3
  23.4 2.3 %copy-start.5 = (s32[64]{0:T(128)S(1)}, s32[64]{0:T(128)}, u32[]{:S(2)}) copy-start(s32[64]{0:T(128)} %lengths_ref.3) | copy-start | bytes 772
  24.1 9.3 %collective-permute-start.7 = (bf16[256,128]{1,0:T(8,128)(2,1)S(1)}, bf16[256,128]{1,0:T(8,128)(2,1)S(1)}, u32[]{:S(2)}, u32[]{:S(2)}) collective-permute-start(bf16[256,128]{1,0:T(8,128)(2,1)S(1)} %pick.1), channel_id=1, source_target_pairs={{0,56},{1,57},{2,58},{3,59},{4,60},{5,61},{6,62},{7,63},{8,0},{9,1... | collective-permute-start | bytes 196616 | tf_op jit(solution)/shard_map/ppermute | solution.py:372
  25.4 8.0 %collective-permute-start.6 = (bf16[256,128]{1,0:T(8,128)(2,1)S(1)}, bf16[256,128]{1,0:T(8,128)(2,1)S(1)}, u32[]{:S(2)}, u32[]{:S(2)}) collective-permute-start(bf16[256,128]{1,0:T(8,128)(2,1)S(1)} %pick.1), channel_id=1, source_target_pairs={{0,8},{1,9},{2,10},{3,11},{4,12},{5,13},{6,14},{7,15},{8,16},{9,17... | collective-permute-start | bytes 196616 | tf_op jit(solution)/shard_map/ppermute | solution.py:372
  29.6 17.7 %all-to-all-start.1 = ((f32[8,72,128]{2,1,0:T(8,128)}), f32[8,72,128]{2,1,0:T(8,128)S(1)}, u32[]{:S(2)}, u32[]{:S(2)}) async-start(f32[8,72,128]{2,1,0:T(8,128)} %question_pass.1), calls=%async_computation.1 | async-start | bytes 589824 | tf_op jit(solution)/shard_map/all_to_all | solution.py:388
  33.4 7.1 %collective-permute-start.9 = (bf16[256,128]{1,0:T(8,128)(2,1)S(1)}, bf16[256,128]{1,0:T(8,128)(2,1)S(1)}, u32[]{:S(2)}, u32[]{:S(2)}) collective-permute-start(bf16[256,128]{1,0:T(8,128)(2,1)S(1)} %select_select_fusion.1), channel_id=1, source_target_pairs={{0,40},{1,41},{2,42},{3,43},{4,44},{5,45},{6,46},{7,47},{8,48},{9,... | collective-permute-start | bytes 196616 | tf_op jit(solution)/shard_map/ppermute | solution.py:372
  38.0 9.3 %collective-permute-start.8 = (bf16[256,128]{1,0:T(8,128)(2,1)S(1)}, bf16[256,128]{1,0:T(8,128)(2,1)S(1)}, u32[]{:S(2)}, u32[]{:S(2)}) collective-permute-start(bf16[256,128]{1,0:T(8,128)(2,1)S(1)} %select_select_fusion.1), channel_id=1, source_target_pairs={{0,24},{1,25},{2,26},{3,27},{4,28},{5,29},{6,30},{7,31},{8,32},{9,... | collective-permute-start | bytes 196616 | tf_op jit(solution)/shard_map/ppermute | solution.py:372
  38.6 25.6 %copy-start.4 = (bf16[256,2048]{1,0:T(8,128)(2,1)S(1)}, bf16[256,2048]{1,0:T(8,128)(2,1)}, u32[]{:S(2)}) copy-start(bf16[256,2048]{1,0:T(8,128)(2,1)} %q_ref.1) | copy-start | bytes 3145732
  48.6 15.6 %copy-start = (bf16[256,256]{1,0:T(8,128)(2,1)S(1)}, bf16[256,256]{1,0:T(8,128)(2,1)}, u32[]{:S(2)}) copy-start(bf16[256,256]{1,0:T(8,128)(2,1)} %k_ref.1) | copy-start | bytes 393220
  48.7 15.6 %copy-start.1 = (bf16[256,256]{1,0:T(8,128)(2,1)S(1)}, bf16[256,256]{1,0:T(8,128)(2,1)}, u32[]{:S(2)}) copy-start(bf16[256,256]{1,0:T(8,128)(2,1)} %v_ref.1) | copy-start | bytes 393220
  48.7 22.7 %all-to-all-start.2 = ((bf16[32,8,1024]{2,1,0:T(8,128)(2,1)}), bf16[32,8,1024]{2,1,0:T(8,128)(2,1)S(1)}, u32[]{:S(2)}, u32[]{:S(2)}) async-start(bf16[32,8,1024]{2,1,0:T(8,128)(2,1)} %combine.1), calls=%async_computation.2 | async-start | bytes 1048576 | tf_op jit(solution)/shard_map/all_to_all | solution.py:395
  54.2 8.6 %collective-permute-start.12 = (bf16[256,128]{1,0:T(8,128)(2,1)S(1)}, bf16[256,128]{1,0:T(8,128)(2,1)S(1)}, u32[]{:S(2)}, u32[]{:S(2)}) collective-permute-start(bf16[256,128]{1,0:T(8,128)(2,1)S(1)} %select_select_fusion.refs_0_.piece_ref), channel_id=1, source_target_pairs={{0,3},{1,2},{2,1},{3,0},{4,7},{5,6},{6,5},{7,4},{8,11},{9,10},{10,... | collective-permute-start | bytes 196616 | tf_op jit(solution)/shard_map/ppermute | solution.py:397
  58.9 3.9 %collective-permute-start.11 = (bf16[256,128]{1,0:T(8,128)(2,1)S(1)}, bf16[256,128]{1,0:T(8,128)(2,1)S(1)}, u32[]{:S(2)}, u32[]{:S(2)}) collective-permute-start(bf16[256,128]{1,0:T(8,128)(2,1)S(1)} %select_select_fusion.refs_0_.piece_ref), channel_id=1, source_target_pairs={{0,1},{1,0},{2,3},{3,2},{4,5},{5,4},{6,7},{7,6},{8,9},{9,8},{10,11... | collective-permute-start | bytes 196616 | tf_op jit(solution)/shard_map/ppermute | solution.py:366
  58.9 5.4 %collective-permute-start.10 = (bf16[256,128]{1,0:T(8,128)(2,1)S(1)}, bf16[256,128]{1,0:T(8,128)(2,1)S(1)}, u32[]{:S(2)}, u32[]{:S(2)}) collective-permute-start(bf16[256,128]{1,0:T(8,128)(2,1)S(1)} %select_select_fusion.refs_0_.piece_ref), channel_id=1, source_target_pairs={{0,2},{1,3},{2,0},{3,1},{4,6},{5,7},{6,4},{7,5},{8,10},{9,11},{10,... | collective-permute-start | bytes 196616 | tf_op jit(solution)/shard_map/ppermute | solution.py:396
  71.3 2.7 %collective-permute-start.13 = (bf16[32,8,1024]{2,1,0:T(8,128)(2,1)S(1)}, bf16[32,8,1024]{2,1,0:T(8,128)(2,1)S(1)}, u32[]{:S(2)}, u32[]{:S(2)}) collective-permute-start(bf16[32,8,1024]{2,1,0:T(8,128)(2,1)S(1)} %gate.3.part_ref), channel_id=1, source_target_pairs={{0,1},{1,0},{2,3},{3,2},{4,5},{5,4},{6,7},{7,6},{8,9},{9,8},{10,11... | collective-permute-start | bytes 1572872 | tf_op jit(solution)/shard_map/ppermute | solution.py:366

commit v7 on v6

--- a/solution.py
+++ b/solution.py
@@ -228,7 +228,7 @@
     )(lengths, got, *columns)
 
 
-def combine_kernel(limit_ref, parts_ref, piece_ref, send_ref, columns_ref):
+def combine_kernel(limit_ref, parts_ref, piece_ref, early_ref, send_ref, columns_ref):
     z, y, c = coordinates()
     table = sign_table()
     rank = z % 2 * 4 + z // 2
@@ -253,28 +253,44 @@
         send_ref[i] = back
 
 
-def combine(limit, parts, piece):
+def combine(limit, parts, piece, early):
     return pl.pallas_call(
         combine_kernel,
         out_shape=jax.ShapeDtypeStruct((NZ * NY, 8, 1024), BF),
-        in_specs=[SMEM, VMEM, pl.BlockSpec(memory_space=pl.ANY)],
+        in_specs=[SMEM, VMEM] + [pl.BlockSpec(memory_space=pl.ANY)] * 2,
         out_specs=VMEM,
         scratch_shapes=[pltpu.VMEM((HD, HD), F32)],
         compiler_params=SMALL,
         name="combine",
-    )(limit, parts, piece)
+    )(limit, parts, piece, early)
+
+
+def caches_kernel(k_ref, v_ref, krot_ref, vrot_ref):
+    table = sign_table()
+    for g in range(2):
+        lanes = slice(HD * g, HD * g + HD)
+        krot_ref[:, lanes] = rotated(k_ref[:, lanes], table)
+        vrot_ref[:, lanes] = rotated(v_ref[:, lanes], table)
+
+
+def caches(k, v):
+    return pl.pallas_call(
+        caches_kernel,
+        out_shape=(jax.ShapeDtypeStruct(k.shape, BF), jax.ShapeDtypeStruct(v.shape, BF)),
+        in_specs=[VMEM] * 2,
+        out_specs=(VMEM, VMEM),
+        compiler_params=SMALL,
+        name="caches",
+    )(k, v)
 
 
 def encode_kernel(anchor_ref, lengths_ref, q_ref, k_ref, v_ref, *refs):
     pieces = refs[:4]
-    mixed_ref, krot_ref, vrot_ref, token_ref, far_k_ref, far_v_ref = refs[4:]
+    mixed_ref, token_ref, far_k_ref, far_v_ref = refs[4:]
     z, y, c = coordinates()
     place = index_of(z, y, c)
     anchor = anchor_ref[0]
     k, v = k_ref[...], v_ref[...]
-    table = sign_table()
-    krot_ref[...] = rotated(k, table)
-    vrot_ref[...] = rotated(v, table)
     token_ref[...] = jnp.zeros_like(token_ref)
     g = pl.program_id(0)
     for core in range(2):
@@ -314,12 +330,10 @@
         grid=(2,),
         out_shape=(
             jax.ShapeDtypeStruct(q.shape, BF),
-            jax.ShapeDtypeStruct(k.shape, BF),
-            jax.ShapeDtypeStruct(v.shape, BF),
             jax.ShapeDtypeStruct((8, HD), F32),
         ),
         in_specs=[SMEM, SMEM, heads, group, group] + [VMEM] * 4,
-        out_specs=(heads, group, group, token),
+        out_specs=(heads, token),
         scratch_shapes=[pltpu.VMEM((BLK, HD), BF), pltpu.VMEM((BLK, HD), BF)],
         compiler_params=PARAMS,
         cost_estimate=pl.CostEstimate(
@@ -391,11 +405,12 @@
     below, above = along_z(piece, 3)
     near = (distance < 2) | (distance == NZ - 1)
     piece = jnp.where(near, piece, jnp.where(distance < 5, below, above))
-    spread = combine(question_length, parts, piece)
+    key_cache, value_cache = caches(context_k, context_v)
+    spread = combine(question_length, parts, piece, value_cache)
     own = lax.all_to_all(spread, "ctx", 0, 0, axis_index_groups=CHIP_GROUPS)
     pieces = [piece, lax.ppermute(piece, "ctx", Y_PARTNER)]
     pieces = pieces + [swap(piece), lax.ppermute(piece, "ctx", DIAGONAL)]
-    mixed, key_cache, value_cache, token = encode(
+    mixed, token = encode(
         anchor_index,
         block_lengths,
         context_q,

time: 75.6 us -> 75 us (level)
  waiting for transfers between devices: 21 us -> 20.1 us
    ppermute x2, waiting for transfers between devices: 1.89 us -> 0.93 us  [along_z(): lax.ppermute(x, 'ctx', Z_SHIFTS[NZ - d])]
    pallas_call x0 -> x1, Pallas kernels: none -> 0.94 us  [caches(): pl.pallas_call(caches_kernel, out_shape=(jax.ShapeDtypeStruct(k.shape, BF...]
where the time goes in v7:
time: 75 us; the launch traced here: 74.5 us
  starting transfers between devices  35.1 us (47%)
  waiting for transfers between devices  20.1 us (27%)
  Pallas kernels  15.8 us (21%)
  between operations  1.8 us (2%)
  local copies, waits for them, and re-layouts  1.57 us (2%)
    ppermute x2, waiting for transfers between devices, along_z(): lax.ppermute(x, 'ctx', Z_SHIFTS[d])  6.78 us
    pallas_call x1, Pallas kernels, encode(): pl.pallas_call(encode_kernel, grid=(2,), out_shape=(jax.ShapeDtypeStruct(...  6.69 us
    all_to_all x1, starting transfers between devices, on_device(): got = lax.all_to_all(spread_rows, 'ctx', 0, 0, axis_index_groups=Z_GROUPS)  6.61 us
    all_to_all x1, waiting for transfers between devices, on_device(): got = lax.all_to_all(spread_rows, 'ctx', 0, 0, axis_index_groups=Z_GROUPS)  6.2 us
    ppermute x2, starting transfers between devices, along_z(): lax.ppermute(x, 'ctx', Z_SHIFTS[NZ - d])  5.87 us
    all_to_all x1, starting transfers between devices, on_device(): own = lax.all_to_all(spread, 'ctx', 0, 0, axis_index_groups=CHIP_GROUPS)  5.35 us
    ppermute x5, starting transfers between devices, swap(): return lax.ppermute(x, 'ctx', OTHER_CORE)  4.94 us
    ppermute x1, starting transfers between devices, on_device(): pieces = pieces + [swap(piece), lax.ppermute(piece, 'ctx', DIAGONAL)]  4.72 us
  transfers between devices with their start and end apart: 17, of which 8 were waited for; matrix products, arithmetic and copies ran while one was open for 1% of the time, Pallas kernels for 17%

profile of v7, /device:TPU:1, one launch (start us, length us, event | category | flops | bytes accessed | tf_op | source)
XLA Modules:
  0.0 74.5 jit_solution(11843539638555811041)
XLA Ops:
  0.6 3.3 %collective-permute-start.2 = (bf16[4,2048]{1,0:T(4,128)(2,1)}, bf16[4,2048]{1,0:T(4,128)(2,1)S(1)}, u32[]{:S(2)}, u32[]{:S(2)}) collective-permute-start(bf16[4,2048]{1,0:T(4,128)(2,1)} %own_ref.1), channel_id=1, source_target_pairs={{0,1},{1,0},{2,3},{3,2},{4,5},{5,4},{6,7},{7,6},{8,9},{9,8},{10,11... | collective-permute-start | bytes 49160 | tf_op jit(solution)/shard_map/ppermute | solution.py:380
  4.0 0.1 collective-permute-start
  4.1 0.4 collective-permute-start.1
  4.5 0.9 %constant_dynamic-slice_fusion = (bf16[256,128]{1,0:T(8,128)(2,1)S(1)}, bf16[256,128]{1,0:T(8,128)(2,1)S(1)}) fusion(bf16[256,256]{1,0:T(8,128)(2,1)} %v_ref.3, s32[]{:T(128)S(6)} %select_n.49, bf16[256,256]{1,0:T(8,128)(2,1)} %k_ref.3), kind=kLoop, calls=%fused_computation.3 | loop fusion | bytes 262148 | tf_op jit(solution)/shard_map/dynamic_slice | solution.py:392
  5.4 0.0 copy-start.3
  5.4 0.0 collective-permute-done.2.early_ref.other_ref
  5.4 0.1 collective-permute-done.k_ref
  5.5 0.2 collective-permute-done.1.v_ref
  5.7 1.1 %collective-permute-start.5 = (bf16[1024,128]{1,0:T(8,128)(2,1)S(1)}, bf16[1024,128]{1,0:T(8,128)(2,1)S(1)}, u32[]{:S(2)}, u32[]{:S(2)}) collective-permute-start(bf16[1024,128]{1,0:T(8,128)(2,1)S(1)} %join.1.refs_0_), channel_id=1, source_target_pairs={{0,6},{1,7},{2,4},{3,5},{4,2},{5,3},{6,0},{7,1},{8,14},{9,15},{10,... | collective-permute-start | bytes 786440 | tf_op jit(solution)/shard_map/ppermute | solution.py:383
  6.8 0.3 collective-permute-start.4
  7.2 1.9 %collective-permute-start.3 = (bf16[1024,128]{1,0:T(8,128)(2,1)S(1)}, bf16[1024,128]{1,0:T(8,128)(2,1)S(1)}, u32[]{:S(2)}, u32[]{:S(2)}) collective-permute-start(bf16[1024,128]{1,0:T(8,128)(2,1)S(1)} %join.1.refs_0_), channel_id=1, source_target_pairs={{0,2},{1,3},{2,0},{3,1},{4,6},{5,7},{6,4},{7,5},{8,10},{9,11},{10,... | collective-permute-start | bytes 786440 | tf_op jit(solution)/shard_map/ppermute | solution.py:383
  9.1 0.7 repeat.1
  9.8 6.6 %all-to-all-start = ((bf16[8,64,128]{2,1,0:T(8,128)(2,1)}), bf16[8,64,128]{2,1,0:T(8,128)(2,1)S(1)}, u32[]{:S(2)}, u32[]{:S(2)}) async-start(bf16[8,64,128]{2,1,0:T(8,128)(2,1)} %repeat.1), calls=%async_computation | async-start | bytes 262144 | tf_op jit(solution)/shard_map/all_to_all | solution.py:397
  16.4 0.7 copy-done.4
  17.2 6.2 %all-to-all-done.refs_3_.got_ref = bf16[8,64,128]{2,1,0:T(8,128)(2,1)S(1)} async-done(((bf16[8,64,128]{2,1,0:T(8,128)(2,1)}), bf16[8,64,128]{2,1,0:T(8,128)(2,1)S(1)}, u32[]{:S(2)}, u32[]{:S(2)}) %all-to-all-start) | async-done | bytes 131104 | tf_op jit(solution)/shard_map/all_to_all | solution.py:397
  23.4 0.0 collective-permute-done.5.refs_2_
  23.4 0.0 collective-permute-done.4.refs_1_
  23.4 0.0 collective-permute-done.3.refs_0_
  23.4 0.0 copy-start.6
  23.5 0.6 pick.1
  24.1 1.3 %collective-permute-start.7 = (bf16[256,128]{1,0:T(8,128)(2,1)S(1)}, bf16[256,128]{1,0:T(8,128)(2,1)S(1)}, u32[]{:S(2)}, u32[]{:S(2)}) collective-permute-start(bf16[256,128]{1,0:T(8,128)(2,1)S(1)} %pick.1), channel_id=1, source_target_pairs={{0,56},{1,57},{2,58},{3,59},{4,60},{5,61},{6,62},{7,63},{8,0},{9,1... | collective-permute-start | bytes 196616 | tf_op jit(solution)/shard_map/ppermute | solution.py:386
  25.4 0.3 collective-permute-start.6
  25.7 3.9 %question_pass.1 = f32[8,72,128]{2,1,0:T(8,128)} custom-call(s32[64]{0:T(128)S(1)} %copy-done.6, bf16[8,64,128]{2,1,0:T(8,128)(2,1)S(1)} %all-to-all-done.refs_3_.got_ref, bf16[1024,128]{1,0:T(8,128)(2,1)S(1)} %join.1.refs_0_, bf16[1024,128]{1,0:T(8,128)(2,1)S(1)} %get-tuple-element.11.refs_1_, bf16[1024,128]{1,0:T(8,128)(2,1)S(1)} %get-tuple-element.12.refs_2_, ...), custom_call_target="tpu_custom_call" | custom-call | flops 900000000 | bytes 2500000 | tf_op jit(solution)/shard_map/question_pass/pallas_call | solution.py:218
  29.6 3.8 %all-to-all-start.1 = ((f32[8,72,128]{2,1,0:T(8,128)}), f32[8,72,128]{2,1,0:T(8,128)S(1)}, u32[]{:S(2)}, u32[]{:S(2)}) async-start(f32[8,72,128]{2,1,0:T(8,128)} %question_pass.1), calls=%async_computation.1 | async-start | bytes 589824 | tf_op jit(solution)/shard_map/all_to_all | solution.py:402
  33.4 0.0 copy-start.1
  33.4 0.0 collective-permute-done.7
  33.4 0.0 collective-permute-done.6
  33.4 4.5 %collective-permute-start.9 = (bf16[256,128]{1,0:T(8,128)(2,1)S(1)}, bf16[256,128]{1,0:T(8,128)(2,1)S(1)}, u32[]{:S(2)}, u32[]{:S(2)}) collective-permute-start(bf16[256,128]{1,0:T(8,128)(2,1)S(1)} %select_select_fusion.1), channel_id=1, source_target_pairs={{0,40},{1,41},{2,42},{3,43},{4,44},{5,45},{6,46},{7,47},{8,48},{9,... | collective-permute-start | bytes 196616 | tf_op jit(solution)/shard_map/ppermute | solution.py:386
  38.0 0.0 collective-permute-start.8
  38.0 0.9 %caches.1 = (bf16[256,256]{1,0:T(8,128)(2,1)}, bf16[256,256]{1,0:T(8,128)(2,1)}) custom-call(bf16[256,256]{1,0:T(8,128)(2,1)S(1)} %copy-done, bf16[256,256]{1,0:T(8,128)(2,1)S(1)} %copy-done.1), custom_call_target="tpu_custom_call" | custom-call | tf_op jit(solution)/shard_map/caches/pallas_call | solution.py:277
  39.6 0.0 copy-start.2
  39.6 0.9 %collective-permute-done.9 = bf16[256,128]{1,0:T(8,128)(2,1)S(1)} collective-permute-done((bf16[256,128]{1,0:T(8,128)(2,1)S(1)}, bf16[256,128]{1,0:T(8,128)(2,1)S(1)}, u32[]{:S(2)}, u32[]{:S(2)}) %collective-permute-start.9) | collective-permute-done | bytes 65568 | tf_op jit(solution)/shard_map/ppermute | solution.py:386
  40.5 6.8 %collective-permute-done.8 = bf16[256,128]{1,0:T(8,128)(2,1)S(1)} collective-permute-done((bf16[256,128]{1,0:T(8,128)(2,1)S(1)}, bf16[256,128]{1,0:T(8,128)(2,1)S(1)}, u32[]{:S(2)}, u32[]{:S(2)}) %collective-permute-start.8) | collective-permute-done | bytes 65568 | tf_op jit(solution)/shard_map/ppermute | solution.py:386
  47.3 0.0 copy-start.5
  47.3 0.0 all-to-all-done.1.parts_ref
  47.3 1.3 %combine.1 = bf16[32,8,1024]{2,1,0:T(8,128)(2,1)} custom-call(s32[1]{0:T(128)S(6)} %copy.21.limit_ref, f32[8,72,128]{2,1,0:T(8,128)S(1)} %all-to-all-done.1.parts_ref, bf16[256,128]{1,0:T(8,128)(2,1)S(1)} %select_select_fusion.refs_0_.piece_ref, bf16[256,256]{1,0:T(8,128)(2,1)S(1)} %copy-done.2), custom_call_target="tpu_custom_call" | custom-call | tf_op jit(solution)/shard_map/combine/pallas_call | solution.py:257
  48.7 5.4 %all-to-all-start.2 = ((bf16[32,8,1024]{2,1,0:T(8,128)(2,1)}), bf16[32,8,1024]{2,1,0:T(8,128)(2,1)S(1)}, u32[]{:S(2)}, u32[]{:S(2)}) async-start(bf16[32,8,1024]{2,1,0:T(8,128)(2,1)} %combine.1), calls=%async_computation.2 | async-start | bytes 1048576 | tf_op jit(solution)/shard_map/all_to_all | solution.py:410
  54.0 4.7 %collective-permute-start.12 = (bf16[256,128]{1,0:T(8,128)(2,1)S(1)}, bf16[256,128]{1,0:T(8,128)(2,1)S(1)}, u32[]{:S(2)}, u32[]{:S(2)}) collective-permute-start(bf16[256,128]{1,0:T(8,128)(2,1)S(1)} %select_select_fusion.refs_0_.piece_ref), channel_id=1, source_target_pairs={{0,3},{1,2},{2,1},{3,0},{4,7},{5,6},{6,5},{7,4},{8,11},{9,10},{10,... | collective-permute-start | bytes 196616 | tf_op jit(solution)/shard_map/ppermute | solution.py:412
  58.7 0.2 collective-permute-start.10
  59.0 3.7 %collective-permute-done.12.refs_3_ = bf16[256,128]{1,0:T(8,128)(2,1)S(1)} collective-permute-done((bf16[256,128]{1,0:T(8,128)(2,1)S(1)}, bf16[256,128]{1,0:T(8,128)(2,1)S(1)}, u32[]{:S(2)}, u32[]{:S(2)}) %collective-permute-start.12) | collective-permute-done | bytes 65568 | tf_op jit(solution)/shard_map/ppermute | solution.py:412
  62.7 0.0 collective-permute-done.11.refs_2_
  62.7 1.5 %collective-permute-done.10.refs_1_ = bf16[256,128]{1,0:T(8,128)(2,1)S(1)} collective-permute-done((bf16[256,128]{1,0:T(8,128)(2,1)S(1)}, bf16[256,128]{1,0:T(8,128)(2,1)S(1)}, u32[]{:S(2)}, u32[]{:S(2)}) %collective-permute-start.10) | collective-permute-done | bytes 65568 | tf_op jit(solution)/shard_map/ppermute | solution.py:411
  64.1 6.7 %encode.1 = (bf16[256,2048]{1,0:T(8,128)(2,1)}, f32[8,128]{1,0:T(8,128)S(1)}) custom-call(s32[64]{0:T(128)S(1)} %copy-done.4, s32[64]{0:T(128)S(1)} %copy-done.6, bf16[256,2048]{1,0:T(8,128)(2,1)S(1)} %copy-done.5, bf16[256,256]{1,0:T(8,128)(2,1)S(1)} %copy-done, bf16[256,256]{1,0:T(8,128)(2,1)S(1)} %copy-done.1, ...), custom_call_target="tpu_custom_call" | custom-call | flops 1100000000 | bytes 3500000 | tf_op jit(solution)/shard_map/encode/pallas_call | solution.py:328
  70.8 0.0 all-to-all-done.2.refs_0_
  70.8 1.1 %collective-permute-start.13 = (bf16[32,8,1024]{2,1,0:T(8,128)(2,1)S(1)}, bf16[32,8,1024]{2,1,0:T(8,128)(2,1)S(1)}, u32[]{:S(2)}, u32[]{:S(2)}) collective-permute-start(bf16[32,8,1024]{2,1,0:T(8,128)(2,1)S(1)} %gate.3.part_ref), channel_id=1, source_target_pairs={{0,1},{1,0},{2,3},{3,2},{4,5},{5,4},{6,7},{7,6},{8,9},{9,8},{10,11... | collective-permute-start | bytes 1572872 | tf_op jit(solution)/shard_map/ppermute | solution.py:380
  71.9 0.8 %assemble.2.refs_0_ = bf16[4,2,4,8,2048]{4,3,2,1,0:T(8,128)(2,1)} custom-call(bf16[32,8,1024]{2,1,0:T(8,128)(2,1)S(1)} %gate.3.part_ref), custom_call_target="tpu_custom_call" | custom-call | tf_op jit(solution)/shard_map/assemble/pallas_call | solution.py:364
  72.8 0.7 collective-permute-done.13.part_ref
  73.5 0.8 %assemble.3 = bf16[4,2,4,8,2048]{4,3,2,1,0:T(8,128)(2,1)} custom-call(bf16[32,8,1024]{2,1,0:T(8,128)(2,1)S(1)} %collective-permute-done.13.part_ref, bf16[4,2,4,8,2048]{4,3,2,1,0:T(8,128)(2,1)} %assemble.2.refs_0_), custom_call_target="tpu_custom_call", output_to_operand_aliasing={{}: (1, {})} | custom-call | tf_op jit(solution)/shard_map/assemble/pallas_call | solution.py:364
  (15 shorter events, 0.1 us)
Async XLA Ops:
  0.6 4.8 %collective-permute-start.2 = (bf16[4,2048]{1,0:T(4,128)(2,1)}, bf16[4,2048]{1,0:T(4,128)(2,1)S(1)}, u32[]{:S(2)}, u32[]{:S(2)}) collective-permute-start(bf16[4,2048]{1,0:T(4,128)(2,1)} %own_ref.1), channel_id=1, source_target_pairs={{0,1},{1,0},{2,3},{3,2},{4,5},{5,4},{6,7},{7,6},{8,9},{9,8},{10,11... | collective-permute-start | bytes 49160 | tf_op jit(solution)/shard_map/ppermute | solution.py:380
  4.0 1.6 %collective-permute-start = (bf16[256,256]{1,0:T(8,128)(2,1)}, bf16[256,256]{1,0:T(8,128)(2,1)S(1)}, u32[]{:S(2)}, u32[]{:S(2)}) collective-permute-start(bf16[256,256]{1,0:T(8,128)(2,1)} %k_ref.3), channel_id=1, source_target_pairs={{0,1},{1,0},{2,3},{3,2},{4,5},{5,4},{6,7},{7,6},{8,9},{9,8},{10,11... | collective-permute-start | bytes 393224 | tf_op jit(solution)/shard_map/ppermute | solution.py:380
  4.1 1.6 %collective-permute-start.1 = (bf16[256,256]{1,0:T(8,128)(2,1)}, bf16[256,256]{1,0:T(8,128)(2,1)S(1)}, u32[]{:S(2)}, u32[]{:S(2)}) collective-permute-start(bf16[256,256]{1,0:T(8,128)(2,1)} %v_ref.3), channel_id=1, source_target_pairs={{0,1},{1,0},{2,3},{3,2},{4,5},{5,4},{6,7},{7,6},{8,9},{9,8},{10,11... | collective-permute-start | bytes 393224 | tf_op jit(solution)/shard_map/ppermute | solution.py:380
  5.4 3.7 %copy-start.3 = (bf16[4,2048]{1,0:T(4,128)(2,1)S(1)}, bf16[4,2048]{1,0:T(4,128)(2,1)}, u32[]{:S(2)}) copy-start(bf16[4,2048]{1,0:T(4,128)(2,1)} %own_ref.1) | copy-start | bytes 49156
  5.7 17.7 %collective-permute-start.5 = (bf16[1024,128]{1,0:T(8,128)(2,1)S(1)}, bf16[1024,128]{1,0:T(8,128)(2,1)S(1)}, u32[]{:S(2)}, u32[]{:S(2)}) collective-permute-start(bf16[1024,128]{1,0:T(8,128)(2,1)S(1)} %join.1.refs_0_), channel_id=1, source_target_pairs={{0,6},{1,7},{2,4},{3,5},{4,2},{5,3},{6,0},{7,1},{8,14},{9,15},{10,... | collective-permute-start | bytes 786440 | tf_op jit(solution)/shard_map/ppermute | solution.py:383
  6.8 16.6 %collective-permute-start.4 = (bf16[1024,128]{1,0:T(8,128)(2,1)S(1)}, bf16[1024,128]{1,0:T(8,128)(2,1)S(1)}, u32[]{:S(2)}, u32[]{:S(2)}) collective-permute-start(bf16[1024,128]{1,0:T(8,128)(2,1)S(1)} %join.1.refs_0_), channel_id=1, source_target_pairs={{0,4},{1,5},{2,6},{3,7},{4,0},{5,1},{6,2},{7,3},{8,12},{9,13},{10,... | collective-permute-start | bytes 786440 | tf_op jit(solution)/shard_map/ppermute | solution.py:383
  7.2 16.2 %collective-permute-start.3 = (bf16[1024,128]{1,0:T(8,128)(2,1)S(1)}, bf16[1024,128]{1,0:T(8,128)(2,1)S(1)}, u32[]{:S(2)}, u32[]{:S(2)}) collective-permute-start(bf16[1024,128]{1,0:T(8,128)(2,1)S(1)} %join.1.refs_0_), channel_id=1, source_target_pairs={{0,2},{1,3},{2,0},{3,1},{4,6},{5,7},{6,4},{7,5},{8,10},{9,11},{10,... | collective-permute-start | bytes 786440 | tf_op jit(solution)/shard_map/ppermute | solution.py:383
  9.8 13.6 %all-to-all-start = ((bf16[8,64,128]{2,1,0:T(8,128)(2,1)}), bf16[8,64,128]{2,1,0:T(8,128)(2,1)S(1)}, u32[]{:S(2)}, u32[]{:S(2)}) async-start(bf16[8,64,128]{2,1,0:T(8,128)(2,1)} %repeat.1), calls=%async_computation | async-start | bytes 262144 | tf_op jit(solution)/shard_map/all_to_all | solution.py:397
  16.4 0.7 copy-start.4
  23.4 2.3 %copy-start.6 = (s32[64]{0:T(128)S(1)}, s32[64]{0:T(128)}, u32[]{:S(2)}) copy-start(s32[64]{0:T(128)} %lengths_ref.3) | copy-start | bytes 772
  24.1 9.3 %collective-permute-start.7 = (bf16[256,128]{1,0:T(8,128)(2,1)S(1)}, bf16[256,128]{1,0:T(8,128)(2,1)S(1)}, u32[]{:S(2)}, u32[]{:S(2)}) collective-permute-start(bf16[256,128]{1,0:T(8,128)(2,1)S(1)} %pick.1), channel_id=1, source_target_pairs={{0,56},{1,57},{2,58},{3,59},{4,60},{5,61},{6,62},{7,63},{8,0},{9,1... | collective-permute-start | bytes 196616 | tf_op jit(solution)/shard_map/ppermute | solution.py:386
  25.4 8.0 %collective-permute-start.6 = (bf16[256,128]{1,0:T(8,128)(2,1)S(1)}, bf16[256,128]{1,0:T(8,128)(2,1)S(1)}, u32[]{:S(2)}, u32[]{:S(2)}) collective-permute-start(bf16[256,128]{1,0:T(8,128)(2,1)S(1)} %pick.1), channel_id=1, source_target_pairs={{0,8},{1,9},{2,10},{3,11},{4,12},{5,13},{6,14},{7,15},{8,16},{9,17... | collective-permute-start | bytes 196616 | tf_op jit(solution)/shard_map/ppermute | solution.py:386
  29.6 17.7 %all-to-all-start.1 = ((f32[8,72,128]{2,1,0:T(8,128)}), f32[8,72,128]{2,1,0:T(8,128)S(1)}, u32[]{:S(2)}, u32[]{:S(2)}) async-start(f32[8,72,128]{2,1,0:T(8,128)} %question_pass.1), calls=%async_computation.1 | async-start | bytes 589824 | tf_op jit(solution)/shard_map/all_to_all | solution.py:402
  33.4 4.6 %copy-start = (bf16[256,256]{1,0:T(8,128)(2,1)S(1)}, bf16[256,256]{1,0:T(8,128)(2,1)}, u32[]{:S(2)}) copy-start(bf16[256,256]{1,0:T(8,128)(2,1)} %k_ref.3) | copy-start | bytes 393220
  33.4 4.6 %copy-start.1 = (bf16[256,256]{1,0:T(8,128)(2,1)S(1)}, bf16[256,256]{1,0:T(8,128)(2,1)}, u32[]{:S(2)}) copy-start(bf16[256,256]{1,0:T(8,128)(2,1)} %v_ref.3) | copy-start | bytes 393220
  33.4 7.1 %collective-permute-start.9 = (bf16[256,128]{1,0:T(8,128)(2,1)S(1)}, bf16[256,128]{1,0:T(8,128)(2,1)S(1)}, u32[]{:S(2)}, u32[]{:S(2)}) collective-permute-start(bf16[256,128]{1,0:T(8,128)(2,1)S(1)} %select_select_fusion.1), channel_id=1, source_target_pairs={{0,40},{1,41},{2,42},{3,43},{4,44},{5,45},{6,46},{7,47},{8,48},{9,... | collective-permute-start | bytes 196616 | tf_op jit(solution)/shard_map/ppermute | solution.py:386
  38.0 9.3 %collective-permute-start.8 = (bf16[256,128]{1,0:T(8,128)(2,1)S(1)}, bf16[256,128]{1,0:T(8,128)(2,1)S(1)}, u32[]{:S(2)}, u32[]{:S(2)}) collective-permute-start(bf16[256,128]{1,0:T(8,128)(2,1)S(1)} %select_select_fusion.1), channel_id=1, source_target_pairs={{0,24},{1,25},{2,26},{3,27},{4,28},{5,29},{6,30},{7,31},{8,32},{9,... | collective-permute-start | bytes 196616 | tf_op jit(solution)/shard_map/ppermute | solution.py:386
  39.6 7.8 %copy-start.2 = (bf16[256,256]{1,0:T(8,128)(2,1)S(1)}, bf16[256,256]{1,0:T(8,128)(2,1)}, u32[]{:S(2)}) copy-start(bf16[256,256]{1,0:T(8,128)(2,1)} %get-tuple-element.9.early_ref) | copy-start | bytes 393220
  47.3 16.8 %copy-start.5 = (bf16[256,2048]{1,0:T(8,128)(2,1)S(1)}, bf16[256,2048]{1,0:T(8,128)(2,1)}, u32[]{:S(2)}) copy-start(bf16[256,2048]{1,0:T(8,128)(2,1)} %q_ref.1) | copy-start | bytes 3145732
  48.7 22.1 %all-to-all-start.2 = ((bf16[32,8,1024]{2,1,0:T(8,128)(2,1)}), bf16[32,8,1024]{2,1,0:T(8,128)(2,1)S(1)}, u32[]{:S(2)}, u32[]{:S(2)}) async-start(bf16[32,8,1024]{2,1,0:T(8,128)(2,1)} %combine.1), calls=%async_computation.2 | async-start | bytes 1048576 | tf_op jit(solution)/shard_map/all_to_all | solution.py:410
  54.0 8.6 %collective-permute-start.12 = (bf16[256,128]{1,0:T(8,128)(2,1)S(1)}, bf16[256,128]{1,0:T(8,128)(2,1)S(1)}, u32[]{:S(2)}, u32[]{:S(2)}) collective-permute-start(bf16[256,128]{1,0:T(8,128)(2,1)S(1)} %select_select_fusion.refs_0_.piece_ref), channel_id=1, source_target_pairs={{0,3},{1,2},{2,1},{3,0},{4,7},{5,6},{6,5},{7,4},{8,11},{9,10},{10,... | collective-permute-start | bytes 196616 | tf_op jit(solution)/shard_map/ppermute | solution.py:412
  58.7 3.9 %collective-permute-start.11 = (bf16[256,128]{1,0:T(8,128)(2,1)S(1)}, bf16[256,128]{1,0:T(8,128)(2,1)S(1)}, u32[]{:S(2)}, u32[]{:S(2)}) collective-permute-start(bf16[256,128]{1,0:T(8,128)(2,1)S(1)} %select_select_fusion.refs_0_.piece_ref), channel_id=1, source_target_pairs={{0,1},{1,0},{2,3},{3,2},{4,5},{5,4},{6,7},{7,6},{8,9},{9,8},{10,11... | collective-permute-start | bytes 196616 | tf_op jit(solution)/shard_map/ppermute | solution.py:380
  58.7 5.4 %collective-permute-start.10 = (bf16[256,128]{1,0:T(8,128)(2,1)S(1)}, bf16[256,128]{1,0:T(8,128)(2,1)S(1)}, u32[]{:S(2)}, u32[]{:S(2)}) collective-permute-start(bf16[256,128]{1,0:T(8,128)(2,1)S(1)} %select_select_fusion.refs_0_.piece_ref), channel_id=1, source_target_pairs={{0,2},{1,3},{2,0},{3,1},{4,6},{5,7},{6,4},{7,5},{8,10},{9,11},{10,... | collective-permute-start | bytes 196616 | tf_op jit(solution)/shard_map/ppermute | solution.py:411
  70.8 2.6 %collective-permute-start.13 = (bf16[32,8,1024]{2,1,0:T(8,128)(2,1)S(1)}, bf16[32,8,1024]{2,1,0:T(8,128)(2,1)S(1)}, u32[]{:S(2)}, u32[]{:S(2)}) collective-permute-start(bf16[32,8,1024]{2,1,0:T(8,128)(2,1)S(1)} %gate.3.part_ref), channel_id=1, source_target_pairs={{0,1},{1,0},{2,3},{3,2},{4,5},{5,4},{6,7},{7,6},{8,9},{9,8},{10,11... | collective-permute-start | bytes 1572872 | tf_op jit(solution)/shard_map/ppermute | solution.py:380

commit v8 on v7

--- a/solution.py
+++ b/solution.py
@@ -39,7 +39,6 @@
 CHIP_GROUPS = [[index_of(z, y, c) for y in range(NY) for z in Z_ORDER] for c in range(NC)]
 OTHER_CORE = permutation(lambda z, y, c: (z, y, 1 - c))
 Y_PARTNER = permutation(lambda z, y, c: (z, y ^ 1, c))
-DIAGONAL = permutation(lambda z, y, c: (z, y ^ 1, 1 - c))
 Y_MOVES = [permutation(lambda z, y, c, d=d: (z, y ^ d, c)) for d in range(NY)]
 Z_SHIFTS = [permutation(lambda z, y, c, d=d: ((z + d) % NZ, y, c)) for d in range(NZ)]
 
@@ -409,7 +408,7 @@
     spread = combine(question_length, parts, piece, value_cache)
     own = lax.all_to_all(spread, "ctx", 0, 0, axis_index_groups=CHIP_GROUPS)
     pieces = [piece, lax.ppermute(piece, "ctx", Y_PARTNER)]
-    pieces = pieces + [swap(piece), lax.ppermute(piece, "ctx", DIAGONAL)]
+    pieces = pieces + [swap(x) for x in pieces]
     mixed, token = encode(
         anchor_index,
         block_lengths,

time: 75 us -> 74.9 us (level)
  waiting for transfers between devices: 20.1 us -> 15.8 us
  starting transfers between devices: 35.1 us -> 39.4 us
    ppermute x5 -> x6, starting transfers between devices: 4.94 us -> 12.8 us  [swap(): return lax.ppermute(x, 'ctx', OTHER_CORE)]
    ppermute x1 -> x0, starting transfers between devices: 4.72 us -> none  [on_device(): pieces = pieces + [swap(piece), lax.ppermute(piece, 'ctx', DIAGONAL)]]
    ppermute x1 -> x0, waiting for transfers between devices: 3.69 us -> none  [on_device(): pieces = pieces + [swap(piece), lax.ppermute(piece, 'ctx', DIAGONAL)]]
    ppermute x1, waiting for transfers between devices: 1.47 us -> 0.01 us  [on_device(): pieces = [piece, lax.ppermute(piece, 'ctx', Y_PARTNER)]]
    ppermute x1, starting transfers between devices: 0.21 us -> 1.32 us  [on_device(): pieces = [piece, lax.ppermute(piece, 'ctx', Y_PARTNER)]]
    ppermute x5 -> x6, waiting for transfers between devices: 1 us -> 1.9 us  [swap(): return lax.ppermute(x, 'ctx', OTHER_CORE)]
  transfers between devices with their start and end apart: 17 -> 17, of which waited for: 8 -> 7; matrix products, arithmetic and copies ran while one was open for 1% -> 1% of each run, Pallas kernels for 17% -> 17%
where the time goes in v8:
time: 74.9 us; the launch traced here: 74.5 us
  starting transfers between devices  39.4 us (53%)
  Pallas kernels  15.9 us (21%)
  waiting for transfers between devices  15.8 us (21%)
  between operations  1.8 us (2%)
  local copies, waits for them, and re-layouts  1.57 us (2%)
    ppermute x6, starting transfers between devices, swap(): return lax.ppermute(x, 'ctx', OTHER_CORE)  12.8 us
    ppermute x2, waiting for transfers between devices, along_z(): lax.ppermute(x, 'ctx', Z_SHIFTS[d])  6.78 us
    pallas_call x1, Pallas kernels, encode(): pl.pallas_call(encode_kernel, grid=(2,), out_shape=(jax.ShapeDtypeStruct(...  6.7 us
    all_to_all x1, starting transfers between devices, on_device(): got = lax.all_to_all(spread_rows, 'ctx', 0, 0, axis_index_groups=Z_GROUPS)  6.61 us
    all_to_all x1, waiting for transfers between devices, on_device(): got = lax.all_to_all(spread_rows, 'ctx', 0, 0, axis_index_groups=Z_GROUPS)  6.2 us
    ppermute x2, starting transfers between devices, along_z(): lax.ppermute(x, 'ctx', Z_SHIFTS[NZ - d])  5.87 us
    all_to_all x1, starting transfers between devices, on_device(): own = lax.all_to_all(spread, 'ctx', 0, 0, axis_index_groups=CHIP_GROUPS)  5.35 us
    pallas_call x1, Pallas kernels, question_pass(): pl.pallas_call(question_kernel, out_shape=jax.ShapeDtypeStruct((NZ, 72, H...  3.88 us
  transfers between devices with their start and end apart: 17, of which 7 were waited for; matrix products, arithmetic and copies ran while one was open for 1% of the time, Pallas kernels for 17%

profile of v8, /device:TPU:1, one launch (start us, length us, event | category | flops | bytes accessed | tf_op | source)
XLA Modules:
  0.0 74.5 jit_solution(4337907501856168360)
XLA Ops:
  0.6 3.3 %collective-permute-start.2 = (bf16[4,2048]{1,0:T(4,128)(2,1)}, bf16[4,2048]{1,0:T(4,128)(2,1)S(1)}, u32[]{:S(2)}, u32[]{:S(2)}) collective-permute-start(bf16[4,2048]{1,0:T(4,128)(2,1)} %own_ref.1), channel_id=1, source_target_pairs={{0,1},{1,0},{2,3},{3,2},{4,5},{5,4},{6,7},{7,6},{8,9},{9,8},{10,11... | collective-permute-start | bytes 49160 | tf_op jit(solution)/shard_map/ppermute | solution.py:379
  4.0 0.1 collective-permute-start
  4.1 0.4 collective-permute-start.1
  4.5 0.9 %constant_dynamic-slice_fusion = (bf16[256,128]{1,0:T(8,128)(2,1)S(1)}, bf16[256,128]{1,0:T(8,128)(2,1)S(1)}) fusion(bf16[256,256]{1,0:T(8,128)(2,1)} %v_ref.3, s32[]{:T(128)S(6)} %select_n.49, bf16[256,256]{1,0:T(8,128)(2,1)} %k_ref.3), kind=kLoop, calls=%fused_computation.3 | loop fusion | bytes 262148 | tf_op jit(solution)/shard_map/dynamic_slice | solution.py:391
  5.4 0.0 copy-start.3
  5.4 0.0 collective-permute-done.2.early_ref.other_ref
  5.4 0.1 collective-permute-done.k_ref
  5.5 0.2 collective-permute-done.1.v_ref
  5.7 1.1 %collective-permute-start.5 = (bf16[1024,128]{1,0:T(8,128)(2,1)S(1)}, bf16[1024,128]{1,0:T(8,128)(2,1)S(1)}, u32[]{:S(2)}, u32[]{:S(2)}) collective-permute-start(bf16[1024,128]{1,0:T(8,128)(2,1)S(1)} %join.1.refs_0_), channel_id=1, source_target_pairs={{0,6},{1,7},{2,4},{3,5},{4,2},{5,3},{6,0},{7,1},{8,14},{9,15},{10,... | collective-permute-start | bytes 786440 | tf_op jit(solution)/shard_map/ppermute | solution.py:382
  6.8 0.3 collective-permute-start.4
  7.2 1.9 %collective-permute-start.3 = (bf16[1024,128]{1,0:T(8,128)(2,1)S(1)}, bf16[1024,128]{1,0:T(8,128)(2,1)S(1)}, u32[]{:S(2)}, u32[]{:S(2)}) collective-permute-start(bf16[1024,128]{1,0:T(8,128)(2,1)S(1)} %join.1.refs_0_), channel_id=1, source_target_pairs={{0,2},{1,3},{2,0},{3,1},{4,6},{5,7},{6,4},{7,5},{8,10},{9,11},{10,... | collective-permute-start | bytes 786440 | tf_op jit(solution)/shard_map/ppermute | solution.py:382
  9.1 0.7 repeat.1
  9.8 6.6 %all-to-all-start = ((bf16[8,64,128]{2,1,0:T(8,128)(2,1)}), bf16[8,64,128]{2,1,0:T(8,128)(2,1)S(1)}, u32[]{:S(2)}, u32[]{:S(2)}) async-start(bf16[8,64,128]{2,1,0:T(8,128)(2,1)} %repeat.1), calls=%async_computation | async-start | bytes 262144 | tf_op jit(solution)/shard_map/all_to_all | solution.py:396
  16.4 0.7 copy-done.4
  17.2 6.2 %all-to-all-done.refs_3_.got_ref = bf16[8,64,128]{2,1,0:T(8,128)(2,1)S(1)} async-done(((bf16[8,64,128]{2,1,0:T(8,128)(2,1)}), bf16[8,64,128]{2,1,0:T(8,128)(2,1)S(1)}, u32[]{:S(2)}, u32[]{:S(2)}) %all-to-all-start) | async-done | bytes 131104 | tf_op jit(solution)/shard_map/all_to_all | solution.py:396
  23.4 0.0 collective-permute-done.5.refs_2_
  23.4 0.0 collective-permute-done.4.refs_1_
  23.4 0.0 collective-permute-done.3.refs_0_
  23.4 0.0 copy-start.6
  23.5 0.6 pick.1
  24.1 1.3 %collective-permute-start.7 = (bf16[256,128]{1,0:T(8,128)(2,1)S(1)}, bf16[256,128]{1,0:T(8,128)(2,1)S(1)}, u32[]{:S(2)}, u32[]{:S(2)}) collective-permute-start(bf16[256,128]{1,0:T(8,128)(2,1)S(1)} %pick.1), channel_id=1, source_target_pairs={{0,56},{1,57},{2,58},{3,59},{4,60},{5,61},{6,62},{7,63},{8,0},{9,1... | collective-permute-start | bytes 196616 | tf_op jit(solution)/shard_map/ppermute | solution.py:385
  25.4 0.3 collective-permute-start.6
  25.7 3.9 %question_pass.1 = f32[8,72,128]{2,1,0:T(8,128)} custom-call(s32[64]{0:T(128)S(1)} %copy-done.6, bf16[8,64,128]{2,1,0:T(8,128)(2,1)S(1)} %all-to-all-done.refs_3_.got_ref, bf16[1024,128]{1,0:T(8,128)(2,1)S(1)} %join.1.refs_0_, bf16[1024,128]{1,0:T(8,128)(2,1)S(1)} %get-tuple-element.11.refs_1_, bf16[1024,128]{1,0:T(8,128)(2,1)S(1)} %get-tuple-element.12.refs_2_, ...), custom_call_target="tpu_custom_call" | custom-call | flops 900000000 | bytes 2500000 | tf_op jit(solution)/shard_map/question_pass/pallas_call | solution.py:217
  29.6 3.8 %all-to-all-start.1 = ((f32[8,72,128]{2,1,0:T(8,128)}), f32[8,72,128]{2,1,0:T(8,128)S(1)}, u32[]{:S(2)}, u32[]{:S(2)}) async-start(f32[8,72,128]{2,1,0:T(8,128)} %question_pass.1), calls=%async_computation.1 | async-start | bytes 589824 | tf_op jit(solution)/shard_map/all_to_all | solution.py:401
  33.4 0.0 copy-start.1
  33.4 0.0 collective-permute-done.7
  33.4 0.0 collective-permute-done.6
  33.4 4.5 %collective-permute-start.9 = (bf16[256,128]{1,0:T(8,128)(2,1)S(1)}, bf16[256,128]{1,0:T(8,128)(2,1)S(1)}, u32[]{:S(2)}, u32[]{:S(2)}) collective-permute-start(bf16[256,128]{1,0:T(8,128)(2,1)S(1)} %select_select_fusion.1), channel_id=1, source_target_pairs={{0,40},{1,41},{2,42},{3,43},{4,44},{5,45},{6,46},{7,47},{8,48},{9,... | collective-permute-start | bytes 196616 | tf_op jit(solution)/shard_map/ppermute | solution.py:385
  38.0 0.9 %caches.1 = (bf16[256,256]{1,0:T(8,128)(2,1)}, bf16[256,256]{1,0:T(8,128)(2,1)}) custom-call(bf16[256,256]{1,0:T(8,128)(2,1)S(1)} %copy-done, bf16[256,256]{1,0:T(8,128)(2,1)S(1)} %copy-done.1), custom_call_target="tpu_custom_call" | custom-call | tf_op jit(solution)/shard_map/caches/pallas_call | solution.py:276
  39.6 0.0 copy-start.2
  39.6 0.9 %collective-permute-done.9 = bf16[256,128]{1,0:T(8,128)(2,1)S(1)} collective-permute-done((bf16[256,128]{1,0:T(8,128)(2,1)S(1)}, bf16[256,128]{1,0:T(8,128)(2,1)S(1)}, u32[]{:S(2)}, u32[]{:S(2)}) %collective-permute-start.9) | collective-permute-done | bytes 65568 | tf_op jit(solution)/shard_map/ppermute | solution.py:385
  40.5 6.8 %collective-permute-done.8 = bf16[256,128]{1,0:T(8,128)(2,1)S(1)} collective-permute-done((bf16[256,128]{1,0:T(8,128)(2,1)S(1)}, bf16[256,128]{1,0:T(8,128)(2,1)S(1)}, u32[]{:S(2)}, u32[]{:S(2)}) %collective-permute-start.8) | collective-permute-done | bytes 65568 | tf_op jit(solution)/shard_map/ppermute | solution.py:385
  47.3 0.0 copy-start.5
  47.3 0.0 all-to-all-done.1.parts_ref
  47.3 1.3 %combine.1 = bf16[32,8,1024]{2,1,0:T(8,128)(2,1)} custom-call(s32[1]{0:T(128)S(6)} %copy.21.limit_ref, f32[8,72,128]{2,1,0:T(8,128)S(1)} %all-to-all-done.1.parts_ref, bf16[256,128]{1,0:T(8,128)(2,1)S(1)} %select_select_fusion.refs_0_.piece_ref, bf16[256,256]{1,0:T(8,128)(2,1)S(1)} %copy-done.2), custom_call_target="tpu_custom_call" | custom-call | tf_op jit(solution)/shard_map/combine/pallas_call | solution.py:256
  48.7 5.4 %all-to-all-start.2 = ((bf16[32,8,1024]{2,1,0:T(8,128)(2,1)}), bf16[32,8,1024]{2,1,0:T(8,128)(2,1)S(1)}, u32[]{:S(2)}, u32[]{:S(2)}) async-start(bf16[32,8,1024]{2,1,0:T(8,128)(2,1)} %combine.1), calls=%async_computation.2 | async-start | bytes 1048576 | tf_op jit(solution)/shard_map/all_to_all | solution.py:409
  54.0 1.3 %collective-permute-start.10 = (bf16[256,128]{1,0:T(8,128)(2,1)S(1)}, bf16[256,128]{1,0:T(8,128)(2,1)S(1)}, u32[]{:S(2)}, u32[]{:S(2)}) collective-permute-start(bf16[256,128]{1,0:T(8,128)(2,1)S(1)} %select_select_fusion.refs_0_.piece_ref), channel_id=1, source_target_pairs={{0,2},{1,3},{2,0},{3,1},{4,6},{5,7},{6,4},{7,5},{8,10},{9,11},{10,... | collective-permute-start | bytes 196616 | tf_op jit(solution)/shard_map/ppermute | solution.py:410
  55.3 3.8 %collective-permute-start.11 = (bf16[256,128]{1,0:T(8,128)(2,1)S(1)}, bf16[256,128]{1,0:T(8,128)(2,1)S(1)}, u32[]{:S(2)}, u32[]{:S(2)}) collective-permute-start(bf16[256,128]{1,0:T(8,128)(2,1)S(1)} %select_select_fusion.refs_0_.piece_ref), channel_id=1, source_target_pairs={{0,1},{1,0},{2,3},{3,2},{4,5},{5,4},{6,7},{7,6},{8,9},{9,8},{10,11... | collective-permute-start | bytes 196616 | tf_op jit(solution)/shard_map/ppermute | solution.py:379
  59.1 0.0 collective-permute-done.10.refs_1_
  59.1 2.9 %collective-permute-start.12 = (bf16[256,128]{1,0:T(8,128)(2,1)S(1)}, bf16[256,128]{1,0:T(8,128)(2,1)S(1)}, u32[]{:S(2)}, u32[]{:S(2)}) collective-permute-start(bf16[256,128]{1,0:T(8,128)(2,1)S(1)} %collective-permute-done.10.refs_1_), channel_id=1, source_target_pairs={{0,1},{1,0},{2,3},{3,2},{4,5},{5,4},{6,7},{7,6},{8,9},{9,8},{10,11... | collective-permute-start | bytes 196616 | tf_op jit(solution)/shard_map/ppermute | solution.py:379
  62.1 0.0 collective-permute-done.11.refs_2_
  62.1 0.9 %collective-permute-done.12.refs_3_ = bf16[256,128]{1,0:T(8,128)(2,1)S(1)} collective-permute-done((bf16[256,128]{1,0:T(8,128)(2,1)S(1)}, bf16[256,128]{1,0:T(8,128)(2,1)S(1)}, u32[]{:S(2)}, u32[]{:S(2)}) %collective-permute-start.12) | collective-permute-done | bytes 65568 | tf_op jit(solution)/shard_map/ppermute | solution.py:379
  63.0 6.7 %encode.1 = (bf16[256,2048]{1,0:T(8,128)(2,1)}, f32[8,128]{1,0:T(8,128)S(1)}) custom-call(s32[64]{0:T(128)S(1)} %copy-done.4, s32[64]{0:T(128)S(1)} %copy-done.6, bf16[256,2048]{1,0:T(8,128)(2,1)S(1)} %copy-done.5, bf16[256,256]{1,0:T(8,128)(2,1)S(1)} %copy-done, bf16[256,256]{1,0:T(8,128)(2,1)S(1)} %copy-done.1, ...), custom_call_target="tpu_custom_call" | custom-call | flops 1100000000 | bytes 3500000 | tf_op jit(solution)/shard_map/encode/pallas_call | solution.py:327
  69.7 0.0 all-to-all-done.2.refs_0_
  69.7 2.2 %collective-permute-start.13 = (bf16[32,8,1024]{2,1,0:T(8,128)(2,1)S(1)}, bf16[32,8,1024]{2,1,0:T(8,128)(2,1)S(1)}, u32[]{:S(2)}, u32[]{:S(2)}) collective-permute-start(bf16[32,8,1024]{2,1,0:T(8,128)(2,1)S(1)} %gate.3.part_ref), channel_id=1, source_target_pairs={{0,1},{1,0},{2,3},{3,2},{4,5},{5,4},{6,7},{7,6},{8,9},{9,8},{10,11... | collective-permute-start | bytes 1572872 | tf_op jit(solution)/shard_map/ppermute | solution.py:379
  71.9 0.8 %assemble.2.refs_0_ = bf16[4,2,4,8,2048]{4,3,2,1,0:T(8,128)(2,1)} custom-call(bf16[32,8,1024]{2,1,0:T(8,128)(2,1)S(1)} %gate.3.part_ref), custom_call_target="tpu_custom_call" | custom-call | tf_op jit(solution)/shard_map/assemble/pallas_call | solution.py:363
  72.8 0.7 collective-permute-done.13.part_ref
  73.5 0.8 %assemble.3 = bf16[4,2,4,8,2048]{4,3,2,1,0:T(8,128)(2,1)} custom-call(bf16[32,8,1024]{2,1,0:T(8,128)(2,1)S(1)} %collective-permute-done.13.part_ref, bf16[4,2,4,8,2048]{4,3,2,1,0:T(8,128)(2,1)} %assemble.2.refs_0_), custom_call_target="tpu_custom_call", output_to_operand_aliasing={{}: (1, {})} | custom-call | tf_op jit(solution)/shard_map/assemble/pallas_call | solution.py:363
  (15 shorter events, 0.1 us)
Async XLA Ops:
  0.6 4.8 %collective-permute-start.2 = (bf16[4,2048]{1,0:T(4,128)(2,1)}, bf16[4,2048]{1,0:T(4,128)(2,1)S(1)}, u32[]{:S(2)}, u32[]{:S(2)}) collective-permute-start(bf16[4,2048]{1,0:T(4,128)(2,1)} %own_ref.1), channel_id=1, source_target_pairs={{0,1},{1,0},{2,3},{3,2},{4,5},{5,4},{6,7},{7,6},{8,9},{9,8},{10,11... | collective-permute-start | bytes 49160 | tf_op jit(solution)/shard_map/ppermute | solution.py:379
  4.0 1.6 %collective-permute-start = (bf16[256,256]{1,0:T(8,128)(2,1)}, bf16[256,256]{1,0:T(8,128)(2,1)S(1)}, u32[]{:S(2)}, u32[]{:S(2)}) collective-permute-start(bf16[256,256]{1,0:T(8,128)(2,1)} %k_ref.3), channel_id=1, source_target_pairs={{0,1},{1,0},{2,3},{3,2},{4,5},{5,4},{6,7},{7,6},{8,9},{9,8},{10,11... | collective-permute-start | bytes 393224 | tf_op jit(solution)/shard_map/ppermute | solution.py:379
  4.1 1.6 %collective-permute-start.1 = (bf16[256,256]{1,0:T(8,128)(2,1)}, bf16[256,256]{1,0:T(8,128)(2,1)S(1)}, u32[]{:S(2)}, u32[]{:S(2)}) collective-permute-start(bf16[256,256]{1,0:T(8,128)(2,1)} %v_ref.3), channel_id=1, source_target_pairs={{0,1},{1,0},{2,3},{3,2},{4,5},{5,4},{6,7},{7,6},{8,9},{9,8},{10,11... | collective-permute-start | bytes 393224 | tf_op jit(solution)/shard_map/ppermute | solution.py:379
  5.4 3.7 %copy-start.3 = (bf16[4,2048]{1,0:T(4,128)(2,1)S(1)}, bf16[4,2048]{1,0:T(4,128)(2,1)}, u32[]{:S(2)}) copy-start(bf16[4,2048]{1,0:T(4,128)(2,1)} %own_ref.1) | copy-start | bytes 49156
  5.7 17.7 %collective-permute-start.5 = (bf16[1024,128]{1,0:T(8,128)(2,1)S(1)}, bf16[1024,128]{1,0:T(8,128)(2,1)S(1)}, u32[]{:S(2)}, u32[]{:S(2)}) collective-permute-start(bf16[1024,128]{1,0:T(8,128)(2,1)S(1)} %join.1.refs_0_), channel_id=1, source_target_pairs={{0,6},{1,7},{2,4},{3,5},{4,2},{5,3},{6,0},{7,1},{8,14},{9,15},{10,... | collective-permute-start | bytes 786440 | tf_op jit(solution)/shard_map/ppermute | solution.py:382
  6.8 16.6 %collective-permute-start.4 = (bf16[1024,128]{1,0:T(8,128)(2,1)S(1)}, bf16[1024,128]{1,0:T(8,128)(2,1)S(1)}, u32[]{:S(2)}, u32[]{:S(2)}) collective-permute-start(bf16[1024,128]{1,0:T(8,128)(2,1)S(1)} %join.1.refs_0_), channel_id=1, source_target_pairs={{0,4},{1,5},{2,6},{3,7},{4,0},{5,1},{6,2},{7,3},{8,12},{9,13},{10,... | collective-permute-start | bytes 786440 | tf_op jit(solution)/shard_map/ppermute | solution.py:382
  7.2 16.2 %collective-permute-start.3 = (bf16[1024,128]{1,0:T(8,128)(2,1)S(1)}, bf16[1024,128]{1,0:T(8,128)(2,1)S(1)}, u32[]{:S(2)}, u32[]{:S(2)}) collective-permute-start(bf16[1024,128]{1,0:T(8,128)(2,1)S(1)} %join.1.refs_0_), channel_id=1, source_target_pairs={{0,2},{1,3},{2,0},{3,1},{4,6},{5,7},{6,4},{7,5},{8,10},{9,11},{10,... | collective-permute-start | bytes 786440 | tf_op jit(solution)/shard_map/ppermute | solution.py:382
  9.8 13.6 %all-to-all-start = ((bf16[8,64,128]{2,1,0:T(8,128)(2,1)}), bf16[8,64,128]{2,1,0:T(8,128)(2,1)S(1)}, u32[]{:S(2)}, u32[]{:S(2)}) async-start(bf16[8,64,128]{2,1,0:T(8,128)(2,1)} %repeat.1), calls=%async_computation | async-start | bytes 262144 | tf_op jit(solution)/shard_map/all_to_all | solution.py:396
  16.4 0.7 copy-start.4
  23.4 2.3 %copy-start.6 = (s32[64]{0:T(128)S(1)}, s32[64]{0:T(128)}, u32[]{:S(2)}) copy-start(s32[64]{0:T(128)} %lengths_ref.3) | copy-start | bytes 772
  24.1 9.3 %collective-permute-start.7 = (bf16[256,128]{1,0:T(8,128)(2,1)S(1)}, bf16[256,128]{1,0:T(8,128)(2,1)S(1)}, u32[]{:S(2)}, u32[]{:S(2)}) collective-permute-start(bf16[256,128]{1,0:T(8,128)(2,1)S(1)} %pick.1), channel_id=1, source_target_pairs={{0,56},{1,57},{2,58},{3,59},{4,60},{5,61},{6,62},{7,63},{8,0},{9,1... | collective-permute-start | bytes 196616 | tf_op jit(solution)/shard_map/ppermute | solution.py:385
  25.4 8.0 %collective-permute-start.6 = (bf16[256,128]{1,0:T(8,128)(2,1)S(1)}, bf16[256,128]{1,0:T(8,128)(2,1)S(1)}, u32[]{:S(2)}, u32[]{:S(2)}) collective-permute-start(bf16[256,128]{1,0:T(8,128)(2,1)S(1)} %pick.1), channel_id=1, source_target_pairs={{0,8},{1,9},{2,10},{3,11},{4,12},{5,13},{6,14},{7,15},{8,16},{9,17... | collective-permute-start | bytes 196616 | tf_op jit(solution)/shard_map/ppermute | solution.py:385
  29.6 17.7 %all-to-all-start.1 = ((f32[8,72,128]{2,1,0:T(8,128)}), f32[8,72,128]{2,1,0:T(8,128)S(1)}, u32[]{:S(2)}, u32[]{:S(2)}) async-start(f32[8,72,128]{2,1,0:T(8,128)} %question_pass.1), calls=%async_computation.1 | async-start | bytes 589824 | tf_op jit(solution)/shard_map/all_to_all | solution.py:401
  33.4 4.6 %copy-start = (bf16[256,256]{1,0:T(8,128)(2,1)S(1)}, bf16[256,256]{1,0:T(8,128)(2,1)}, u32[]{:S(2)}) copy-start(bf16[256,256]{1,0:T(8,128)(2,1)} %k_ref.3) | copy-start | bytes 393220
  33.4 4.6 %copy-start.1 = (bf16[256,256]{1,0:T(8,128)(2,1)S(1)}, bf16[256,256]{1,0:T(8,128)(2,1)}, u32[]{:S(2)}) copy-start(bf16[256,256]{1,0:T(8,128)(2,1)} %v_ref.3) | copy-start | bytes 393220
  33.4 7.1 %collective-permute-start.9 = (bf16[256,128]{1,0:T(8,128)(2,1)S(1)}, bf16[256,128]{1,0:T(8,128)(2,1)S(1)}, u32[]{:S(2)}, u32[]{:S(2)}) collective-permute-start(bf16[256,128]{1,0:T(8,128)(2,1)S(1)} %select_select_fusion.1), channel_id=1, source_target_pairs={{0,40},{1,41},{2,42},{3,43},{4,44},{5,45},{6,46},{7,47},{8,48},{9,... | collective-permute-start | bytes 196616 | tf_op jit(solution)/shard_map/ppermute | solution.py:385
  38.0 9.3 %collective-permute-start.8 = (bf16[256,128]{1,0:T(8,128)(2,1)S(1)}, bf16[256,128]{1,0:T(8,128)(2,1)S(1)}, u32[]{:S(2)}, u32[]{:S(2)}) collective-permute-start(bf16[256,128]{1,0:T(8,128)(2,1)S(1)} %select_select_fusion.1), channel_id=1, source_target_pairs={{0,24},{1,25},{2,26},{3,27},{4,28},{5,29},{6,30},{7,31},{8,32},{9,... | collective-permute-start | bytes 196616 | tf_op jit(solution)/shard_map/ppermute | solution.py:385
  39.6 7.8 %copy-start.2 = (bf16[256,256]{1,0:T(8,128)(2,1)S(1)}, bf16[256,256]{1,0:T(8,128)(2,1)}, u32[]{:S(2)}) copy-start(bf16[256,256]{1,0:T(8,128)(2,1)} %get-tuple-element.9.early_ref) | copy-start | bytes 393220
  47.3 15.7 %copy-start.5 = (bf16[256,2048]{1,0:T(8,128)(2,1)S(1)}, bf16[256,2048]{1,0:T(8,128)(2,1)}, u32[]{:S(2)}) copy-start(bf16[256,2048]{1,0:T(8,128)(2,1)} %q_ref.1) | copy-start | bytes 3145732
  48.7 21.0 %all-to-all-start.2 = ((bf16[32,8,1024]{2,1,0:T(8,128)(2,1)}), bf16[32,8,1024]{2,1,0:T(8,128)(2,1)S(1)}, u32[]{:S(2)}, u32[]{:S(2)}) async-start(bf16[32,8,1024]{2,1,0:T(8,128)(2,1)} %combine.1), calls=%async_computation.2 | async-start | bytes 1048576 | tf_op jit(solution)/shard_map/all_to_all | solution.py:409
  54.0 5.1 %collective-permute-start.10 = (bf16[256,128]{1,0:T(8,128)(2,1)S(1)}, bf16[256,128]{1,0:T(8,128)(2,1)S(1)}, u32[]{:S(2)}, u32[]{:S(2)}) collective-permute-start(bf16[256,128]{1,0:T(8,128)(2,1)S(1)} %select_select_fusion.refs_0_.piece_ref), channel_id=1, source_target_pairs={{0,2},{1,3},{2,0},{3,1},{4,6},{5,7},{6,4},{7,5},{8,10},{9,11},{10,... | collective-permute-start | bytes 196616 | tf_op jit(solution)/shard_map/ppermute | solution.py:410
  55.3 6.7 %collective-permute-start.11 = (bf16[256,128]{1,0:T(8,128)(2,1)S(1)}, bf16[256,128]{1,0:T(8,128)(2,1)S(1)}, u32[]{:S(2)}, u32[]{:S(2)}) collective-permute-start(bf16[256,128]{1,0:T(8,128)(2,1)S(1)} %select_select_fusion.refs_0_.piece_ref), channel_id=1, source_target_pairs={{0,1},{1,0},{2,3},{3,2},{4,5},{5,4},{6,7},{7,6},{8,9},{9,8},{10,11... | collective-permute-start | bytes 196616 | tf_op jit(solution)/shard_map/ppermute | solution.py:379
  59.1 3.9 %collective-permute-start.12 = (bf16[256,128]{1,0:T(8,128)(2,1)S(1)}, bf16[256,128]{1,0:T(8,128)(2,1)S(1)}, u32[]{:S(2)}, u32[]{:S(2)}) collective-permute-start(bf16[256,128]{1,0:T(8,128)(2,1)S(1)} %collective-permute-done.10.refs_1_), channel_id=1, source_target_pairs={{0,1},{1,0},{2,3},{3,2},{4,5},{5,4},{6,7},{7,6},{8,9},{9,8},{10,11... | collective-permute-start | bytes 196616 | tf_op jit(solution)/shard_map/ppermute | solution.py:379
  69.7 3.8 %collective-permute-start.13 = (bf16[32,8,1024]{2,1,0:T(8,128)(2,1)S(1)}, bf16[32,8,1024]{2,1,0:T(8,128)(2,1)S(1)}, u32[]{:S(2)}, u32[]{:S(2)}) collective-permute-start(bf16[32,8,1024]{2,1,0:T(8,128)(2,1)S(1)} %gate.3.part_ref), channel_id=1, source_target_pairs={{0,1},{1,0},{2,3},{3,2},{4,5},{5,4},{6,7},{7,6},{8,9},{9,8},{10,11... | collective-permute-start | bytes 1572872 | tf_op jit(solution)/shard_map/ppermute | solution.py:379
